TPU v7x, 128 devices: a whole 4x4x4 slice. The times are simulated.
128 devices in a mesh: frame: 8 (over y, core), region: 16 (over z, x).
Axes of the slice: x: 4, y: 4, z: 4, core: 2. Of those that a mesh axis runs over, the one named last changes fastest.
Arguments:
- queries: bfloat16 [8, 4096, 3072], P('frame', 'region'), may hold values from -54 to 54
- keys: bfloat16 [8, 4096, 3072], P('frame', 'region'), may hold values from -18 to 18
- values: bfloat16 [8, 4096, 3072], P('frame', 'region'), may hold values from -6 to 6
- head_kind: int32 [24], replicated, may hold values from 0 to 1, as said below
- spatial_mask: int32 [24, 32, 32], replicated, may hold values 0 or 1
- temporal_mask: int32 [24, 8, 8], replicated, may hold values 0 or 1
- frame_valid: int32 [8], replicated, may hold values from 0 to 1, as said below
Outputs:
- attended: bfloat16 [8, 4096, 3072], P('frame', 'region')
Inputs may be any that keep to these rules, and one draw needn't show every extreme that they name: `head_kind`: exactly 12 entries are 1. `frame_valid`: the last frame is always padding.
All inputs are finite; a program needn't handle non-finite values.
Results may differ from a plain program's by a relative error of at most 0.01.
Values may be sent and summed in bfloat16 or wider, within the bound.
No kernel may reach another device: no remote copies, remote signals or barrier semaphores. Data moves between devices by JAX's collectives and lax.ppermute only.
A program may use at most 192 MiB of HBM per device.

v0:
```python
import jax
import jax.numpy as jnp
from jax import lax
from jax.sharding import PartitionSpec as P

HEADS = 24
TEMP_HEADS = 12
BLK = 128


def softmax_weights(scores, allowed):
    masked = jnp.where(allowed, scores, -jnp.inf)
    top = jnp.max(masked, axis=-1, keepdims=True)
    expo = jnp.where(allowed, jnp.exp(masked - top), 0.0)
    return (expo / jnp.sum(expo, axis=-1, keepdims=True)).astype(jnp.bfloat16)


def pick_heads(tensor, chosen):
    return jnp.take(tensor, chosen, axis=2)


def masked_rows(spatial_mask, head, first_block, block_rows, block_total):
    blocks = lax.dynamic_index_in_dim(spatial_mask, head, 0, False)
    own_rows = lax.dynamic_slice_in_dim(blocks, first_block, block_rows, 0)
    query_blocks = first_block + jnp.arange(block_rows)
    diagonal = query_blocks[:, None] == jnp.arange(block_total)[None, :]
    return (own_rows == 1) | diagonal


def shards(queries, keys, values, head_kind, spatial_mask, temporal_mask, frame_valid):
    frames_dev, rows, width = queries.shape
    head_size = width // HEADS
    scale = 1.0 / head_size**0.5
    shape4 = (frames_dev, rows, HEADS, head_size)
    q_heads = queries.reshape(shape4)
    k_heads = keys.reshape(shape4)
    v_heads = values.reshape(shape4)
    spatial_count = HEADS - TEMP_HEADS
    ordering = jnp.argsort(head_kind, stable=True)
    spatial_idx = ordering[:spatial_count]
    temporal_idx = ordering[spatial_count:]
    block_rows = rows // BLK
    k_gath, v_gath = (
        lax.all_gather(pick_heads(k_heads, spatial_idx), "region", axis=1, tiled=True),
        lax.all_gather(pick_heads(v_heads, spatial_idx), "region", axis=1, tiled=True),
    )
    q_spatial = pick_heads(q_heads, spatial_idx)
    frame_tokens = k_gath.shape[1]
    block_total = frame_tokens // BLK
    first_block = lax.axis_index("region") * block_rows

    def spatial_head(index):
        head = spatial_idx[index]
        allowed_blocks = masked_rows(spatial_mask, head, first_block, block_rows, block_total)
        allowed = jnp.repeat(jnp.repeat(allowed_blocks, BLK, 0), BLK, 1)
        q_one = lax.dynamic_index_in_dim(q_spatial[0], index, 1, False)
        k_one = lax.dynamic_index_in_dim(k_gath[0], index, 1, False)
        v_one = lax.dynamic_index_in_dim(v_gath[0], index, 1, False)
        scores = jnp.dot(q_one, k_one.T, preferred_element_type=jnp.float32) * scale
        weights = softmax_weights(scores, allowed)
        return jnp.dot(weights, v_one, preferred_element_type=jnp.float32).astype(jnp.bfloat16)

    spatial_out = lax.map(spatial_head, jnp.arange(spatial_count))
    spatial_out = jnp.transpose(spatial_out, (1, 0, 2))[None]
    q_every, k_every_t, v_every_t = (
        lax.all_to_all(q_heads, "frame", split_axis=1, concat_axis=0, tiled=True),
        lax.all_to_all(k_heads, "frame", split_axis=1, concat_axis=0, tiled=True),
        lax.all_to_all(v_heads, "frame", split_axis=1, concat_axis=0, tiled=True),
    )
    q_time = pick_heads(q_every, temporal_idx)
    k_time = pick_heads(k_every_t, temporal_idx)
    v_time = pick_heads(v_every_t, temporal_idx)
    frame_count = q_time.shape[0]
    eye_frames = jnp.arange(frame_count)[:, None] == jnp.arange(frame_count)[None, :]
    pairs = jnp.take(temporal_mask, temporal_idx, axis=0)
    allowed_time = (pairs == 1) & (frame_valid[None, None, :] == 1) | eye_frames[None]
    time_scores = (
        jnp.einsum("fnhd,gnhd->hnfg", q_time, k_time, preferred_element_type=jnp.float32) * scale
    )
    time_weights = softmax_weights(time_scores, allowed_time[:, None])
    time_out = jnp.einsum(
        "hnfg,gnhd->fnhd", time_weights, v_time, preferred_element_type=jnp.float32
    ).astype(jnp.bfloat16)
    temporal_out = lax.all_to_all(time_out, "frame", split_axis=0, concat_axis=1, tiled=True)
    combined = jnp.zeros(shape4, jnp.bfloat16)
    combined = combined.at[:, :, spatial_idx, :].set(spatial_out)
    combined = combined.at[:, :, temporal_idx, :].set(temporal_out)
    return combined.reshape(frames_dev, rows, width)


def solution(mesh):
    in_specs = (
        P("frame", "region", None),
        P("frame", "region", None),
        P("frame", "region", None),
        P(),
        P(),
        P(),
        P(),
    )
    out_specs = P("frame", "region", None)
    return jax.shard_map(shards, mesh=mesh, in_specs=in_specs, out_specs=out_specs, check_vma=False)
```

profile of v0, /device:TPU:1, one launch (start us, length us, event | category | flops | bytes accessed | tf_op | source)
XLA Modules:
  0.0 406.1 jit_solution(4564602978352737560)
XLA Ops:
  6.5 2.3 sort.17
  8.9 2.7 copy.106
  17.1 3.0 gather_fusion.1
  20.1 3.0 gather_fusion.2
  23.1 2.6 copy.107
  25.7 3.0 gather_fusion.3
  28.7 3.3 bitcast_select_fusion
  32.7 2.8 copy.108
  35.5 6.0 %all-to-all-start = ((bf16[1,256,24,128]{3,2,0,1:T(8,128)(2,1)}), bf16[1,256,24,128]{3,2,0,1:T(8,128)(2,1)}, u32[]{:S(2)}, u32[]{:S(2)}) async-start(bf16[1,256,24,128]{3,2,0,1:T(8,128)(2,1)} %copy.108), calls=%async_computation | async-start | bytes 3145728 | tf_op jit(solution)/shard_map/all_to_all | solution.py:68
  43.4 18.9 %all-to-all-done = bf16[1,256,24,128]{3,2,0,1:T(8,128)(2,1)} async-done(((bf16[1,256,24,128]{3,2,0,1:T(8,128)(2,1)}), bf16[1,256,24,128]{3,2,0,1:T(8,128)(2,1)}, u32[]{:S(2)}, u32[]{:S(2)}) %all-to-all-start) | async-done | bytes 1572896 | tf_op jit(solution)/shard_map/all_to_all | solution.py:68
  62.3 4.4 %all-to-all-start.1 = ((bf16[1,256,24,128]{3,2,0,1:T(8,128)(2,1)}), bf16[1,256,24,128]{3,2,0,1:T(8,128)(2,1)S(1)}, u32[]{:S(2)}, u32[]{:S(2)}) async-start(bf16[1,256,24,128]{3,2,0,1:T(8,128)(2,1)} %copy.111), calls=%async_computation.1 | async-start | bytes 3145728 | tf_op jit(solution)/shard_map/all_to_all | solution.py:66
  68.6 18.8 %all-to-all-done.1 = bf16[1,256,24,128]{3,2,0,1:T(8,128)(2,1)S(1)} async-done(((bf16[1,256,24,128]{3,2,0,1:T(8,128)(2,1)}), bf16[1,256,24,128]{3,2,0,1:T(8,128)(2,1)S(1)}, u32[]{:S(2)}, u32[]{:S(2)}) %all-to-all-start.1) | async-done | bytes 1572896 | tf_op jit(solution)/shard_map/all_to_all | solution.py:66
  87.4 4.4 %all-to-all-start.2 = ((bf16[1,256,24,128]{3,2,0,1:T(8,128)(2,1)}), bf16[1,256,24,128]{3,2,0,1:T(8,128)(2,1)S(1)}, u32[]{:S(2)}, u32[]{:S(2)}) async-start(bf16[1,256,24,128]{3,2,0,1:T(8,128)(2,1)} %copy.113), calls=%async_computation.2 | async-start | bytes 3145728 | tf_op jit(solution)/shard_map/all_to_all | solution.py:67
  92.6 2.9 copy.109
  95.5 3.0 gather_fusion.4
  100.0 3.0 gather_fusion.5
  103.0 9.5 %all-to-all-done.2 = bf16[1,256,24,128]{3,2,0,1:T(8,128)(2,1)S(1)} async-done(((bf16[1,256,24,128]{3,2,0,1:T(8,128)(2,1)}), bf16[1,256,24,128]{3,2,0,1:T(8,128)(2,1)S(1)}, u32[]{:S(2)}, u32[]{:S(2)}) %all-to-all-start.2) | async-done | bytes 1572896 | tf_op jit(solution)/shard_map/all_to_all | solution.py:67
  116.9 9.5 %fusion.33 = (f32[12,32,8]{1,2,0:T(8,128)S(1)}, f32[12,32,8,8]{1,3,2,0:T(8,128)S(1)}) fusion(f32[12,32,8,8]{1,3,2,0:T(8,128)S(1)} %copy.117, pred[12,8,8]{2,1,0:T(8,128)(4,1)S(1)} %fusion.29), kind=kOutput, calls=%fused_computation.66 | output fusion | flops 122887 | bytes 209664 | tf_op jit(solution)/shard_map/sub | solution.py:14
  129.5 4.3 %all-to-all-start.3 = ((bf16[8,32,12,128]{3,1,2,0:T(8,128)(2,1)}), bf16[8,32,12,128]{3,1,2,0:T(8,128)(2,1)S(1)}, u32[]{:S(2)}, u32[]{:S(2)}) async-start(bf16[8,32,12,128]{3,1,2,0:T(8,128)(2,1)} %copy.120), calls=%async_computation.3 | async-start | bytes 1572864 | tf_op jit(solution)/shard_map/all_to_all | solution.py:84
  133.8 12.3 %all-to-all-done.3 = bf16[8,32,12,128]{3,1,2,0:T(8,128)(2,1)S(1)} async-done(((bf16[8,32,12,128]{3,1,2,0:T(8,128)(2,1)}), bf16[8,32,12,128]{3,1,2,0:T(8,128)(2,1)S(1)}, u32[]{:S(2)}, u32[]{:S(2)}) %all-to-all-start.3) | async-done | bytes 786464 | tf_op jit(solution)/shard_map/all_to_all | solution.py:84
  146.2 71.2 %all-gather.5.cloned.1.call-done = bf16[1,4096,12,128]{3,1,2,0:T(8,128)(2,1)} async-done(((bf16[1,256,12,128]{3,1,2,0:T(8,128)(2,1)}), bf16[1,4096,12,128]{3,1,2,0:T(8,128)(2,1)}) %all-gather.5.cloned.1.call-update) | async-done | bytes 12582928 | tf_op jit(solution)/shard_map/all_gather | solution.py:45
  217.5 176.7 %while.13 = (s32[]{:T(128)}, bf16[12,256,128]{2,1,0:T(8,128)(2,1)S(1)}, s32[12]{0:T(128)S(1)}, s32[12]{0:T(128)S(1)}, s32[24,32,32]{2,1,0:T(8,128)}, /*index=5*/...) while((s32[]{:T(128)}, ...), condition=%wide.region_4.6_spmd, body=%wide.region_1.5_spmd.sunk | while | flops 547389120 | bytes 19029144 | solution.py:63
  223.3 2.1 broadcast_in_dim.177
  225.4 2.5 fusion.40
  229.1 3.1 fusion.42
  238.1 2.1 broadcast_in_dim.177
  240.1 2.5 fusion.40
  243.8 3.1 fusion.42
  254.9 2.5 fusion.40
  258.5 3.1 fusion.42
  269.6 2.5 fusion.40
  273.3 3.1 fusion.42
  284.3 2.5 fusion.40
  288.0 3.1 fusion.42
  299.0 2.5 fusion.40
  302.7 3.1 fusion.42
  313.8 2.5 fusion.40
  317.4 3.1 fusion.42
  328.5 2.5 fusion.40
  332.2 3.1 fusion.42
  343.2 2.5 fusion.40
  346.9 3.1 fusion.42
  358.0 2.5 fusion.40
  361.6 3.1 fusion.42
  372.7 2.5 fusion.40
  376.4 3.1 fusion.42
  387.4 2.5 fusion.40
  391.1 3.1 fusion.42
  (130 shorter events, 83.5 us)
Async XLA Ops:
  6.5 139.7 %all-gather.3.cloned.1.call-start = ((), (), s32[]{:S(2)}) async-start(), calls=%async_computation.4 | async-start | bytes 13369344 | tf_op jit(solution)/shard_map/all_gather | solution.py:44
  8.9 2.7 copy-start.2
  32.0 185.5 %all-gather.5.cloned.1.call-start = ((), (), s32[]{:S(2)}) async-start(), calls=%async_computation.5 | async-start | bytes 13369344 | tf_op jit(solution)/shard_map/all_gather | solution.py:45
  35.5 26.8 %all-to-all-start = ((bf16[1,256,24,128]{3,2,0,1:T(8,128)(2,1)}), bf16[1,256,24,128]{3,2,0,1:T(8,128)(2,1)}, u32[]{:S(2)}, u32[]{:S(2)}) async-start(bf16[1,256,24,128]{3,2,0,1:T(8,128)(2,1)} %copy.108), calls=%async_computation | async-start | bytes 3145728 | tf_op jit(solution)/shard_map/all_to_all | solution.py:68
  62.3 25.1 %all-to-all-start.1 = ((bf16[1,256,24,128]{3,2,0,1:T(8,128)(2,1)}), bf16[1,256,24,128]{3,2,0,1:T(8,128)(2,1)S(1)}, u32[]{:S(2)}, u32[]{:S(2)}) async-start(bf16[1,256,24,128]{3,2,0,1:T(8,128)(2,1)} %copy.111), calls=%async_computation.1 | async-start | bytes 3145728 | tf_op jit(solution)/shard_map/all_to_all | solution.py:66
  68.6 23.2 %copy-start.3 = (s32[24,8,8]{0,2,1:T(8,128)S(1)}, s32[24,8,8]{0,2,1:T(8,128)}, u32[]{:S(2)}) copy-start(s32[24,8,8]{0,2,1:T(8,128)} %param.18) | copy-start | bytes 18436
  68.6 23.9 %copy-start.4 = (s32[8]{0:T(128)S(1)}, s32[8]{0:T(128)}, u32[]{:S(2)}) copy-start(s32[8]{0:T(128)} %param.19) | copy-start | bytes 100
  87.4 25.1 %all-to-all-start.2 = ((bf16[1,256,24,128]{3,2,0,1:T(8,128)(2,1)}), bf16[1,256,24,128]{3,2,0,1:T(8,128)(2,1)S(1)}, u32[]{:S(2)}, u32[]{:S(2)}) async-start(bf16[1,256,24,128]{3,2,0,1:T(8,128)(2,1)} %copy.113), calls=%async_computation.2 | async-start | bytes 3145728 | tf_op jit(solution)/shard_map/all_to_all | solution.py:67
  112.8 1.6 copy-start
  112.8 1.6 copy-start.1
  129.5 16.6 %all-to-all-start.3 = ((bf16[8,32,12,128]{3,1,2,0:T(8,128)(2,1)}), bf16[8,32,12,128]{3,1,2,0:T(8,128)(2,1)S(1)}, u32[]{:S(2)}, u32[]{:S(2)}) async-start(bf16[8,32,12,128]{3,1,2,0:T(8,128)(2,1)} %copy.120), calls=%async_computation.3 | async-start | bytes 1572864 | tf_op jit(solution)/shard_map/all_to_all | solution.py:84
Sparse Core Ops, SparseCore 0:
  32.1 93.4 all-gather.2
  127.7 89.6 all-gather.4
where the time goes:
time: 409 us; the launch traced here: 406 us
  waiting for transfers between devices  132 us (32%)
  local copies, waits for them, and re-layouts  86.3 us (21%)
  matrix products  68.2 us (17%)
  loops' own time  47.1 us (12%)
  other arithmetic  40.4 us (10%)
  starting transfers between devices  19.1 us (5%)
  between operations  13.6 us (3%)
    all_gather x1, waiting for transfers between devices, shards(): lax.all_gather(pick_heads(v_heads, spatial_idx), 'region', axis=1, tiled=...  71.2 us
    another operation x1, loops' own time, shards(): spatial_out = lax.map(spatial_head, jnp.arange(spatial_count))  47.1 us
    dot_general x12, matrix products, spatial_head(): jnp.dot(weights, v_one, preferred_element_type=jnp.float32)  37.2 us
    dot_general x12, matrix products, spatial_head(): scores = jnp.dot(q_one, k_one.T, preferred_element_type=jnp.float32) * scale  29.8 us
    broadcast_in_dim x24, local copies, waits for them, and re-layouts, spatial_head(): allowed = jnp.repeat(jnp.repeat(allowed_blocks, BLK, 0), BLK, 1)  24.9 us
    all_to_all x1, waiting for transfers between devices, shards(): lax.all_to_all(v_heads, 'frame', split_axis=1, concat_axis=0, tiled=True)  18.9 us
    all_to_all x1, waiting for transfers between devices, shards(): lax.all_to_all(q_heads, 'frame', split_axis=1, concat_axis=0, tiled=True)  18.8 us
    gather x6, local copies, waits for them, and re-layouts, pick_heads(): return jnp.take(tensor, chosen, axis=2)  16.5 us
  transfers between devices with their start and end apart: 6, of which 5 were waited for; matrix products, arithmetic and copies ran while one was open for 9% of the time, Pallas kernels for 0%

commit v1 on v0

v1 whole, which is shorter than its diff:
```python
import functools

import jax
import jax.numpy as jnp
from jax import lax
from jax.experimental import pallas as pl
from jax.experimental.pallas import tpu as pltpu
from jax.sharding import PartitionSpec as P

HEADS = 24
TEMP_HEADS = 12
SPAT_HEADS = HEADS - TEMP_HEADS
BLK = 128
HEAD = 128
RING = 4
GROUP = SPAT_HEADS // RING
FRAMES = 8
ROWS = 256
PART = ROWS // FRAMES
WIDTH = HEADS * HEAD
NEG = -1e30
LOG2_SCALE = 1.4426950408889634 / HEAD**0.5
AXES = ("frame", "region")
VMEM = 56 * 1024 * 1024
BF16 = jnp.bfloat16
F32 = jnp.float32
ANY = pl.BlockSpec(memory_space=pl.ANY)
SMEM = pl.BlockSpec(memory_space=pltpu.SMEM)


def flat(y, core, z, x):
    return ((y * 2 + core) * RING + z) * RING + x


def axis_groups(first):
    groups = []
    for y in range(RING):
        for core in range(2):
            along_x = (core == 0) == first
            for other in range(RING):
                groups.append([
                    flat(y, core, other, i) if along_x else flat(y, core, i, other)
                    for i in range(RING)
                ])
    return groups


def ring_pairs(first, shift):
    pairs = []
    for group in axis_groups(first):
        for i in range(RING):
            pairs.append((group[i], group[(i + shift) % RING]))
    return sorted(pairs)


def swap(tensor):
    return lax.all_to_all(tensor, AXES, 0, 0, tiled=True, axis_index_groups=axis_groups(True))


def shift(tensor, step):
    return lax.ppermute(tensor, AXES, ring_pairs(False, step))


def columns(index):
    return pl.ds(pl.multiple_of(index * HEAD, HEAD), HEAD)


def pack_kv(kind, k_ref, v_ref, kv_ref, order_ref, sem):
    spatial = jnp.int32(0)
    temporal = jnp.int32(0)
    for head in range(HEADS):
        one = kind[head]
        order_ref[jnp.where(one == 1, SPAT_HEADS + temporal, spatial)] = head

        @pl.when(one == 0)
        def _(spatial=spatial, head=head):
            group, place = spatial // GROUP, spatial % GROUP
            for which, ref in enumerate((k_ref, v_ref)):
                pltpu.make_async_copy(
                    ref.at[:, pl.ds(head * HEAD, HEAD)], kv_ref.at[group, which, place], sem
                ).start()

        spatial += 1 - one
        temporal += one
    pltpu.make_async_copy(kv_ref, kv_ref, sem).wait()


def pack_rest(kind, q_ref, k_ref, v_ref, sq_ref, tm_ref, sem_s, sem_t):
    spatial = jnp.int32(0)
    temporal = jnp.int32(0)
    for head in range(HEADS):
        one = kind[head]

        @pl.when(one == 0)
        def _(spatial=spatial, head=head):
            pltpu.make_async_copy(
                q_ref.at[:, pl.ds(head * HEAD, HEAD)],
                sq_ref.at[spatial // GROUP, spatial % GROUP],
                sem_s,
            ).start()

        @pl.when(one == 1)
        def _(temporal=temporal, head=head):
            for which, ref in enumerate((q_ref, k_ref, v_ref)):
                pltpu.make_async_copy(
                    ref.at[:, pl.ds(head * HEAD, HEAD)],
                    tm_ref.at[:, columns(which * TEMP_HEADS + temporal)],
                    sem_t,
                ).start()

        spatial += 1 - one
        temporal += one
    pltpu.make_async_copy(sq_ref, sq_ref, sem_s).wait()
    pltpu.make_async_copy(tm_ref, tm_ref, sem_t).wait()


def place_temporal(kind, src_ref, out_ref, sem):
    temporal = jnp.int32(0)
    for head in range(HEADS):
        one = kind[head]

        @pl.when(one == 1)
        def _(temporal=temporal, head=head):
            pltpu.make_async_copy(
                src_ref.at[:, columns(temporal)], out_ref.at[:, pl.ds(head * HEAD, HEAD)], sem
            ).start()

        temporal += one
    pltpu.make_async_copy(src_ref, src_ref, sem).wait()


def place_spatial(kind, src_ref, base_ref, out_ref, sem):
    spatial = jnp.int32(0)
    for head in range(HEADS):
        one = kind[head]

        @pl.when(one == 0)
        def _(spatial=spatial, head=head):
            pltpu.make_async_copy(
                src_ref.at[spatial // GROUP, spatial % GROUP],
                out_ref.at[:, pl.ds(head * HEAD, HEAD)],
                sem,
            ).start()

        spatial += 1 - one
    pltpu.make_async_copy(src_ref, src_ref, sem).wait()


def region_of(where, piece, ring):
    return jnp.where(where[0] == 0, ring * RING + piece, piece * RING + ring)


def attend(chunks, has_state, last, order, where, q_ref, bias_ref, *refs):
    kv_refs = refs[: len(chunks)]
    refs = refs[len(chunks):]
    if has_state:
        acc_in, stat_in = refs[:2]
        refs = refs[2:]
    if last:
        (out_ref,) = refs[:1]
        refs = refs[1:]
    else:
        acc_out, stat_out = refs[:2]
        refs = refs[2:]
    keys, vals = refs
    ring = where[1]
    row = 0
    for (offset, pieces), kv_ref in zip(chunks, kv_refs):
        source = (ring + offset) % RING
        for slot, piece in enumerate(pieces):
            region = region_of(where, piece, source)
            keys[pl.ds(row, ROWS), :HEAD] = kv_ref[slot, 0, 0]
            vals[pl.ds(row, ROWS), :HEAD] = kv_ref[slot, 1, 0]
            for half in range(ROWS // BLK):
                line = bias_ref[0, pl.ds(region * (ROWS // BLK) + half, 1), :]
                keys[pl.ds(row + half * BLK, BLK), HEAD:] = jnp.broadcast_to(
                    line, (BLK, HEAD)
                ).astype(BF16)
            row += ROWS
    vals[:, HEAD:] = jnp.ones((row, HEAD), BF16)
    lane = lax.broadcasted_iota(jnp.int32, (ROWS, HEAD), 1)
    half = lax.broadcasted_iota(jnp.int32, (ROWS, HEAD), 0) // BLK
    for piece in range(RING):
        block = region_of(where, piece, ring) * (ROWS // BLK) + half
        mark = jnp.where(lane == block, 1.0, 0.0).astype(BF16)
        query = jnp.concatenate([q_ref[piece, 0], mark], axis=1)
        scores = lax.dot_general(
            query, keys[...], (((1,), (1,)), ((), ())), preferred_element_type=F32
        )
        top = jnp.max(scores, axis=1, keepdims=True)
        if has_state:
            stat = stat_in[0, piece]
            old = stat[:, :1]
            top = jnp.maximum(top, old)
        weights = jnp.exp2((scores - top) * LOG2_SCALE).astype(BF16)
        both = jnp.dot(weights, vals[...], preferred_element_type=F32)
        total, sums = both[:, :HEAD], both[:, HEAD:]
        if has_state:
            decay = jnp.exp2((old - top) * LOG2_SCALE)
            total = total + acc_in[0, piece] * decay
            sums = sums + stat[:, HEAD - 1:] * decay
        if last:
            out_ref[piece, 0] = (total / sums).astype(BF16)
        else:
            acc_out[0, piece] = total
            stat_out[0, piece] = jnp.where(lane < HEAD // 2, top, sums)


def attention(order, where, bias, queries, chunks, arrays, state=None, last=False):
    keys = sum(len(pieces) for _, pieces in chunks) * ROWS
    kv_specs = [
        pl.BlockSpec((len(pieces), 2, 1, ROWS, HEAD), lambda h, o, w: (0, 0, h, 0, 0))
        for _, pieces in chunks
    ]
    q_spec = pl.BlockSpec((RING, 1, ROWS, HEAD), lambda h, o, w: (0, h, 0, 0))
    state_spec = pl.BlockSpec((1, RING, ROWS, HEAD), lambda h, o, w: (h, 0, 0, 0))
    bias_spec = pl.BlockSpec(
        (1, bias.shape[1], HEAD), lambda h, o, w: (o[w[2] * GROUP + h], 0, 0)
    )
    state_shape = jax.ShapeDtypeStruct((GROUP, RING, ROWS, HEAD), F32)
    flops = 8 * GROUP * RING * ROWS * keys * HEAD
    return pl.pallas_call(
        functools.partial(attend, chunks, state is not None, last),
        grid_spec=pltpu.PrefetchScalarGridSpec(
            num_scalar_prefetch=2,
            grid=(GROUP,),
            in_specs=[q_spec, bias_spec] + kv_specs + [state_spec] * (0 if state is None else 2),
            out_specs=q_spec if last else [state_spec] * 2,
            scratch_shapes=[pltpu.VMEM((keys, 2 * HEAD), BF16)] * 2,
        ),
        out_shape=jax.ShapeDtypeStruct(queries.shape, BF16) if last else [state_shape] * 2,
        compiler_params=pltpu.CompilerParams(vmem_limit_bytes=VMEM),
        cost_estimate=pl.CostEstimate(flops=flops, bytes_accessed=4 << 20, transcendentals=0),
        name="spatial_attention",
    )(order, where, queries, bias, *arrays, *(state or ()))


def attend_time(order, bias_ref, q_ref, k_ref, v_ref, out_ref):
    lane = lax.broadcasted_iota(jnp.int32, (ROWS, HEAD), 1)
    row = lax.broadcasted_iota(jnp.int32, (ROWS, HEAD), 0)
    frame, place = row // PART, row % PART
    mark = jnp.where((lane == frame) | (lane == FRAMES + place), 1.0, 0.0).astype(BF16)
    apart = jnp.where(
        (lane >= FRAMES) & (lane < FRAMES + PART) & (lane != FRAMES + place), NEG, 0.0
    )
    pairs = jnp.broadcast_to(bias_ref[0][:, None, :], (FRAMES, PART, HEAD)).reshape(ROWS, HEAD)
    query = jnp.concatenate([q_ref[...], mark], axis=1)
    keys = jnp.concatenate([k_ref[...], (pairs + apart).astype(BF16)], axis=1)
    vals = jnp.concatenate([v_ref[...], jnp.ones((ROWS, HEAD), BF16)], axis=1)
    scores = lax.dot_general(query, keys, (((1,), (1,)), ((), ())), preferred_element_type=F32)
    top = jnp.max(scores, axis=1, keepdims=True)
    weights = jnp.exp2((scores - top) * LOG2_SCALE).astype(BF16)
    both = jnp.dot(weights, vals, preferred_element_type=F32)
    out_ref[...] = (both[:, :HEAD] / both[:, HEAD:]).astype(BF16)


def time_attention(order, bias, gathered):
    def at(which):
        return pl.BlockSpec((ROWS, HEAD), lambda h, o: (0, which * TEMP_HEADS + h))

    return pl.pallas_call(
        attend_time,
        grid_spec=pltpu.PrefetchScalarGridSpec(
            num_scalar_prefetch=1,
            grid=(TEMP_HEADS,),
            in_specs=[pl.BlockSpec((1, FRAMES, HEAD), lambda h, o: (o[SPAT_HEADS + h], 0, 0))]
            + [at(which) for which in range(3)],
            out_specs=at(0),
        ),
        out_shape=jax.ShapeDtypeStruct((ROWS, TEMP_HEADS * HEAD), BF16),
        compiler_params=pltpu.CompilerParams(vmem_limit_bytes=VMEM),
        cost_estimate=pl.CostEstimate(flops=4 << 30, bytes_accessed=4 << 20, transcendentals=0),
        name="temporal_attention",
    )(order, bias, gathered, gathered, gathered)


def moved(count):
    return pl.CostEstimate(flops=0, bytes_accessed=count, transcendentals=0)


def shards(queries, keys, values, head_kind, spatial_mask, temporal_mask, frame_valid):
    rows, width = queries.shape[1:]
    queries, keys, values = (t.reshape(rows, width) for t in (queries, keys, values))
    dma = pltpu.SemaphoreType.DMA
    core = lax.axis_index("frame") % 2
    region = lax.axis_index("region")
    place_z, place_x = region // RING, region % RING
    own = jnp.where(core == 0, place_x, place_z)
    ring = jnp.where(core == 0, place_z, place_x)
    where = jnp.stack([core, ring, own]).astype(jnp.int32)

    kv, order = pl.pallas_call(
        pack_kv,
        in_specs=[SMEM, ANY, ANY],
        out_specs=[ANY, SMEM],
        out_shape=[
            jax.ShapeDtypeStruct((RING, 2, GROUP, ROWS, HEAD), BF16),
            jax.ShapeDtypeStruct((HEADS,), jnp.int32),
        ],
        scratch_shapes=[dma],
        cost_estimate=moved(3 << 20),
        name="pack_keys_values",
    )(head_kind, keys, values)
    kv = swap(kv)
    sq, tm = pl.pallas_call(
        pack_rest,
        in_specs=[SMEM, ANY, ANY, ANY],
        out_specs=[ANY, ANY],
        out_shape=[
            jax.ShapeDtypeStruct((RING, GROUP, ROWS, HEAD), BF16),
            jax.ShapeDtypeStruct((ROWS, 3 * TEMP_HEADS * HEAD), BF16),
        ],
        scratch_shapes=[dma, dma],
        cost_estimate=moved(6 << 20),
        name="pack_rest",
    )(head_kind, queries, keys, values)
    sq = swap(sq)
    tm = lax.all_to_all(tm, "frame", 0, 0, tiled=True)

    blocks = spatial_mask.shape[1]
    same = jnp.eye(blocks, dtype=jnp.bool_)[None]
    bias = jnp.where((jnp.swapaxes(spatial_mask, 1, 2) == 1) | same, 0.0, NEG).astype(F32)
    bias = jnp.pad(bias, ((0, 0), (0, 0), (0, HEAD - blocks)))
    alike = jnp.eye(FRAMES, dtype=jnp.bool_)[None]
    seen = (jnp.swapaxes(temporal_mask, 1, 2) == 1) & (frame_valid[None, :, None] == 1)
    time_bias = jnp.where(seen | alike, 0.0, NEG).astype(F32)
    time_bias = jnp.pad(time_bias, ((0, 0), (0, 0), (0, HEAD - FRAMES)))

    whole = tuple(range(RING))
    half = RING // 2
    right, left = shift(kv, 1), shift(kv, RING - 1)
    state = attention(order, where, bias, sq, [(0, whole)], [kv])
    right2, left2 = shift(right[:half], 1), shift(left[half:], RING - 1)
    state = attention(
        order, where, bias, sq, [(RING - 1, whole), (1, whole)], [right, left], state
    )
    spatial = attention(
        order, where, bias, sq, [(2, whole[:half]), (2, whole[half:])], [right2, left2], state, True
    )
    time_out = time_attention(order, time_bias, tm)
    time_out = lax.all_to_all(time_out, "frame", 0, 0, tiled=True)
    out_shape = jax.ShapeDtypeStruct((rows, width), BF16)
    base = pl.pallas_call(
        place_temporal,
        in_specs=[SMEM, ANY],
        out_specs=ANY,
        out_shape=out_shape,
        scratch_shapes=[dma],
        cost_estimate=moved(2 << 20),
        name="place_temporal",
    )(head_kind, time_out)
    spatial = swap(spatial)
    result = pl.pallas_call(
        place_spatial,
        in_specs=[SMEM, ANY, ANY],
        out_specs=ANY,
        out_shape=out_shape,
        scratch_shapes=[dma],
        input_output_aliases={2: 0},
        cost_estimate=moved(2 << 20),
        name="place_spatial",
    )(head_kind, spatial, base)
    return result[None]


def solution(mesh):
    wide = P("frame", "region", None)
    return jax.shard_map(
        shards,
        mesh=mesh,
        in_specs=(wide, wide, wide, P(), P(), P(), P()),
        out_specs=wide,
        check_vma=False,
    )
```

time: 409 us -> 303 us (0.74)
  Pallas kernels: 0 us -> 240 us
  waiting for transfers between devices: 132 us -> 9.53 us
  local copies, waits for them, and re-layouts: 86.3 us -> 7.34 us
  matrix products: 68.2 us -> 0 us
  loops' own time: 47.1 us -> 0 us
  other arithmetic: 40.4 us -> 0.78 us
  blocking collectives: 0 us -> 17.3 us
  between operations: 13.6 us -> 0.15 us
  starting transfers between devices: 19.1 us -> 26.5 us
    pallas_call x0 -> x8, Pallas kernels: none -> 240 us  [the longest x1 97.1 us: shards(): pl.pallas_call(pack_rest, in_specs=[SMEM, ANY, ANY, ANY], out_specs=[ANY,...]
    all_gather x2 -> x0, waiting for transfers between devices: 71.3 us -> none  [the longest x1 71.2 us: shards(): lax.all_gather(pick_heads(v_heads, spatial_idx), 'region', axis=1, tiled=...]
    dot_general x26 -> x0, matrix products: 68.2 us -> none  [the longest x12 37.2 us: spatial_head(): jnp.dot(weights, v_one, preferred_element_type=jnp.float32)]
    all_to_all x4, waiting for transfers between devices: 59.6 us -> 2.04 us  [the longest x1 2.03 us: shards(): tm = lax.all_to_all(tm, 'frame', 0, 0, tiled=True)]
    another operation x1 -> x0, loops' own time: 47.1 us -> none  [shards(): spatial_out = lax.map(spatial_head, jnp.arange(spatial_count))]
    broadcast_in_dim x25 -> x0, local copies, waits for them, and re-layouts: 25.2 us -> none  [the longest x24 24.9 us: spatial_head(): allowed = jnp.repeat(jnp.repeat(allowed_blocks, BLK, 0), BLK, 1)]
    all_to_all x0 -> x1, blocking collectives: none -> 17.3 us  [swap(): lax.all_to_all(tensor, AXES, 0, 0, tiled=True, axis_index_groups=axis_gro...]
    gather x7 -> x0, local copies, waits for them, and re-layouts: 17.1 us -> none  [the longest x6 16.5 us: pick_heads(): return jnp.take(tensor, chosen, axis=2)]
  transfers between devices with their start and end apart: 6 -> 8, of which waited for: 5 -> 2; matrix products, arithmetic and copies ran while one was open for 9% -> 2% of each run, Pallas kernels for 0% -> 39%
where the time goes in v1:
time: 303 us; the launch traced here: 302 us
  Pallas kernels  240 us (79%)
  starting transfers between devices  26.5 us (9%)
  blocking collectives  17.3 us (6%)
  waiting for transfers between devices  9.53 us (3%)
  local copies, waits for them, and re-layouts  7.34 us (2%)
    pallas_call x1, Pallas kernels, shards(): pl.pallas_call(pack_rest, in_specs=[SMEM, ANY, ANY, ANY], out_specs=[ANY,...  97.1 us
    pallas_call x1, Pallas kernels, shards(): pl.pallas_call(pack_kv, in_specs=[SMEM, ANY, ANY], out_specs=[ANY, SMEM],...  49.9 us
    pallas_call x3, Pallas kernels, attention(): pl.pallas_call(functools.partial(attend, chunks, state is not None, last)...  31.7 us
    pallas_call x1, Pallas kernels, shards(): pl.pallas_call(place_temporal, in_specs=[SMEM, ANY], out_specs=ANY, out_s...  25.6 us
    pallas_call x1, Pallas kernels, shards(): pl.pallas_call(place_spatial, in_specs=[SMEM, ANY, ANY], out_specs=ANY, o...  25.6 us
    all_to_all x1, blocking collectives, swap(): lax.all_to_all(tensor, AXES, 0, 0, tiled=True, axis_index_groups=axis_gro...  17.3 us
    pallas_call x1, Pallas kernels, time_attention(): pl.pallas_call(attend_time, grid_spec=pltpu.PrefetchScalarGridSpec(num_sc...  10.5 us
    all_to_all x2, starting transfers between devices, swap(): lax.all_to_all(tensor, AXES, 0, 0, tiled=True, axis_index_groups=axis_gro...  10.2 us
  transfers between devices with their start and end apart: 8, of which 2 were waited for; matrix products, arithmetic and copies ran while one was open for 2% of the time, Pallas kernels for 39%

profile of v1, /device:TPU:1, one launch (start us, length us, event | category | flops | bytes accessed | tf_op | source)
XLA Modules:
  0.0 302.1 jit_solution(421520019714686877)
XLA Ops:
  0.0 97.1 %pack_rest.1 = (bf16[4,3,256,128]{3,2,1,0:T(8,128)(2,1)}, bf16[256,4608]{1,0:T(8,128)(2,1)}) custom-call(s32[24]{0:T(128)} %kind.7, bf16[256,3072]{1,0:T(8,128)(2,1)} %bitcast.27, bf16[256,3072]{1,0:T(8,128)(2,1)} %bitcast.19, bf16[256,3072]{1,0:T(8,128)(2,1)} %bitcast.21), custom_call_target="tpu_custom_call" | custom-call | bytes 6291456 | tf_op jit(solution)/shard_map/pack_rest/pallas_call | solution.py:305
  97.1 5.9 %all-to-all-start = ((bf16[4,3,256,128]{3,2,1,0:T(8,128)(2,1)}), bf16[4,3,256,128]{3,2,1,0:T(8,128)(2,1)S(1)}, u32[]{:S(2)}, u32[]{:S(2)}) async-start(bf16[4,3,256,128]{3,2,1,0:T(8,128)(2,1)} %get-tuple-element.14), calls=%async_computation | async-start | bytes 1572864 | tf_op jit(solution)/shard_map/all_to_all | solution.py:57
  103.0 49.9 %pack_keys_values.1 = (bf16[4,2,3,256,128]{4,3,2,1,0:T(8,128)(2,1)}, s32[24]{0:T(128)}) custom-call(s32[24]{0:T(128)} %kind.7, bf16[256,3072]{1,0:T(8,128)(2,1)} %bitcast.20, bf16[256,3072]{1,0:T(8,128)(2,1)} %bitcast.22), custom_call_target="tpu_custom_call" | custom-call | bytes 3145728 | tf_op jit(solution)/shard_map/pack_keys_values/pallas_call | solution.py:292
  152.9 0.0 all-to-all-done.q_ref
  152.9 0.0 copy-start.3
  152.9 17.3 %all_to_all.37.refs_0_ = bf16[4,2,3,256,128]{4,3,2,1,0:T(8,128)(2,1)} all-to-all(bf16[4,2,3,256,128]{4,3,2,1,0:T(8,128)(2,1)} %get-tuple-element.15), channel_id=1, replica_groups={{0,1,2,3},{4,5,6,7},{8,9,10,11},{12,13,14,15},{16,20,24,28},{17,21,25,2..., dimensions={0} | all-to-all | bytes 3145728 | tf_op jit(solution)/shard_map/all_to_all | solution.py:57
  170.2 0.0 copy-done.3
  170.2 0.0 copy-start.4
  170.2 0.0 copy-start.5
  170.2 5.8 %all-to-all-start.3 = ((bf16[8,32,4608]{2,1,0:T(8,128)(2,1)}), bf16[8,32,4608]{2,1,0:T(8,128)(2,1)S(1)}, u32[]{:S(2)}, u32[]{:S(2)}) async-start(bf16[8,32,4608]{2,1,0:T(8,128)(2,1)} %bitcast.8), calls=%async_computation.3 | async-start | bytes 4718592 | tf_op jit(solution)/shard_map/all_to_all | solution.py:318
  176.1 0.0 copy-start.6
  176.1 0.3 collective-permute-start
  176.4 2.4 collective-permute-start.2
  178.8 0.0 copy-done.4
  178.8 0.2 copy.11
  178.9 0.0 copy-done.5
  178.9 0.1 copy.12
  179.1 0.1 fusion
  179.2 0.8 pad.8.bias_ref
  180.0 0.0 copy-done.6
  180.0 0.1 fusion.1
  180.1 0.7 pad.9.bias_ref
  180.7 0.6 pad_add_fusion.where
  181.3 8.4 %spatial_attention.3 = (f32[3,4,256,128]{3,2,1,0:T(8,128)}, f32[3,4,256,128]{3,2,1,0:T(8,128)}) custom-call(s32[24]{0:T(128)} %get-tuple-element.13.order, s32[3]{0:T(128)} %pad_add_fusion.where, bf16[4,3,256,128]{3,2,1,0:T(8,128)(2,1)} %copy-done.3, f32[24,32,128]{2,1,0:T(8,128)} %pad.8.bias_ref, bf16[4,2,3,256,128]{4,3,2,1,0:T(8,128)(2,1)} %all_to_all.37.refs_0_), custom_call_target="tpu_custom_call" | custom-call | flops 3221225472 | bytes 4194304 | tf_op jit(solution)/shard_map/spatial_attention/pallas_call | solution.py:222
  189.7 7.5 %collective-permute-done.refs_0_ = bf16[4,2,3,256,128]{4,3,2,1,0:T(8,128)(2,1)} collective-permute-done((bf16[4,2,3,256,128]{4,3,2,1,0:T(8,128)(2,1)}, bf16[4,2,3,256,128]{4,3,2,1,0:T(8,128)(2,1)}, u32[]{:S(2)}, u32[]{:S(2)}) %collective-permute-start) | collective-permute-done | bytes 1572896 | tf_op jit(solution)/shard_map/ppermute | solution.py:61
  197.2 1.2 slice.8
  198.4 0.1 collective-permute-start.1
  198.4 0.0 collective-permute-done.2.refs_1_
  198.5 2.1 slice.9
  200.5 2.7 collective-permute-start.3
  203.2 2.0 all-to-all-done.3
  205.2 0.0 copy-start.2
  205.2 1.4 copy-done.2
  206.7 10.5 %temporal_attention.1 = bf16[256,1536]{1,0:T(8,128)(2,1)} custom-call(s32[24]{0:T(128)} %get-tuple-element.13.order, f32[24,8,128]{2,1,0:T(8,128)} %pad.9.bias_ref, bf16[256,4608]{1,0:T(8,128)(2,1)} %bitcast.24, bf16[256,4608]{1,0:T(8,128)(2,1)} %bitcast.25, bf16[256,4608]{1,0:T(8,128)(2,1)} %bitcast.26), custom_call_target="tpu_custom_call" | custom-call | flops 4294967296 | bytes 4194304 | tf_op jit(solution)/shard_map/temporal_attention/pallas_call | solution.py:261
  217.2 5.0 %all-to-all-start.4 = ((bf16[8,32,1536]{2,1,0:T(8,128)(2,1)}), bf16[8,32,1536]{2,1,0:T(8,128)(2,1)S(1)}, u32[]{:S(2)}, u32[]{:S(2)}) async-start(bf16[8,32,1536]{2,1,0:T(8,128)(2,1)} %bitcast.28), calls=%async_computation.4 | async-start | bytes 1572864 | tf_op jit(solution)/shard_map/all_to_all | solution.py:341
  222.2 14.1 %spatial_attention.4 = (f32[3,4,256,128]{3,2,1,0:T(8,128)}, f32[3,4,256,128]{3,2,1,0:T(8,128)}) custom-call(s32[24]{0:T(128)} %get-tuple-element.13.order, s32[3]{0:T(128)} %pad_add_fusion.where, bf16[4,3,256,128]{3,2,1,0:T(8,128)(2,1)} %copy-done.3, f32[24,32,128]{2,1,0:T(8,128)} %pad.8.bias_ref, bf16[4,2,3,256,128]{4,3,2,1,0:T(8,128)(2,1)} %collective-permute-done.refs_0_, ...), custom_call_target="tpu_custom_call" | custom-call | flops 6442450944 | bytes 4194304 | tf_op jit(solution)/shard_map/spatial_attention/pallas_call | solution.py:222
  236.3 0.0 collective-permute-done.1.refs_0_
  236.3 0.0 collective-permute-done.3.refs_1_
  236.3 9.2 %spatial_attention.5 = bf16[4,3,256,128]{3,2,1,0:T(8,128)(2,1)} custom-call(s32[24]{0:T(128)} %get-tuple-element.13.order, s32[3]{0:T(128)} %pad_add_fusion.where, bf16[4,3,256,128]{3,2,1,0:T(8,128)(2,1)} %copy-done.3, f32[24,32,128]{2,1,0:T(8,128)} %pad.8.bias_ref, bf16[2,2,3,256,128]{4,3,2,1,0:T(8,128)(2,1)} %collective-permute-done.1.refs_0_, ...), custom_call_target="tpu_custom_call" | custom-call | flops 3221225472 | bytes 4194304 | tf_op jit(solution)/shard_map/spatial_attention/pallas_call | solution.py:222
  245.6 0.0 all-to-all-done.4
  245.6 0.0 copy-start
  245.6 4.4 %all-to-all-start.2 = ((bf16[4,3,256,128]{3,2,1,0:T(8,128)(2,1)}), bf16[4,3,256,128]{3,2,1,0:T(8,128)(2,1)S(1)}, u32[]{:S(2)}, u32[]{:S(2)}) async-start(bf16[4,3,256,128]{3,2,1,0:T(8,128)(2,1)} %spatial_attention.5), calls=%async_computation.2 | async-start | bytes 1572864 | tf_op jit(solution)/shard_map/all_to_all | solution.py:57
  249.9 0.0 copy-done
  249.9 25.6 %place_temporal.1.base_ref = bf16[256,3072]{1,0:T(8,128)(2,1)} custom-call(s32[24]{0:T(128)} %kind.7, bf16[256,1536]{1,0:T(8,128)(2,1)} %bitcast.23), custom_call_target="tpu_custom_call" | custom-call | bytes 2097152 | tf_op jit(solution)/shard_map/place_temporal/pallas_call | solution.py:343
  275.6 0.0 all-to-all-done.2.src_ref
  275.6 0.0 copy-start.1
  275.6 0.9 copy-done.1
  276.5 25.6 %place_spatial.1 = bf16[256,3072]{1,0:T(8,128)(2,1)} custom-call(s32[24]{0:T(128)} %kind.7, bf16[4,3,256,128]{3,2,1,0:T(8,128)(2,1)} %copy-done.1, bf16[256,3072]{1,0:T(8,128)(2,1)} %place_temporal.1.base_ref), custom_call_target="tpu_custom_call", output_to_operand_aliasing={{}: (2, {})} | custom-call | bytes 2097152 | tf_op jit(solution)/shard_map/place_spatial/pallas_call | solution.py:353
  (3 shorter events, 0.0 us)
Async XLA Ops:
  97.1 55.8 %all-to-all-start = ((bf16[4,3,256,128]{3,2,1,0:T(8,128)(2,1)}), bf16[4,3,256,128]{3,2,1,0:T(8,128)(2,1)S(1)}, u32[]{:S(2)}, u32[]{:S(2)}) async-start(bf16[4,3,256,128]{3,2,1,0:T(8,128)(2,1)} %get-tuple-element.14), calls=%async_computation | async-start | bytes 1572864 | tf_op jit(solution)/shard_map/all_to_all | solution.py:57
  152.9 17.3 %copy-start.3 = (bf16[4,3,256,128]{3,2,1,0:T(8,128)(2,1)}, bf16[4,3,256,128]{3,2,1,0:T(8,128)(2,1)S(1)}, u32[]{:S(2)}) copy-start(bf16[4,3,256,128]{3,2,1,0:T(8,128)(2,1)S(1)} %all-to-all-done.q_ref) | copy-start | bytes 2359300
  170.2 8.5 %copy-start.4 = (s32[24,32,32]{2,1,0:T(8,128)S(1)}, s32[24,32,32]{2,1,0:T(8,128)}, u32[]{:S(2)}) copy-start(s32[24,32,32]{2,1,0:T(8,128)} %param.11) | copy-start | bytes 294916
  170.2 8.7 %copy-start.5 = (s32[24,8,8]{0,2,1:T(8,128)S(1)}, s32[24,8,8]{0,2,1:T(8,128)}, u32[]{:S(2)}) copy-start(s32[24,8,8]{0,2,1:T(8,128)} %param.12) | copy-start | bytes 18436
  170.2 35.0 %all-to-all-start.3 = ((bf16[8,32,4608]{2,1,0:T(8,128)(2,1)}), bf16[8,32,4608]{2,1,0:T(8,128)(2,1)S(1)}, u32[]{:S(2)}, u32[]{:S(2)}) async-start(bf16[8,32,4608]{2,1,0:T(8,128)(2,1)} %bitcast.8), calls=%async_computation.3 | async-start | bytes 4718592 | tf_op jit(solution)/shard_map/all_to_all | solution.py:318
  176.1 3.9 %copy-start.6 = (s32[8]{0:T(128)S(1)}, s32[8]{0:T(128)}, u32[]{:S(2)}) copy-start(s32[8]{0:T(128)} %param.13) | copy-start | bytes 100
  176.1 21.1 %collective-permute-start = (bf16[4,2,3,256,128]{4,3,2,1,0:T(8,128)(2,1)}, bf16[4,2,3,256,128]{4,3,2,1,0:T(8,128)(2,1)}, u32[]{:S(2)}, u32[]{:S(2)}) collective-permute-start(bf16[4,2,3,256,128]{4,3,2,1,0:T(8,128)(2,1)} %all_to_all.37.refs_0_), channel_id=1, source_target_pairs={{0,4},{1,5},{2,6},{3,7},{4,8},{5,9},{6,10},{7,11},{8,12},{9,13},{1... | collective-permute-start | bytes 4718600 | tf_op jit(solution)/shard_map/ppermute | solution.py:61
  176.4 22.1 %collective-permute-start.2 = (bf16[4,2,3,256,128]{4,3,2,1,0:T(8,128)(2,1)}, bf16[4,2,3,256,128]{4,3,2,1,0:T(8,128)(2,1)}, u32[]{:S(2)}, u32[]{:S(2)}) collective-permute-start(bf16[4,2,3,256,128]{4,3,2,1,0:T(8,128)(2,1)} %all_to_all.37.refs_0_), channel_id=1, source_target_pairs={{0,12},{1,13},{2,14},{3,15},{4,0},{5,1},{6,2},{7,3},{8,4},{9,5},{1... | collective-permute-start | bytes 4718600 | tf_op jit(solution)/shard_map/ppermute | solution.py:61
  198.4 38.0 %collective-permute-start.1 = (bf16[2,2,3,256,128]{4,3,2,1,0:T(8,128)(2,1)S(1)}, bf16[2,2,3,256,128]{4,3,2,1,0:T(8,128)(2,1)}, u32[]{:S(2)}, u32[]{:S(2)}) collective-permute-start(bf16[2,2,3,256,128]{4,3,2,1,0:T(8,128)(2,1)S(1)} %slice.8), channel_id=1, source_target_pairs={{0,4},{1,5},{2,6},{3,7},{4,8},{5,9},{6,10},{7,11},{8,12},{9,13},{1... | collective-permute-start | bytes 2359304 | tf_op jit(solution)/shard_map/ppermute | solution.py:61
  200.5 35.8 %collective-permute-start.3 = (bf16[2,2,3,256,128]{4,3,2,1,0:T(8,128)(2,1)}, bf16[2,2,3,256,128]{4,3,2,1,0:T(8,128)(2,1)}, u32[]{:S(2)}, u32[]{:S(2)}) collective-permute-start(bf16[2,2,3,256,128]{4,3,2,1,0:T(8,128)(2,1)} %slice.9), channel_id=1, source_target_pairs={{0,12},{1,13},{2,14},{3,15},{4,0},{5,1},{6,2},{7,3},{8,4},{9,5},{1... | collective-permute-start | bytes 2359304 | tf_op jit(solution)/shard_map/ppermute | solution.py:61
  205.2 1.4 copy-start.2
  217.2 28.4 %all-to-all-start.4 = ((bf16[8,32,1536]{2,1,0:T(8,128)(2,1)}), bf16[8,32,1536]{2,1,0:T(8,128)(2,1)S(1)}, u32[]{:S(2)}, u32[]{:S(2)}) async-start(bf16[8,32,1536]{2,1,0:T(8,128)(2,1)} %bitcast.28), calls=%async_computation.4 | async-start | bytes 1572864 | tf_op jit(solution)/shard_map/all_to_all | solution.py:341
  245.6 4.4 %copy-start = (bf16[8,32,1536]{2,1,0:T(8,128)(2,1)}, bf16[8,32,1536]{2,1,0:T(8,128)(2,1)S(1)}, u32[]{:S(2)}) copy-start(bf16[8,32,1536]{2,1,0:T(8,128)(2,1)S(1)} %all-to-all-done.4) | copy-start | bytes 2359300
  245.6 30.0 %all-to-all-start.2 = ((bf16[4,3,256,128]{3,2,1,0:T(8,128)(2,1)}), bf16[4,3,256,128]{3,2,1,0:T(8,128)(2,1)S(1)}, u32[]{:S(2)}, u32[]{:S(2)}) async-start(bf16[4,3,256,128]{3,2,1,0:T(8,128)(2,1)} %spatial_attention.5), calls=%async_computation.2 | async-start | bytes 1572864 | tf_op jit(solution)/shard_map/all_to_all | solution.py:57
  275.6 0.9 copy-start.1

commit v2 on v1

v2 whole, which is shorter than its diff:
```python
import functools

import jax
import jax.numpy as jnp
from jax import lax
from jax.experimental import pallas as pl
from jax.experimental.pallas import tpu as pltpu
from jax.sharding import PartitionSpec as P

HEADS = 24
TEMP_HEADS = 12
SPAT_HEADS = HEADS - TEMP_HEADS
BLK = 128
HEAD = 128
RING = 4
GROUP = SPAT_HEADS // RING
FRAMES = 8
ROWS = 256
PART = ROWS // FRAMES
WIDTH = HEADS * HEAD
NEG = -1e30
LEVEL = 32
LARGE = 2.0**100
STEP = 1024
TIME_STEP = 6
LOG2_SCALE = 1.4426950408889634 / HEAD**0.5
AXES = ("frame", "region")
VMEM = 56 * 1024 * 1024
BF16 = jnp.bfloat16
F32 = jnp.float32
ANY = pl.BlockSpec(memory_space=pl.ANY)
SMEM = pl.BlockSpec(memory_space=pltpu.SMEM)


def flat(y, core, z, x):
    return ((y * 2 + core) * RING + z) * RING + x


def axis_groups(first):
    groups = []
    for y in range(RING):
        for core in range(2):
            along_x = (core == 0) == first
            for other in range(RING):
                groups.append([
                    flat(y, core, other, i) if along_x else flat(y, core, i, other)
                    for i in range(RING)
                ])
    return groups


def ring_pairs(first, shift):
    pairs = []
    for group in axis_groups(first):
        for i in range(RING):
            pairs.append((group[i], group[(i + shift) % RING]))
    return sorted(pairs)


def swap(tensor):
    return lax.all_to_all(tensor, AXES, 0, 0, tiled=True, axis_index_groups=axis_groups(True))


def shift(tensor, step):
    return lax.ppermute(tensor, AXES, ring_pairs(False, step))


def columns(index):
    return pl.ds(pl.multiple_of(index * HEAD, HEAD), HEAD)


def pack_kv(kind, k_ref, v_ref, kv_ref, order_ref, held, sem_in, sem_out):
    spatial = jnp.int32(0)
    temporal = jnp.int32(0)
    for head in range(HEADS):
        one = kind[head]

        @pl.when(one == 0)
        def _(spatial=spatial, head=head):
            group, place = spatial // GROUP, spatial % GROUP
            for which, ref in enumerate((k_ref, v_ref)):
                pltpu.make_async_copy(
                    ref.at[:, pl.ds(head * HEAD, HEAD)],
                    held.at[which, group, place],
                    sem_in.at[which],
                ).start()

        order_ref[jnp.where(one == 1, SPAT_HEADS + temporal, spatial)] = head
        spatial += 1 - one
        temporal += one
    copies = [
        pltpu.make_async_copy(held.at[which], kv_ref.at[:, which], sem_out.at[which])
        for which in range(2)
    ]
    for which, copy in enumerate(copies):
        pltpu.make_async_copy(held.at[which], held.at[which], sem_in.at[which]).wait()
        copy.start()
    for copy in copies:
        copy.wait()


def pack_rest(kind, order, q_ref, k_ref, v_ref, sq_ref, tm_ref, held_s, held_t, sem_in, sem_out):
    spatial = jnp.int32(0)
    temporal = jnp.int32(0)
    for head in range(HEADS):
        one = kind[head]

        @pl.when(one == 0)
        def _(spatial=spatial, head=head):
            pltpu.make_async_copy(
                q_ref.at[:, pl.ds(head * HEAD, HEAD)],
                held_s.at[spatial // GROUP, spatial % GROUP],
                sem_in.at[0],
            ).start()

        @pl.when(one == 1)
        def _(temporal=temporal, head=head):
            for which, ref in enumerate((q_ref, k_ref, v_ref)):
                pltpu.make_async_copy(
                    ref.at[:, pl.ds(head * HEAD, HEAD)],
                    held_t.at[:, columns(which * TEMP_HEADS + temporal)],
                    sem_in.at[1],
                ).start()

        spatial += 1 - one
        temporal += one
    copies = []
    for which, (held, ref) in enumerate(((held_s, sq_ref), (held_t, tm_ref))):
        pltpu.make_async_copy(held, held, sem_in.at[which]).wait()
        copies.append(pltpu.make_async_copy(held, ref, sem_out.at[which]))
        copies[-1].start()
    for copy in copies:
        copy.wait()


def place_temporal(kind, src_ref, out_ref, held, sem_in, sem_out):
    copy = pltpu.make_async_copy(src_ref, held, sem_in)
    copy.start()
    copy.wait()
    temporal = jnp.int32(0)
    for head in range(HEADS):
        one = kind[head]

        @pl.when(one == 1)
        def _(temporal=temporal, head=head):
            pltpu.make_async_copy(
                held.at[:, columns(temporal)], out_ref.at[:, pl.ds(head * HEAD, HEAD)], sem_out
            ).start()

        temporal += one
    pltpu.make_async_copy(held, held, sem_out).wait()


def place_spatial(kind, src_ref, base_ref, out_ref, held, sem_in, sem_out):
    copy = pltpu.make_async_copy(src_ref, held, sem_in)
    copy.start()
    copy.wait()
    spatial = jnp.int32(0)
    for head in range(HEADS):
        one = kind[head]

        @pl.when(one == 0)
        def _(spatial=spatial, head=head):
            pltpu.make_async_copy(
                held.at[spatial // GROUP, spatial % GROUP],
                out_ref.at[:, pl.ds(head * HEAD, HEAD)],
                sem_out,
            ).start()

        spatial += 1 - one
    pltpu.make_async_copy(held, held, sem_out).wait()


def region_of(where, piece, ring):
    return jnp.where(where[0] == 0, ring * RING + piece, piece * RING + ring)


def mark_queries(where, q_ref, k_ref, marked_ref):
    lane = lax.broadcasted_iota(jnp.int32, (ROWS, HEAD), 1)
    half = lax.broadcasted_iota(jnp.int32, (ROWS, HEAD), 0) // BLK
    for piece in range(RING):
        block = region_of(where, piece, where[1]) * (ROWS // BLK) + half
        query = q_ref[piece, 0]
        level = jnp.sum(
            query.astype(F32) * k_ref[piece, 0, 0].astype(F32), axis=1, keepdims=True
        )
        mark = jnp.where(lane == block, 1.0, jnp.where(lane == LEVEL, -level, 0.0))
        rows = pl.ds(piece * ROWS, ROWS)
        marked_ref[0, rows, :HEAD] = query
        marked_ref[0, rows, HEAD:] = mark.astype(BF16)


def mark_keys(where, bias_ref, region, keys, row):
    for half in range(ROWS // BLK):
        line = bias_ref[0, pl.ds(region * (ROWS // BLK) + half, 1), :]
        keys[pl.ds(row + half * BLK, BLK), HEAD:] = jnp.broadcast_to(line, (BLK, HEAD)).astype(BF16)


def attend_again(all_chunks, where, bias_ref, marked_ref, kv_all, out_ref, keys, vals, top_ref, sum_ref, acc_ref, sem):
    head = pl.program_id(0)
    lane = lax.broadcasted_iota(jnp.int32, (ROWS, 2 * HEAD), 1)
    top_ref[...] = jnp.full(top_ref.shape, -3e38, F32)
    sum_ref[...] = jnp.zeros(sum_ref.shape, F32)
    acc_ref[...] = jnp.zeros(acc_ref.shape, F32)
    for (offset, pieces), kv_ref in zip(all_chunks, kv_all):
        source = (where[1] + offset) % RING

        @pl.loop(0, len(pieces))
        def _(slot, kv_ref=kv_ref, pieces=pieces, source=source):
            copies = [
                pltpu.make_async_copy(kv_ref.at[slot, 0, head], keys.at[:, :HEAD], sem.at[0]),
                pltpu.make_async_copy(kv_ref.at[slot, 1, head], vals, sem.at[1]),
            ]
            for copy in copies:
                copy.start()
            mark_keys(where, bias_ref, region_of(where, slot + pieces[0], source), keys, 0)
            for copy in copies:
                copy.wait()
            for piece in range(RING):
                rows = pl.ds(piece * ROWS, ROWS)
                query = marked_ref[0, rows, :]
                query = jnp.where(lane == HEAD + LEVEL, jnp.zeros_like(query), query)
                scores = lax.dot_general(
                    query, keys[...], (((1,), (1,)), ((), ())), preferred_element_type=F32
                )
                old = top_ref[rows, :]
                top = jnp.maximum(old, jnp.max(scores, axis=1, keepdims=True))
                decay = jnp.exp2((old - top) * LOG2_SCALE)
                weights = jnp.exp2((scores - top[:, :1]) * LOG2_SCALE).astype(BF16)
                sums = jnp.sum(weights.astype(F32), axis=1, keepdims=True)
                total = jnp.dot(weights, vals[...], preferred_element_type=F32)
                top_ref[rows, :] = top
                sum_ref[rows, :] = sum_ref[rows, :] * decay + sums
                acc_ref[rows, :] = acc_ref[rows, :] * decay + total

    for piece in range(RING):
        rows = pl.ds(piece * ROWS, ROWS)
        out_ref[piece, 0] = (acc_ref[rows, :] / sum_ref[rows, :]).astype(BF16)


def attend(chunks, all_chunks, first, order, where, bias_ref, *refs):
    kv_refs, refs = refs[: len(chunks)], refs[len(chunks):]
    last = all_chunks is not None
    if first:
        q_ref, marked_ref, state_ref, keys, vals = refs
        mark_queries(where, q_ref, kv_refs[0], marked_ref)
        state = jnp.zeros((HEAD + 8, RING * ROWS), F32)
    else:
        marked_ref, before_ref = refs[:2]
        state = before_ref[0]
        if last:
            kv_all, refs = refs[2:2 + len(all_chunks)], refs[2 + len(all_chunks):]
            out_ref, keys, vals = refs[:3]
        else:
            state_ref, keys, vals = refs[2:]
    row = 0
    for (offset, pieces), kv_ref in zip(chunks, kv_refs):
        source = (where[1] + offset) % RING
        for slot, piece in enumerate(pieces):
            keys[pl.ds(row, ROWS), :HEAD] = kv_ref[slot, 0, 0]
            mark_keys(where, bias_ref, region_of(where, piece, source), keys, row)
            vals[:HEAD, pl.ds(row, ROWS)] = kv_ref[slot, 1, 0].T
            row += ROWS
    vals[HEAD:, :] = jnp.ones((8, row), BF16)
    span = min(row, STEP)
    for start in range(0, row, span):
        scores = lax.dot_general(
            keys[pl.ds(start, span), :],
            marked_ref[0],
            (((1,), (1,)), ((), ())),
            preferred_element_type=F32,
        )
        weights = jnp.exp2(scores * LOG2_SCALE).astype(BF16)
        state += lax.dot_general(
            vals[:, pl.ds(start, span)],
            weights,
            (((1,), (0,)), ((), ())),
            preferred_element_type=F32,
        )
    if not last:
        state_ref[0] = state
        return
    sums = state[HEAD:HEAD + 1]
    result = state[:HEAD] / sums
    for piece in range(RING):
        out_ref[piece, 0] = result[:, piece * ROWS:(piece + 1) * ROWS].T.astype(BF16)
    fine = jnp.max(jnp.where(sums < LARGE, 0.0, 1.0)) == 0.0

    @pl.when(jnp.logical_not(fine))
    def _():
        attend_again(all_chunks, where, bias_ref, marked_ref, kv_all, out_ref, *refs[3:])


def attention(order, where, bias, chunks, arrays, queries=None, carried=None, everything=None):
    keys = sum(len(pieces) for _, pieces in chunks) * ROWS
    tokens = RING * ROWS
    kv_specs = [
        pl.BlockSpec((len(pieces), 2, 1, ROWS, HEAD), lambda h, o, w: (0, 0, h, 0, 0))
        for _, pieces in chunks
    ]
    bias_spec = pl.BlockSpec(
        (1, bias.shape[1], HEAD), lambda h, o, w: (o[w[2] * GROUP + h], 0, 0)
    )
    q_spec = pl.BlockSpec((RING, 1, ROWS, HEAD), lambda h, o, w: (0, h, 0, 0))
    marked_spec = pl.BlockSpec((1, tokens, 2 * HEAD), lambda h, o, w: (h, 0, 0))
    state_spec = pl.BlockSpec((1, HEAD + 8, tokens), lambda h, o, w: (h, 0, 0))
    marked_shape = jax.ShapeDtypeStruct((GROUP, tokens, 2 * HEAD), BF16)
    state_shape = jax.ShapeDtypeStruct((GROUP, HEAD + 8, tokens), F32)
    scratch = [pltpu.VMEM((keys, 2 * HEAD), BF16), pltpu.VMEM((HEAD + 8, keys), BF16)]
    all_chunks = None
    if queries is not None:
        more, more_specs = [queries], [q_spec]
        out_specs, out_shape = [marked_spec, state_spec], [marked_shape, state_shape]
    elif everything is None:
        more, more_specs = list(carried), [marked_spec, state_spec]
        out_specs, out_shape = state_spec, state_shape
    else:
        all_chunks, all_arrays = everything
        more = list(carried) + list(all_arrays)
        more_specs = [marked_spec, state_spec] + [ANY] * len(all_arrays)
        out_specs = q_spec
        out_shape = jax.ShapeDtypeStruct((RING, GROUP, ROWS, HEAD), BF16)
        scratch += [pltpu.VMEM((ROWS, 2 * HEAD), BF16), pltpu.VMEM((ROWS, HEAD), BF16)]
        scratch += [pltpu.VMEM((tokens, HEAD), F32)] * 3 + [pltpu.SemaphoreType.DMA((2,))]
    flops = 8 * GROUP * tokens * keys * HEAD
    return pl.pallas_call(
        functools.partial(attend, chunks, all_chunks, queries is not None),
        grid_spec=pltpu.PrefetchScalarGridSpec(
            num_scalar_prefetch=2,
            grid=(GROUP,),
            in_specs=[bias_spec] + kv_specs + more_specs,
            out_specs=out_specs,
            scratch_shapes=scratch,
        ),
        out_shape=out_shape,
        compiler_params=pltpu.CompilerParams(vmem_limit_bytes=VMEM),
        cost_estimate=pl.CostEstimate(flops=flops, bytes_accessed=4 << 20, transcendentals=0),
        name="spatial_attention",
    )(order, where, bias, *arrays, *more)


def attend_time(order, bias_ref, q_ref, k_ref, v_ref, out_ref):
    lane = lax.broadcasted_iota(jnp.int32, (ROWS, HEAD), 1)
    row = lax.broadcasted_iota(jnp.int32, (ROWS, HEAD), 0)
    frame, place = row // PART, row % PART
    mark = jnp.where((lane == frame) | (lane == FRAMES + place), 1.0, 0.0).astype(BF16)
    apart = jnp.where(
        (lane >= FRAMES) & (lane < FRAMES + PART) & (lane != FRAMES + place), NEG, 0.0
    )
    ones = jnp.ones((ROWS, HEAD), BF16)
    for slot in range(TIME_STEP):
        head = order[SPAT_HEADS + pl.program_id(0) * TIME_STEP + slot]
        at = slice(slot * HEAD, (slot + 1) * HEAD)
        pairs = jnp.broadcast_to(bias_ref[head][:, None, :], (FRAMES, PART, HEAD))
        pairs = pairs.reshape(ROWS, HEAD)
        query = jnp.concatenate([q_ref[:, at], mark], axis=1)
        keys = jnp.concatenate([k_ref[:, at], (pairs + apart).astype(BF16)], axis=1)
        vals = jnp.concatenate([v_ref[:, at], ones], axis=1)
        scores = lax.dot_general(
            query, keys, (((1,), (1,)), ((), ())), preferred_element_type=F32
        )
        top = jnp.max(scores, axis=1, keepdims=True)
        weights = jnp.exp2((scores - top) * LOG2_SCALE).astype(BF16)
        both = jnp.dot(weights, vals, preferred_element_type=F32)
        out_ref[:, at] = (both[:, :HEAD] / both[:, HEAD:]).astype(BF16)


def time_attention(order, bias, gathered):
    steps = TEMP_HEADS // TIME_STEP

    def at(which):
        return pl.BlockSpec((ROWS, TIME_STEP * HEAD), lambda h, o: (0, which * steps + h))

    return pl.pallas_call(
        attend_time,
        grid_spec=pltpu.PrefetchScalarGridSpec(
            num_scalar_prefetch=1,
            grid=(steps,),
            in_specs=[pl.BlockSpec(bias.shape, lambda h, o: (0, 0, 0))]
            + [at(which) for which in range(3)],
            out_specs=at(0),
        ),
        out_shape=jax.ShapeDtypeStruct((ROWS, TEMP_HEADS * HEAD), BF16),
        compiler_params=pltpu.CompilerParams(vmem_limit_bytes=VMEM),
        cost_estimate=pl.CostEstimate(flops=3 << 30, bytes_accessed=4 << 20, transcendentals=0),
        name="temporal_attention",
    )(order, bias, gathered, gathered, gathered)


def moved(count):
    return pl.CostEstimate(flops=0, bytes_accessed=count, transcendentals=0)


def shards(queries, keys, values, head_kind, spatial_mask, temporal_mask, frame_valid):
    rows, width = queries.shape[1:]
    queries, keys, values = (t.reshape(rows, width) for t in (queries, keys, values))
    dma = pltpu.SemaphoreType.DMA
    core = lax.axis_index("frame") % 2
    region = lax.axis_index("region")
    place_z, place_x = region // RING, region % RING
    own = jnp.where(core == 0, place_x, place_z)
    ring = jnp.where(core == 0, place_z, place_x)
    where = jnp.stack([core, ring, own]).astype(jnp.int32)

    pair = pltpu.SemaphoreType.DMA((2,))
    spatial_shape = (RING, GROUP, rows, HEAD)
    time_shape = (rows, TEMP_HEADS * HEAD)
    kv, order = pl.pallas_call(
        pack_kv,
        in_specs=[SMEM, ANY, ANY],
        out_specs=[ANY, SMEM],
        out_shape=[
            jax.ShapeDtypeStruct((RING, 2, GROUP, rows, HEAD), BF16),
            jax.ShapeDtypeStruct((HEADS,), jnp.int32),
        ],
        scratch_shapes=[pltpu.VMEM((2,) + spatial_shape, BF16), pair, pair],
        compiler_params=pltpu.CompilerParams(vmem_limit_bytes=VMEM),
        cost_estimate=moved(3 << 20),
        name="pack_keys_values",
    )(head_kind, keys, values)
    kv = swap(kv)
    sq, tm = pl.pallas_call(
        pack_rest,
        in_specs=[SMEM, SMEM, ANY, ANY, ANY],
        out_specs=[ANY, ANY],
        out_shape=[
            jax.ShapeDtypeStruct(spatial_shape, BF16),
            jax.ShapeDtypeStruct((rows, 3 * TEMP_HEADS * HEAD), BF16),
        ],
        scratch_shapes=[
            pltpu.VMEM(spatial_shape, BF16),
            pltpu.VMEM((rows, 3 * TEMP_HEADS * HEAD), BF16),
            pair,
            pair,
        ],
        compiler_params=pltpu.CompilerParams(vmem_limit_bytes=VMEM),
        cost_estimate=moved(6 << 20),
        name="pack_rest",
    )(head_kind, order, queries, keys, values)
    sq = swap(sq)
    tm = lax.all_to_all(tm, "frame", 0, 0, tiled=True)

    blocks = spatial_mask.shape[1]
    same = jnp.eye(blocks, dtype=jnp.bool_)[None]
    bias = jnp.where((jnp.swapaxes(spatial_mask, 1, 2) == 1) | same, 0.0, NEG).astype(F32)
    bias = jnp.pad(bias, ((0, 0), (0, 0), (0, HEAD - blocks)), constant_values=1.0)
    alike = jnp.eye(FRAMES, dtype=jnp.bool_)[None]
    seen = (jnp.swapaxes(temporal_mask, 1, 2) == 1) & (frame_valid[None, :, None] == 1)
    time_bias = jnp.where(seen | alike, 0.0, NEG).astype(F32)
    time_bias = jnp.pad(time_bias, ((0, 0), (0, 0), (0, HEAD - FRAMES)))

    whole = tuple(range(RING))
    half = RING // 2
    right, left = shift(kv, 1), shift(kv, RING - 1)
    marked, state = attention(order, where, bias, [(0, whole)], [kv], queries=sq)
    right2, left2 = shift(right[:half], 1), shift(left[half:], RING - 1)
    near = [(RING - 1, whole), (1, whole)]
    far = [(2, whole[:half]), (2, whole[half:])]
    state = attention(order, where, bias, near, [right, left], carried=(marked, state))
    everything = ([(0, whole)] + near + far, [kv, right, left, right2, left2])
    spatial = attention(
        order, where, bias, far, [right2, left2], carried=(marked, state), everything=everything
    )
    time_out = time_attention(order, time_bias, tm)
    time_out = lax.all_to_all(time_out, "frame", 0, 0, tiled=True)
    out_shape = jax.ShapeDtypeStruct((rows, width), BF16)
    base = pl.pallas_call(
        place_temporal,
        in_specs=[SMEM, ANY],
        out_specs=ANY,
        out_shape=out_shape,
        scratch_shapes=[pltpu.VMEM(time_shape, BF16), dma, dma],
        compiler_params=pltpu.CompilerParams(vmem_limit_bytes=VMEM),
        cost_estimate=moved(2 << 20),
        name="place_temporal",
    )(head_kind, time_out)
    spatial = swap(spatial)
    result = pl.pallas_call(
        place_spatial,
        in_specs=[SMEM, ANY, ANY],
        out_specs=ANY,
        out_shape=out_shape,
        scratch_shapes=[pltpu.VMEM(spatial_shape, BF16), dma, dma],
        compiler_params=pltpu.CompilerParams(vmem_limit_bytes=VMEM),
        input_output_aliases={2: 0},
        cost_estimate=moved(2 << 20),
        name="place_spatial",
    )(head_kind, spatial, base)
    return result[None]


def solution(mesh):
    wide = P("frame", "region", None)
    return jax.shard_map(
        shards,
        mesh=mesh,
        in_specs=(wide, wide, wide, P(), P(), P(), P()),
        out_specs=wide,
        check_vma=False,
    )
```

time: 303 us -> 118 us (0.39)
  Pallas kernels: 240 us -> 40.9 us
  blocking collectives: 17.3 us -> 29.7 us
  starting transfers between devices: 26.5 us -> 21.1 us
  waiting for transfers between devices: 9.53 us -> 14.9 us
    pallas_call x4, Pallas kernels: 129 us -> 26.8 us  [the longest x3 22.5 us: attention(): pl.pallas_call(functools.partial(attend, chunks, all_chunks, queries is n...]
    pallas_call x1, Pallas kernels: 49.9 us -> 3.86 us  [shards(): pl.pallas_call(pack_kv, in_specs=[SMEM, ANY, ANY], out_specs=[ANY, SMEM],...]
    pallas_call x1, Pallas kernels: 25.6 us -> 2.67 us  [shards(): pl.pallas_call(place_temporal, in_specs=[SMEM, ANY], out_specs=ANY, out_s...]
    pallas_call x1, Pallas kernels: 25.6 us -> 2.67 us  [shards(): pl.pallas_call(place_spatial, in_specs=[SMEM, ANY, ANY], out_specs=ANY, o...]
    all_to_all x1 -> x2, blocking collectives: 17.3 us -> 29.7 us  [swap(): lax.all_to_all(tensor, AXES, 0, 0, tiled=True, axis_index_groups=axis_gro...]
    all_to_all x2 -> x1, waiting for transfers between devices: 0.01 us -> 5.66 us  [swap(): lax.all_to_all(tensor, AXES, 0, 0, tiled=True, axis_index_groups=axis_gro...]
    pallas_call x1, Pallas kernels: 10.5 us -> 4.9 us  [time_attention(): pl.pallas_call(attend_time, grid_spec=pltpu.PrefetchScalarGridSpec(num_sc...]
    all_to_all x2 -> x1, starting transfers between devices: 10.2 us -> 4.98 us  [swap(): lax.all_to_all(tensor, AXES, 0, 0, tiled=True, axis_index_groups=axis_gro...]
  transfers between devices with their start and end apart: 8 -> 7, of which waited for: 2 -> 3; matrix products, arithmetic and copies ran while one was open for 2% -> 7% of each run, Pallas kernels for 39% -> 26%
where the time goes in v2:
time: 118 us; the launch traced here: 117 us
  Pallas kernels  40.9 us (35%)
  blocking collectives  29.7 us (25%)
  starting transfers between devices  21.1 us (18%)
  waiting for transfers between devices  14.9 us (13%)
  local copies, waits for them, and re-layouts  9.03 us (8%)
    all_to_all x2, blocking collectives, swap(): lax.all_to_all(tensor, AXES, 0, 0, tiled=True, axis_index_groups=axis_gro...  29.7 us
    pallas_call x3, Pallas kernels, attention(): pl.pallas_call(functools.partial(attend, chunks, all_chunks, queries is n...  22.5 us
    ppermute x4, waiting for transfers between devices, shift(): return lax.ppermute(tensor, AXES, ring_pairs(False, step))  6.73 us
    all_to_all x1, starting transfers between devices, shards(): tm = lax.all_to_all(tm, 'frame', 0, 0, tiled=True)  6.41 us
    all_to_all x1, waiting for transfers between devices, swap(): lax.all_to_all(tensor, AXES, 0, 0, tiled=True, axis_index_groups=axis_gro...  5.66 us
    ppermute x4, starting transfers between devices, shift(): return lax.ppermute(tensor, AXES, ring_pairs(False, step))  5.35 us
    all_to_all x1, starting transfers between devices, swap(): lax.all_to_all(tensor, AXES, 0, 0, tiled=True, axis_index_groups=axis_gro...  4.98 us
    pallas_call x1, Pallas kernels, time_attention(): pl.pallas_call(attend_time, grid_spec=pltpu.PrefetchScalarGridSpec(num_sc...  4.9 us
  transfers between devices with their start and end apart: 7, of which 3 were waited for; matrix products, arithmetic and copies ran while one was open for 7% of the time, Pallas kernels for 26%

profile of v2, /device:TPU:1, one launch (start us, length us, event | category | flops | bytes accessed | tf_op | source)
XLA Modules:
  0.0 116.8 jit_solution(7333895271795288118)
XLA Ops:
  0.0 3.9 %pack_keys_values.1 = (bf16[4,2,3,256,128]{4,3,2,1,0:T(8,128)(2,1)}, s32[24]{0:T(128)}) custom-call(s32[24]{0:T(128)} %kind.7, bf16[256,3072]{1,0:T(8,128)(2,1)} %bitcast.19, bf16[256,3072]{1,0:T(8,128)(2,1)} %bitcast.21), custom_call_target="tpu_custom_call" | custom-call | bytes 3145728 | tf_op jit(solution)/shard_map/pack_keys_values/pallas_call | solution.py:408
  3.9 4.4 %pack_rest.1 = (bf16[4,3,256,128]{3,2,1,0:T(8,128)(2,1)}, bf16[256,4608]{1,0:T(8,128)(2,1)}) custom-call(s32[24]{0:T(128)} %kind.7, s32[24]{0:T(128)} %get-tuple-element.11.order, bf16[256,3072]{1,0:T(8,128)(2,1)} %bitcast.25, bf16[256,3072]{1,0:T(8,128)(2,1)} %bitcast.20, bf16[256,3072]{1,0:T(8,128)(2,1)} %bitcast.22), custom_call_target="tpu_custom_call" | custom-call | bytes 6291456 | tf_op jit(solution)/shard_map/pack_rest/pallas_call | solution.py:422
  8.2 0.0 copy-start.5
  8.3 14.4 %all_to_all.37.refs_1_ = bf16[4,3,256,128]{3,2,1,0:T(8,128)(2,1)} all-to-all(bf16[4,3,256,128]{3,2,1,0:T(8,128)(2,1)} %get-tuple-element.13), channel_id=1, replica_groups={{0,1,2,3},{4,5,6,7},{8,9,10,11},{12,13,14,15},{16,20,24,28},{17,21,25,2..., dimensions={0} | all-to-all | bytes 1572864 | tf_op jit(solution)/shard_map/all_to_all | solution.py:61
  22.7 0.0 copy-done.5
  22.7 15.3 %all_to_all.38.refs_0_.refs_4_ = bf16[4,2,3,256,128]{4,3,2,1,0:T(8,128)(2,1)S(1)} all-to-all(bf16[4,2,3,256,128]{4,3,2,1,0:T(8,128)(2,1)S(1)} %copy-done.5), channel_id=1, replica_groups={{0,1,2,3},{4,5,6,7},{8,9,10,11},{12,13,14,15},{16,20,24,28},{17,21,25,2..., dimensions={0} | all-to-all | bytes 3145728 | tf_op jit(solution)/shard_map/all_to_all | solution.py:61
  38.0 0.0 copy-start
  38.0 6.4 %all-to-all-start.3 = ((bf16[8,32,4608]{2,1,0:T(8,128)(2,1)}), bf16[8,32,4608]{2,1,0:T(8,128)(2,1)}, u32[]{:S(2)}, u32[]{:S(2)}) async-start(bf16[8,32,4608]{2,1,0:T(8,128)(2,1)} %bitcast.24), calls=%async_computation.3 | async-start | bytes 4718592 | tf_op jit(solution)/shard_map/all_to_all | solution.py:441
  44.4 0.0 copy-start.7
  44.4 0.3 collective-permute-start
  44.7 0.0 copy-done
  44.7 2.4 %collective-permute-start.2 = (bf16[4,2,3,256,128]{4,3,2,1,0:T(8,128)(2,1)S(1)}, bf16[4,2,3,256,128]{4,3,2,1,0:T(8,128)(2,1)}, u32[]{:S(2)}, u32[]{:S(2)}) collective-permute-start(bf16[4,2,3,256,128]{4,3,2,1,0:T(8,128)(2,1)S(1)} %all_to_all.38.refs_0_.refs_4_), channel_id=1, source_target_pairs={{0,12},{1,13},{2,14},{3,15},{4,0},{5,1},{6,2},{7,3},{8,4},{9,5},{1... | collective-permute-start | bytes 4718600 | tf_op jit(solution)/shard_map/ppermute | solution.py:65
  47.1 1.2 copy.11
  48.2 1.5 %copy.12 = s32[24,8,8]{1,2,0:T(8,128)} copy(s32[24,8,8]{0,2,1:T(8,128)} %param.12) | data formatting | bytes 12288 | tf_op args[5]
  49.7 0.1 fusion
  49.8 0.8 pad.8.bias_ref
  50.6 0.0 copy-done.7
  50.6 0.0 copy-done.6
  50.6 0.1 fusion.1
  50.7 0.6 pad.9.bias_ref
  51.4 0.6 pad_add_fusion.where
  52.0 6.6 %spatial_attention.3 = (bf16[3,1024,256]{2,1,0:T(8,128)(2,1)}, f32[3,136,1024]{2,1,0:T(8,128)}) custom-call(s32[24]{0:T(128)} %get-tuple-element.11.order, s32[3]{0:T(128)} %pad_add_fusion.where, f32[24,32,128]{2,1,0:T(8,128)} %pad.8.bias_ref, bf16[4,2,3,256,128]{4,3,2,1,0:T(8,128)(2,1)} %copy-done, bf16[4,3,256,128]{3,2,1,0:T(8,128)(2,1)} %all_to_all.37.refs_1_), custom_call_target="tpu_custom_call" | custom-call | flops 3221225472 | bytes 4194304 | tf_op jit(solution)/shard_map/spatial_attention/pallas_call | solution.py:326
  58.6 6.7 %collective-permute-done.refs_0_.refs_5_ = bf16[4,2,3,256,128]{4,3,2,1,0:T(8,128)(2,1)S(1)} collective-permute-done((bf16[4,2,3,256,128]{4,3,2,1,0:T(8,128)(2,1)S(1)}, bf16[4,2,3,256,128]{4,3,2,1,0:T(8,128)(2,1)S(1)}, u32[]{:S(2)}, u32[]{:S(2)}) %collective-permute-start) | collective-permute-done | bytes 1572896 | tf_op jit(solution)/shard_map/ppermute | solution.py:65
  65.3 0.0 copy-start.1
  65.3 1.1 slice.8
  66.3 0.0 collective-permute-start.1
  66.3 0.0 collective-permute-done.2.refs_1_.refs_6_
  66.3 2.1 %slice.9 = bf16[2,2,3,256,128]{4,3,2,1,0:T(8,128)(2,1)} slice(bf16[4,2,3,256,128]{4,3,2,1,0:T(8,128)(2,1)} %collective-permute-done.2.refs_1_.refs_6_), slice={[2:4], [0:2], [0:3], [0:256], [0:128]} | slice | bytes 1572864 | tf_op jit(solution)/shard_map/slice | solution.py:456
  68.4 0.0 copy-done.1
  68.4 2.7 %collective-permute-start.3 = (bf16[2,2,3,256,128]{4,3,2,1,0:T(8,128)(2,1)}, bf16[2,2,3,256,128]{4,3,2,1,0:T(8,128)(2,1)S(1)}, u32[]{:S(2)}, u32[]{:S(2)}) collective-permute-start(bf16[2,2,3,256,128]{4,3,2,1,0:T(8,128)(2,1)} %slice.9), channel_id=1, source_target_pairs={{0,12},{1,13},{2,14},{3,15},{4,0},{5,1},{6,2},{7,3},{8,4},{9,5},{1... | collective-permute-start | bytes 2359304 | tf_op jit(solution)/shard_map/ppermute | solution.py:65
  71.1 2.5 %all-to-all-done.3 = bf16[8,32,4608]{2,1,0:T(8,128)(2,1)} async-done(((bf16[8,32,4608]{2,1,0:T(8,128)(2,1)}), bf16[8,32,4608]{2,1,0:T(8,128)(2,1)}, u32[]{:S(2)}, u32[]{:S(2)}) %all-to-all-start.3) | async-done | bytes 2359328 | tf_op jit(solution)/shard_map/all_to_all | solution.py:441
  73.6 4.9 %temporal_attention.1 = bf16[256,1536]{1,0:T(8,128)(2,1)} custom-call(s32[24]{0:T(128)} %get-tuple-element.11.order, f32[24,8,128]{2,1,0:T(8,128)} %pad.9.bias_ref, bf16[256,4608]{1,0:T(8,128)(2,1)} %bitcast.9.q_ref.k_ref.v_ref, bf16[256,4608]{1,0:T(8,128)(2,1)} %bitcast.9.q_ref.k_ref.v_ref, bf16[256,4608]{1,0:T(8,128)(2,1)} %bitcast.9.q_ref.k_ref.v_ref), custom_call_target="tpu_custom_call" | custom-call | flops 3221225472 | bytes 4194304 | tf_op jit(solution)/shard_map/temporal_attention/pallas_call | solution.py:374
  78.6 4.4 %all-to-all-start.4 = ((bf16[8,32,1536]{2,1,0:T(8,128)(2,1)}), bf16[8,32,1536]{2,1,0:T(8,128)(2,1)S(1)}, u32[]{:S(2)}, u32[]{:S(2)}) async-start(bf16[8,32,1536]{2,1,0:T(8,128)(2,1)} %bitcast.26), calls=%async_computation.4 | async-start | bytes 1572864 | tf_op jit(solution)/shard_map/all_to_all | solution.py:465
  82.9 9.1 %spatial_attention.4.refs_3_ = f32[3,136,1024]{2,1,0:T(8,128)} custom-call(s32[24]{0:T(128)} %get-tuple-element.11.order, s32[3]{0:T(128)} %pad_add_fusion.where, f32[24,32,128]{2,1,0:T(8,128)} %pad.8.bias_ref, bf16[4,2,3,256,128]{4,3,2,1,0:T(8,128)(2,1)} %copy-done.1, bf16[4,2,3,256,128]{4,3,2,1,0:T(8,128)(2,1)} %collective-permute-done.2.refs_1_.refs_6_, ...), custom_call_target="tpu_custom_call" | custom-call | flops 6442450944 | bytes 4194304 | tf_op jit(solution)/shard_map/spatial_attention/pallas_call | solution.py:326
  92.0 0.0 collective-permute-done.1.refs_0_.refs_7_
  92.0 0.0 collective-permute-done.3.refs_1_.refs_8_
  92.0 0.0 copy-start.2
  92.0 0.9 copy-done.2
  92.9 6.8 %spatial_attention.5 = bf16[4,3,256,128]{3,2,1,0:T(8,128)(2,1)} custom-call(s32[24]{0:T(128)} %get-tuple-element.11.order, s32[3]{0:T(128)} %pad_add_fusion.where, f32[24,32,128]{2,1,0:T(8,128)} %pad.8.bias_ref, bf16[2,2,3,256,128]{4,3,2,1,0:T(8,128)(2,1)} %collective-permute-done.1.refs_0_.refs_7_, bf16[2,2,3,256,128]{4,3,2,1,0:T(8,128)(2,1)} %copy-done.2, ...), custom_call_target="tpu_custom_call" | custom-call | flops 3221225472 | bytes 4194304 | tf_op jit(solution)/shard_map/spatial_attention/pallas_call | solution.py:326
  99.8 0.0 all-to-all-done.4
  99.8 0.0 copy-start.3
  99.8 5.0 %all-to-all-start.2 = ((bf16[4,3,256,128]{3,2,1,0:T(8,128)(2,1)}), bf16[4,3,256,128]{3,2,1,0:T(8,128)(2,1)S(1)}, u32[]{:S(2)}, u32[]{:S(2)}) async-start(bf16[4,3,256,128]{3,2,1,0:T(8,128)(2,1)} %spatial_attention.5), calls=%async_computation.2 | async-start | bytes 1572864 | tf_op jit(solution)/shard_map/all_to_all | solution.py:61
  104.8 0.0 copy-done.3
  104.8 2.7 %place_temporal.1.base_ref = bf16[256,3072]{1,0:T(8,128)(2,1)} custom-call(s32[24]{0:T(128)} %kind.7, bf16[256,1536]{1,0:T(8,128)(2,1)} %bitcast.23), custom_call_target="tpu_custom_call" | custom-call | bytes 2097152 | tf_op jit(solution)/shard_map/place_temporal/pallas_call | solution.py:467
  107.4 5.7 %all-to-all-done.2.src_ref = bf16[4,3,256,128]{3,2,1,0:T(8,128)(2,1)S(1)} async-done(((bf16[4,3,256,128]{3,2,1,0:T(8,128)(2,1)}), bf16[4,3,256,128]{3,2,1,0:T(8,128)(2,1)S(1)}, u32[]{:S(2)}, u32[]{:S(2)}) %all-to-all-start.2) | async-done | bytes 786464 | tf_op jit(solution)/shard_map/all_to_all | solution.py:61
  113.1 0.0 copy-start.4
  113.1 0.9 copy-done.4
  114.0 2.7 %place_spatial.1 = bf16[256,3072]{1,0:T(8,128)(2,1)} custom-call(s32[24]{0:T(128)} %kind.7, bf16[4,3,256,128]{3,2,1,0:T(8,128)(2,1)} %copy-done.4, bf16[256,3072]{1,0:T(8,128)(2,1)} %place_temporal.1.base_ref), custom_call_target="tpu_custom_call", output_to_operand_aliasing={{}: (2, {})} | custom-call | bytes 2097152 | tf_op jit(solution)/shard_map/place_spatial/pallas_call | solution.py:478
  (4 shorter events, 0.0 us)
Async XLA Ops:
  8.2 14.5 %copy-start.5 = (bf16[4,2,3,256,128]{4,3,2,1,0:T(8,128)(2,1)S(1)}, bf16[4,2,3,256,128]{4,3,2,1,0:T(8,128)(2,1)}, u32[]{:S(2)}) copy-start(bf16[4,2,3,256,128]{4,3,2,1,0:T(8,128)(2,1)} %get-tuple-element.12) | copy-start | bytes 4718596
  38.0 6.7 %copy-start = (bf16[4,2,3,256,128]{4,3,2,1,0:T(8,128)(2,1)}, bf16[4,2,3,256,128]{4,3,2,1,0:T(8,128)(2,1)S(1)}, u32[]{:S(2)}) copy-start(bf16[4,2,3,256,128]{4,3,2,1,0:T(8,128)(2,1)S(1)} %all_to_all.38.refs_0_.refs_4_) | copy-start | bytes 4718596
  38.0 35.7 %all-to-all-start.3 = ((bf16[8,32,4608]{2,1,0:T(8,128)(2,1)}), bf16[8,32,4608]{2,1,0:T(8,128)(2,1)}, u32[]{:S(2)}, u32[]{:S(2)}) async-start(bf16[8,32,4608]{2,1,0:T(8,128)(2,1)} %bitcast.24), calls=%async_computation.3 | async-start | bytes 4718592 | tf_op jit(solution)/shard_map/all_to_all | solution.py:441
  44.4 6.2 %copy-start.7 = (s32[8]{0:T(128)S(1)}, s32[8]{0:T(128)}, u32[]{:S(2)}) copy-start(s32[8]{0:T(128)} %param.13) | copy-start | bytes 100
  44.4 20.9 %collective-permute-start = (bf16[4,2,3,256,128]{4,3,2,1,0:T(8,128)(2,1)S(1)}, bf16[4,2,3,256,128]{4,3,2,1,0:T(8,128)(2,1)S(1)}, u32[]{:S(2)}, u32[]{:S(2)}) collective-permute-start(bf16[4,2,3,256,128]{4,3,2,1,0:T(8,128)(2,1)S(1)} %all_to_all.38.refs_0_.refs_4_), channel_id=1, source_target_pairs={{0,4},{1,5},{2,6},{3,7},{4,8},{5,9},{6,10},{7,11},{8,12},{9,13},{1... | collective-permute-start | bytes 4718600 | tf_op jit(solution)/shard_map/ppermute | solution.py:65
  44.7 21.6 %collective-permute-start.2 = (bf16[4,2,3,256,128]{4,3,2,1,0:T(8,128)(2,1)S(1)}, bf16[4,2,3,256,128]{4,3,2,1,0:T(8,128)(2,1)}, u32[]{:S(2)}, u32[]{:S(2)}) collective-permute-start(bf16[4,2,3,256,128]{4,3,2,1,0:T(8,128)(2,1)S(1)} %all_to_all.38.refs_0_.refs_4_), channel_id=1, source_target_pairs={{0,12},{1,13},{2,14},{3,15},{4,0},{5,1},{6,2},{7,3},{8,4},{9,5},{1... | collective-permute-start | bytes 4718600 | tf_op jit(solution)/shard_map/ppermute | solution.py:65
  49.7 0.9 copy-start.6
  65.3 3.1 %copy-start.1 = (bf16[4,2,3,256,128]{4,3,2,1,0:T(8,128)(2,1)}, bf16[4,2,3,256,128]{4,3,2,1,0:T(8,128)(2,1)S(1)}, u32[]{:S(2)}) copy-start(bf16[4,2,3,256,128]{4,3,2,1,0:T(8,128)(2,1)S(1)} %collective-permute-done.refs_0_.refs_5_) | copy-start | bytes 4718596
  66.3 25.7 %collective-permute-start.1 = (bf16[2,2,3,256,128]{4,3,2,1,0:T(8,128)(2,1)}, bf16[2,2,3,256,128]{4,3,2,1,0:T(8,128)(2,1)}, u32[]{:S(2)}, u32[]{:S(2)}) collective-permute-start(bf16[2,2,3,256,128]{4,3,2,1,0:T(8,128)(2,1)} %slice.8), channel_id=1, source_target_pairs={{0,4},{1,5},{2,6},{3,7},{4,8},{5,9},{6,10},{7,11},{8,12},{9,13},{1... | collective-permute-start | bytes 2359304 | tf_op jit(solution)/shard_map/ppermute | solution.py:65
  68.4 23.6 %collective-permute-start.3 = (bf16[2,2,3,256,128]{4,3,2,1,0:T(8,128)(2,1)}, bf16[2,2,3,256,128]{4,3,2,1,0:T(8,128)(2,1)S(1)}, u32[]{:S(2)}, u32[]{:S(2)}) collective-permute-start(bf16[2,2,3,256,128]{4,3,2,1,0:T(8,128)(2,1)} %slice.9), channel_id=1, source_target_pairs={{0,12},{1,13},{2,14},{3,15},{4,0},{5,1},{6,2},{7,3},{8,4},{9,5},{1... | collective-permute-start | bytes 2359304 | tf_op jit(solution)/shard_map/ppermute | solution.py:65
  78.6 21.2 %all-to-all-start.4 = ((bf16[8,32,1536]{2,1,0:T(8,128)(2,1)}), bf16[8,32,1536]{2,1,0:T(8,128)(2,1)S(1)}, u32[]{:S(2)}, u32[]{:S(2)}) async-start(bf16[8,32,1536]{2,1,0:T(8,128)(2,1)} %bitcast.26), calls=%async_computation.4 | async-start | bytes 1572864 | tf_op jit(solution)/shard_map/all_to_all | solution.py:465
  92.0 0.9 copy-start.2
  99.8 5.0 %copy-start.3 = (bf16[8,32,1536]{2,1,0:T(8,128)(2,1)}, bf16[8,32,1536]{2,1,0:T(8,128)(2,1)S(1)}, u32[]{:S(2)}) copy-start(bf16[8,32,1536]{2,1,0:T(8,128)(2,1)S(1)} %all-to-all-done.4) | copy-start | bytes 2359300
  99.8 13.3 %all-to-all-start.2 = ((bf16[4,3,256,128]{3,2,1,0:T(8,128)(2,1)}), bf16[4,3,256,128]{3,2,1,0:T(8,128)(2,1)S(1)}, u32[]{:S(2)}, u32[]{:S(2)}) async-start(bf16[4,3,256,128]{3,2,1,0:T(8,128)(2,1)} %spatial_attention.5), calls=%async_computation.2 | async-start | bytes 1572864 | tf_op jit(solution)/shard_map/all_to_all | solution.py:61
  113.1 0.9 copy-start.4

commit v3 on v0

v3 whole, which is shorter than its diff:
```python
import functools

import jax
import jax.numpy as jnp
from jax import lax
from jax.experimental import pallas as pl
from jax.experimental.pallas import tpu as pltpu
from jax.sharding import PartitionSpec as P

HEADS = 24
TEMP_HEADS = 12
SPAT_HEADS = HEADS - TEMP_HEADS
BLK = 128
HEAD = 128
RING = 4
GROUP = SPAT_HEADS // RING
FRAMES = 8
BLOCKS = 32
ROWS = 256
TOKENS = RING * ROWS
HALVES = ROWS // BLK
PART = ROWS // FRAMES
TIME_STEP = 6
NEG = -1e30
LEVEL = BLOCKS
LARGE = 2.0**100
LOG2_SCALE = 1.4426950408889634 / HEAD**0.5
AXES = ("frame", "region")
BF16 = jnp.bfloat16
F32 = jnp.float32
ANY = pl.BlockSpec(memory_space=pl.ANY)
SMEM = pl.BlockSpec(memory_space=pltpu.SMEM)
VMEM = pl.BlockSpec(memory_space=pltpu.VMEM)
PARAMS = pltpu.CompilerParams(vmem_limit_bytes=63 * 1024 * 1024)
DMA = pltpu.SemaphoreType.DMA
DMAS = pltpu.SemaphoreType.DMA((RING,))


def flat(y, core, z, x):
    return ((y * 2 + core) * RING + z) * RING + x


def axis_groups(first):
    groups = []
    for y in range(RING):
        for core in range(2):
            along_x = (core == 0) == first
            for other in range(RING):
                groups.append([
                    flat(y, core, other, i) if along_x else flat(y, core, i, other)
                    for i in range(RING)
                ])
    return groups


def shift(tensor, step, first):
    pairs = []
    for group in axis_groups(first):
        for i in range(RING):
            pairs.append((group[i], group[(i + step) % RING]))
    return lax.ppermute(tensor, AXES, sorted(pairs))


def columns(index):
    return pl.ds(pl.multiple_of(index * HEAD, HEAD), HEAD)


def slot_of(own, rank):
    return lax.rem(rank // GROUP - own + RING, RING)


def pack_spatial(kind, q_ref, k_ref, v_ref, *refs):
    outs, (order, where, held, sem_in, sem_out) = refs[:RING], refs[RING:]
    core = lax.rem(lax.axis_index("frame"), 2)
    region = lax.axis_index("region")
    place_z, place_x = region // RING, lax.rem(region, RING)
    own = jnp.where(core == 0, place_x, place_z)
    where[0] = core
    where[1] = jnp.where(core == 0, place_z, place_x)
    where[2] = own
    spatial = jnp.int32(0)
    temporal = jnp.int32(0)
    for head in range(HEADS):
        one = kind[head]

        @pl.when(one == 0)
        def _(spatial=spatial, head=head):
            slot, place = slot_of(own, spatial), lax.rem(spatial, GROUP)
            for which, ref in enumerate((q_ref, k_ref, v_ref)):
                pltpu.make_async_copy(
                    ref.at[:, pl.ds(head * HEAD, HEAD)],
                    held.at[slot, which, place],
                    sem_in.at[slot],
                ).start()

        order[jnp.where(one == 1, SPAT_HEADS + temporal, spatial)] = head
        spatial += 1 - one
        temporal += one
    copies = []
    for slot in (1, 3, 2, 0):
        pltpu.make_async_copy(held.at[slot], held.at[slot], sem_in.at[slot]).wait()
        copies.append(pltpu.make_async_copy(held.at[slot], outs[slot], sem_out.at[slot]))
        copies[-1].start()
    for copy in copies:
        copy.wait()


def pack_temporal(order, q_ref, k_ref, v_ref, out_ref, held, sem_in, sem_out):
    wide = TEMP_HEADS * HEAD
    copies = []
    for which, ref in enumerate((q_ref, k_ref, v_ref)):
        for place in range(TEMP_HEADS):
            pltpu.make_async_copy(
                ref.at[:, columns(order[SPAT_HEADS + place])],
                held.at[:, pl.ds(which * wide + place * HEAD, HEAD)],
                sem_in.at[which],
            ).start()
    for which in range(3):
        part = held.at[:, pl.ds(which * wide, wide)]
        pltpu.make_async_copy(part, part, sem_in.at[which]).wait()
        copies.append(
            pltpu.make_async_copy(part, out_ref.at[:, pl.ds(which * wide, wide)], sem_out.at[which])
        )
        copies[-1].start()
    for copy in copies:
        copy.wait()


def join(*refs):
    k_out, v_out = refs[2 * RING:]
    for slot in range(RING):
        rows = pl.ds(slot * ROWS, ROWS)
        k_out[0, rows, :] = refs[2 * slot][0, 0]
        v_out[0, :, rows] = refs[2 * slot + 1][0, 0].T


def place_first(order, where, time_ref, own_ref, out_ref, held, sem_in, sem_out):
    own = pltpu.make_async_copy(own_ref, held, sem_in)
    own.start()
    for place in range(TEMP_HEADS):
        pltpu.make_async_copy(
            time_ref.at[:, pl.ds(place * HEAD, HEAD)],
            out_ref.at[:, columns(order[SPAT_HEADS + place])],
            sem_out.at[0],
        ).start()
    own.wait()
    place_group(order, where, 0, held, out_ref, sem_out.at[1])
    pltpu.make_async_copy(time_ref, time_ref, sem_out.at[0]).wait()
    pltpu.make_async_copy(held, held, sem_out.at[1]).wait()


def place_group(order, where, slot, held, out_ref, sem):
    group = lax.rem(where[2] + slot, RING)
    for place in range(GROUP):
        pltpu.make_async_copy(
            held.at[place], out_ref.at[:, columns(order[group * GROUP + place])], sem
        ).start()


def place_rest(order, where, *refs):
    count = RING - 1
    parts, (_, out_ref, held, sem_in, sem_out) = refs[:count], refs[count:]
    copies = [
        pltpu.make_async_copy(parts[i], held.at[i], sem_in.at[i]) for i in range(count)
    ]
    for copy in copies:
        copy.start()
    for i, copy in enumerate(copies):
        copy.wait()
        place_group(order, where, i + 1, held.at[i], out_ref, sem_out)
    pltpu.make_async_copy(held, held, sem_out).wait()


def first_block(where, slot, offset):
    place = lax.rem(where[2] - slot + RING, RING)
    ring = lax.rem(where[1] + offset, RING)
    return jnp.where(where[0] == 0, ring * RING + place, place * RING + ring) * HALVES


def mark_queries(where, mask_ref, q_refs, keys, marked_ref):
    lane = lax.broadcasted_iota(jnp.int32, (1, BLOCKS), 1)
    wide = lax.broadcasted_iota(jnp.int32, (BLK, HEAD), 1)
    for slot in range(RING):
        for half in range(HALVES):
            block = first_block(where, slot, 0) + half
            line = mask_ref[0, pl.ds(block, 1), :]
            line = jnp.where((line == 1) | (lane == block), 0.0, NEG)
            line = jnp.concatenate([line, jnp.zeros((1, HEAD - BLOCKS), F32)], axis=1)
            rows = pl.ds(slot * ROWS + half * BLK, BLK)
            query = q_refs[slot][0, 0, half * BLK:(half + 1) * BLK, :]
            level = jnp.sum(
                query.astype(F32) * keys[0, rows, :].astype(F32), axis=1, keepdims=True
            )
            mark = jnp.where(wide == LEVEL, -level, jnp.broadcast_to(line, (BLK, HEAD)))
            marked_ref[0, rows, :HEAD] = query
            marked_ref[0, rows, HEAD:] = mark.astype(BF16)


def mark_keys(where, offset, marks):
    lane = lax.broadcasted_iota(jnp.int32, (ROWS, HEAD), 1)
    half = lax.broadcasted_iota(jnp.int32, (ROWS, HEAD), 0) // BLK
    for slot in range(RING):
        block = first_block(where, slot, offset) + half
        mark = jnp.where((lane == block) | (lane == LEVEL), 1.0, 0.0)
        marks[slot * ROWS:(slot + 1) * ROWS, :] = mark.astype(BF16)


def attend_again(where, marked_ref, keys_all, vals_all, out_refs, marks, keys, vals, sem):
    head = pl.program_id(0)
    lane = lax.broadcasted_iota(jnp.int32, (TOKENS, 2 * HEAD), 1)
    query = marked_ref[0]
    query = jnp.where(lane == HEAD + LEVEL, jnp.zeros_like(query), query)
    offsets = (0, RING - 1, 1, 2)

    def step(turn, carry):
        top, sums, total = carry
        offset = jnp.int32(0)
        for i in range(RING):
            offset = jnp.where(turn == i, offsets[i], offset)

            @pl.when(turn == i)
            def _(i=i):
                copies = [
                    pltpu.make_async_copy(keys_all[i].at[head], keys, sem.at[0]),
                    pltpu.make_async_copy(vals_all[i].at[head], vals, sem.at[1]),
                ]
                for copy in copies:
                    copy.start()
                for copy in copies:
                    copy.wait()

        mark_keys(where, offset, marks)
        scores = lax.dot_general(
            jnp.concatenate([keys[...], marks[...]], axis=1),
            query,
            (((1,), (1,)), ((), ())),
            preferred_element_type=F32,
        )
        new = jnp.maximum(top, jnp.max(scores, axis=0, keepdims=True))
        weights = jnp.exp2((scores - new) * LOG2_SCALE).astype(BF16)
        decay = jnp.exp2((top - new) * LOG2_SCALE)
        sums = sums * decay + jnp.sum(weights.astype(F32), axis=0, keepdims=True)
        total = total * decay + jnp.dot(vals[...], weights, preferred_element_type=F32)
        return new, sums, total

    start = (
        jnp.full((1, TOKENS), -3e38, F32),
        jnp.zeros((1, TOKENS), F32),
        jnp.zeros((HEAD, TOKENS), F32),
    )
    _, sums, total = lax.fori_loop(0, RING, step, start)
    result = total / sums
    for slot in range(RING):
        out_refs[slot][0] = result[:, slot * ROWS:(slot + 1) * ROWS].T.astype(BF16)


def attend(offsets, order, where, *refs):
    count = len(offsets)
    first, last = offsets == (0,), offsets == (2,)
    key_refs, val_refs, refs = refs[:count], refs[count:2 * count], refs[2 * count:]
    if first:
        mask_ref, q_refs, refs = refs[0], refs[1:1 + RING], refs[1 + RING:]
        marked_ref, state_ref, marks = refs
        mark_queries(where, mask_ref, q_refs, key_refs[0], marked_ref)
        state = jnp.zeros((HEAD + 8, TOKENS), F32)
    else:
        marked_ref, before_ref, refs = refs[0], refs[1], refs[2:]
        state = before_ref[0]
        if last:
            keys_all, vals_all, refs = refs[:RING], refs[RING:2 * RING], refs[2 * RING:]
            out_refs, (marks, marks_more, keys, vals, sem) = refs[:RING], refs[RING:]
        else:
            state_ref, marks = refs

    @pl.when(pl.program_id(0) == 0)
    def _():
        for i, offset in enumerate(offsets):
            mark_keys(where, offset, marks.at[pl.ds(i * TOKENS, TOKENS)])

    ones = jnp.ones((8, TOKENS), BF16)
    for i in range(count):
        scores = lax.dot_general(
            jnp.concatenate([key_refs[i][0], marks[i * TOKENS:(i + 1) * TOKENS]], axis=1),
            marked_ref[0],
            (((1,), (1,)), ((), ())),
            preferred_element_type=F32,
        )
        weights = jnp.exp2(scores * LOG2_SCALE).astype(BF16)
        state += jnp.dot(
            jnp.concatenate([val_refs[i][0], ones], axis=0),
            weights,
            preferred_element_type=F32,
        )
    if not last:
        state_ref[0] = state
        return
    sums = state[HEAD:HEAD + 1]
    result = state[:HEAD] / sums
    for slot in range(RING):
        out_refs[slot][0] = result[:, slot * ROWS:(slot + 1) * ROWS].T.astype(BF16)
    fine = jnp.max(jnp.where(sums < LARGE, 0.0, 1.0)) == 0.0

    @pl.when(jnp.logical_not(fine))
    def _():
        attend_again(
            where, marked_ref, keys_all, vals_all, out_refs, marks_more, keys, vals, sem
        )


def attention(offsets, order, where, keys, vals, mask=None, queries=(), carried=(), every=()):
    def at(*block):
        zeros = (0,) * (len(block) - 1)
        return pl.BlockSpec(block, lambda h, o, w: (h,) + zeros)

    count = len(offsets)
    slot_spec = at(1, ROWS, HEAD)
    marked_spec, state_spec = at(1, TOKENS, 2 * HEAD), at(1, HEAD + 8, TOKENS)
    in_specs = [at(1, TOKENS, HEAD)] * count + [at(1, HEAD, TOKENS)] * count
    marked_shape = jax.ShapeDtypeStruct((GROUP, TOKENS, 2 * HEAD), BF16)
    state_shape = jax.ShapeDtypeStruct((GROUP, HEAD + 8, TOKENS), F32)
    scratch = [pltpu.VMEM((count * TOKENS, HEAD), BF16)]
    extra = []
    if queries:
        extra = [mask]
        in_specs += [
            pl.BlockSpec((1, BLOCKS, BLOCKS), lambda h, o, w: (o[w[2] * GROUP + h], 0, 0))
        ]
        in_specs += [
            pl.BlockSpec((1, 1, ROWS, HEAD), lambda h, o, w: (0, h, 0, 0))
        ] * RING
        out_specs, out_shape = [marked_spec, state_spec], [marked_shape, state_shape]
    else:
        in_specs += [marked_spec, state_spec]
        out_specs, out_shape = state_spec, state_shape
    if every:
        in_specs += [ANY] * len(every)
        out_specs = [slot_spec] * RING
        out_shape = [jax.ShapeDtypeStruct((GROUP, ROWS, HEAD), BF16)] * RING
        scratch += [pltpu.VMEM((TOKENS, HEAD), BF16)] * 2
        scratch += [pltpu.VMEM((HEAD, TOKENS), BF16), pltpu.SemaphoreType.DMA((2,))]
    flops = 8 * GROUP * TOKENS * count * TOKENS * HEAD
    return pl.pallas_call(
        functools.partial(attend, offsets),
        grid_spec=pltpu.PrefetchScalarGridSpec(
            num_scalar_prefetch=2,
            grid=(GROUP,),
            in_specs=in_specs,
            out_specs=out_specs,
            scratch_shapes=scratch,
        ),
        out_shape=out_shape,
        compiler_params=PARAMS,
        cost_estimate=pl.CostEstimate(flops=flops, bytes_accessed=4 << 20, transcendentals=0),
        name="spatial_attention",
    )(order, where, *keys, *vals, *extra, *queries, *carried, *every)


def attend_time(order, mask_ref, valid_ref, q_ref, k_ref, v_ref, out_ref):
    lane = lax.broadcasted_iota(jnp.int32, (ROWS, HEAD), 1)
    row = lax.broadcasted_iota(jnp.int32, (ROWS, HEAD), 0)
    frame, place = row // PART, row % PART
    here = lane == FRAMES + place
    inside = (lane >= FRAMES) & (lane < FRAMES + PART)
    key_mark = jnp.where(lane == frame, 1.0, jnp.where(inside & ~here, NEG, 0.0)).astype(BF16)
    ones = jnp.ones((ROWS, HEAD), BF16)
    short = lax.broadcasted_iota(jnp.int32, (FRAMES, FRAMES), 1)
    same = short == lax.broadcasted_iota(jnp.int32, (FRAMES, FRAMES), 0)
    every = range(TIME_STEP)
    at = [slice(slot * HEAD, (slot + 1) * HEAD) for slot in every]
    scores = []
    for slot in every:
        head = order[SPAT_HEADS + pl.program_id(0) * TIME_STEP + slot]
        seen = (mask_ref[head] == 1) & (valid_ref[...] == 1)
        pairs = jnp.where(seen | same, 0.0, NEG)
        pairs = jnp.concatenate([pairs, jnp.zeros((FRAMES, HEAD - FRAMES), F32)], axis=1)
        pairs = jnp.broadcast_to(pairs[:, None, :], (FRAMES, PART, HEAD)).reshape(ROWS, HEAD)
        mark = jnp.where(here, 1.0, pairs).astype(BF16)
        query = jnp.concatenate([q_ref[:, at[slot]], mark], axis=1)
        keys = jnp.concatenate([k_ref[:, at[slot]], key_mark], axis=1)
        scores.append(
            lax.dot_general(query, keys, (((1,), (1,)), ((), ())), preferred_element_type=F32)
        )
    tops = [jnp.max(scores[slot], axis=1, keepdims=True) for slot in every]
    weights = [
        jnp.exp2((scores[slot] - tops[slot]) * LOG2_SCALE).astype(BF16) for slot in every
    ]
    for slot in every:
        vals = jnp.concatenate([v_ref[:, at[slot]], ones], axis=1)
        both = jnp.dot(weights[slot], vals, preferred_element_type=F32)
        out_ref[:, at[slot]] = (both[:, :HEAD] / both[:, HEAD:]).astype(BF16)


def time_attention(order, mask, valid, gathered):
    steps = TEMP_HEADS // TIME_STEP

    def at(which):
        return pl.BlockSpec((ROWS, TIME_STEP * HEAD), lambda h, o: (0, which * steps + h))

    return pl.pallas_call(
        attend_time,
        grid_spec=pltpu.PrefetchScalarGridSpec(
            num_scalar_prefetch=1,
            grid=(steps,),
            in_specs=[
                pl.BlockSpec(mask.shape, lambda h, o: (0, 0, 0)),
                pl.BlockSpec(valid.shape, lambda h, o: (0, 0)),
            ]
            + [at(which) for which in range(3)],
            out_specs=at(0),
        ),
        out_shape=jax.ShapeDtypeStruct((ROWS, TEMP_HEADS * HEAD), BF16),
        compiler_params=PARAMS,
        cost_estimate=pl.CostEstimate(flops=3 << 30, bytes_accessed=4 << 20, transcendentals=0),
        name="temporal_attention",
    )(order, mask, valid, gathered, gathered, gathered)


def call(body, name, moved, in_specs, out_specs, out_shape, scratch, *args, **more):
    return pl.pallas_call(
        body,
        in_specs=in_specs,
        out_specs=out_specs,
        out_shape=out_shape,
        scratch_shapes=scratch,
        compiler_params=PARAMS,
        cost_estimate=pl.CostEstimate(flops=0, bytes_accessed=moved << 20, transcendentals=0),
        name=name,
        **more,
    )(*args)


def shards(queries, keys, values, head_kind, spatial_mask, temporal_mask, frame_valid):
    rows, width = queries.shape[1:]
    queries, keys, values = (t.reshape(rows, width) for t in (queries, keys, values))
    slot_shape = (GROUP, ROWS, HEAD)
    three_shape = (3,) + slot_shape
    wide_shape = (ROWS, 3 * TEMP_HEADS * HEAD)
    *threes, order, where = call(
        pack_spatial,
        "pack_spatial",
        5,
        [SMEM, ANY, ANY, ANY],
        [ANY] * RING + [SMEM] * 2,
        [jax.ShapeDtypeStruct(three_shape, BF16)] * RING
        + [jax.ShapeDtypeStruct((HEADS,), jnp.int32), jax.ShapeDtypeStruct((3,), jnp.int32)],
        [pltpu.VMEM((RING,) + three_shape, BF16), DMAS, DMAS],
        head_kind, queries, keys, values,
    )
    threes = [threes[0]] + [shift(threes[s], s, True) for s in range(1, RING)]
    packed = call(
        pack_temporal,
        "pack_temporal",
        5,
        [SMEM] + [ANY] * 3,
        ANY,
        jax.ShapeDtypeStruct(wide_shape, BF16),
        [pltpu.VMEM(wide_shape, BF16), DMAS, DMAS],
        order, queries, keys, values,
    )
    gathered = lax.all_to_all(packed, "frame", 0, 0, tiled=True)

    def head_block(*block):
        return pl.BlockSpec((1,) + block, lambda h: (h, 0, 0))

    own_keys, own_vals = pl.pallas_call(
        join,
        grid=(GROUP,),
        in_specs=[
            pl.BlockSpec((1, 1, ROWS, HEAD), lambda h, i=i: (i, h, 0, 0))
            for _ in range(RING)
            for i in (1, 2)
        ],
        out_specs=[head_block(TOKENS, HEAD), head_block(HEAD, TOKENS)],
        out_shape=[
            jax.ShapeDtypeStruct((GROUP, TOKENS, HEAD), BF16),
            jax.ShapeDtypeStruct((GROUP, HEAD, TOKENS), BF16),
        ],
        compiler_params=PARAMS,
        cost_estimate=pl.CostEstimate(flops=0, bytes_accessed=3 << 20, transcendentals=0),
        name="join",
    )(*[three for three in threes for _ in range(2)])
    left_keys = shift(own_keys, 1, False)
    right_vals = shift(own_vals, RING - 1, False)
    left_vals = shift(own_vals, 1, False)
    right_keys = shift(own_keys, RING - 1, False)
    carried = attention(
        (0,), order, where, [own_keys], [own_vals], mask=spatial_mask, queries=threes
    )
    far_keys = shift(left_keys, 1, False)
    far_vals = shift(right_vals, RING - 1, False)
    marked, state = carried
    state = attention(
        (RING - 1, 1), order, where, [left_keys, right_keys], [left_vals, right_vals],
        carried=(marked, state),
    )
    every = [own_keys, left_keys, right_keys, far_keys, own_vals, left_vals, right_vals, far_vals]
    parts = attention(
        (2,), order, where, [far_keys], [far_vals], carried=(marked, state), every=every
    )
    parts = [parts[0]] + [shift(parts[s], RING - s, True) for s in range(1, RING)]

    time_out = time_attention(order, temporal_mask, frame_valid[None], gathered)
    time_out = lax.all_to_all(time_out, "frame", 0, 0, tiled=True)
    out_shape = jax.ShapeDtypeStruct((rows, width), BF16)
    base = call(
        place_first,
        "place_first",
        3,
        [SMEM, SMEM, VMEM, ANY],
        ANY,
        out_shape,
        [pltpu.VMEM(slot_shape, BF16), DMA, DMAS],
        order, where, time_out, parts[0],
    )
    result = call(
        place_rest,
        "place_rest",
        1,
        [SMEM, SMEM] + [ANY] * RING,
        ANY,
        out_shape,
        [pltpu.VMEM((RING - 1,) + slot_shape, BF16), DMAS, DMA],
        order, where, *parts[1:], base,
        input_output_aliases={1 + RING: 0},
    )
    return result[None]


def solution(mesh):
    wide = P("frame", "region", None)
    return jax.shard_map(
        shards,
        mesh=mesh,
        in_specs=(wide, wide, wide, P(), P(), P(), P()),
        out_specs=wide,
        check_vma=False,
    )
```

time: 409 us -> 92.1 us (0.23)
  the two profiles are of different devices: /device:TPU:1 before, /device:TPU:8 now
where the time goes in v3:
time: 92.1 us; the launch traced here: 91.3 us
  Pallas kernels  43.7 us (47%)
  starting transfers between devices  31.7 us (34%)
  waiting for transfers between devices  13.5 us (15%)
  local copies, waits for them, and re-layouts  2.29 us (2%)
    pallas_call x3, Pallas kernels, attention(): pl.pallas_call(functools.partial(attend, offsets), grid_spec=pltpu.Prefet...  22.7 us
    ppermute x12, starting transfers between devices, shift(): return lax.ppermute(tensor, AXES, sorted(pairs))  21.8 us
    ppermute x12, waiting for transfers between devices, shift(): return lax.ppermute(tensor, AXES, sorted(pairs))  13.5 us
    pallas_call x4, Pallas kernels, call(): pl.pallas_call(body, in_specs=in_specs, out_specs=out_specs, out_shape=ou...  13.2 us
    all_to_all x1, starting transfers between devices, shards(): gathered = lax.all_to_all(packed, 'frame', 0, 0, tiled=True)  5.06 us
    all_to_all x1, starting transfers between devices, shards(): time_out = lax.all_to_all(time_out, 'frame', 0, 0, tiled=True)  4.8 us
    pallas_call x1, Pallas kernels, time_attention(): pl.pallas_call(attend_time, grid_spec=pltpu.PrefetchScalarGridSpec(num_sc...  4.32 us
    pallas_call x1, Pallas kernels, shards(): pl.pallas_call(join, grid=(GROUP,), in_specs=[pl.BlockSpec((1, 1, ROWS, H...  3.48 us
  transfers between devices with their start and end apart: 14, of which 4 were waited for; matrix products, arithmetic and copies ran while one was open for 1% of the time, Pallas kernels for 37%

profile of v3, /device:TPU:8, one launch (start us, length us, event | category | flops | bytes accessed | tf_op | source)
XLA Modules:
  0.0 91.3 jit_solution(16201962613056193362)
XLA Ops:
  0.0 4.3 %pack_spatial.1 = (bf16[3,3,256,128]{3,2,1,0:T(8,128)(2,1)}, bf16[3,3,256,128]{3,2,1,0:T(8,128)(2,1)}, bf16[3,3,256,128]{3,2,1,0:T(8,128)(2,1)}, bf16[3,3,256,12...) custom-call(s32[24]{0:T(128)} %kind.1, bf16[256,3072]{1,0:T(8,128)(2,1)} %bitcast.10, bf16[256,3072]{1,0:T(8,128)(2,1)} %bitcast.12, ...), custom_call_target="tpu_custom_call" | custom-call | bytes 5242880 | tf_op jit(solution)/shard_map/pack_spatial/pallas_call | solution.py:419
  4.3 3.4 %pack_temporal.1 = bf16[256,4608]{1,0:T(8,128)(2,1)} custom-call(s32[24]{0:T(128)} %get-tuple-element.19.order, bf16[256,3072]{1,0:T(8,128)(2,1)} %bitcast.11, bf16[256,3072]{1,0:T(8,128)(2,1)} %bitcast.13, bf16[256,3072]{1,0:T(8,128)(2,1)} %bitcast.15), custom_call_target="tpu_custom_call" | custom-call | bytes 5242880 | tf_op jit(solution)/shard_map/pack_temporal/pallas_call | solution.py:419
  7.6 0.0 copy-start.6
  7.6 0.0 copy-start.5
  7.7 0.0 copy-start.4
  7.7 5.1 %all-to-all-start = ((bf16[8,32,4608]{2,1,0:T(8,128)(2,1)}), bf16[8,32,4608]{2,1,0:T(8,128)(2,1)}, u32[]{:S(2)}, u32[]{:S(2)}) async-start(bf16[8,32,4608]{2,1,0:T(8,128)(2,1)} %bitcast.9), calls=%async_computation | async-start | bytes 4718592 | tf_op jit(solution)/shard_map/all_to_all | solution.py:460
  12.7 0.0 copy-done.6
  12.7 1.5 %collective-permute-start = (bf16[3,3,256,128]{3,2,1,0:T(8,128)(2,1)S(1)}, bf16[3,3,256,128]{3,2,1,0:T(8,128)(2,1)S(1)}, u32[]{:S(2)}, u32[]{:S(2)}) collective-permute-start(bf16[3,3,256,128]{3,2,1,0:T(8,128)(2,1)S(1)} %copy-done.6), channel_id=1, source_target_pairs={{0,1},{1,2},{2,3},{3,0},{4,5},{5,6},{6,7},{7,4},{8,9},{9,10},{10,1... | collective-permute-start | bytes 1769480 | tf_op jit(solution)/shard_map/ppermute | solution.py:61
  14.2 0.0 copy-done.5
  14.2 2.5 %collective-permute-start.1 = (bf16[3,3,256,128]{3,2,1,0:T(8,128)(2,1)S(1)}, bf16[3,3,256,128]{3,2,1,0:T(8,128)(2,1)}, u32[]{:S(2)}, u32[]{:S(2)}) collective-permute-start(bf16[3,3,256,128]{3,2,1,0:T(8,128)(2,1)S(1)} %copy-done.5), channel_id=1, source_target_pairs={{0,2},{1,3},{2,0},{3,1},{4,6},{5,7},{6,4},{7,5},{8,10},{9,11},{10,... | collective-permute-start | bytes 1769480 | tf_op jit(solution)/shard_map/ppermute | solution.py:61
  16.7 0.0 copy-done.4
  16.8 1.8 %collective-permute-start.2 = (bf16[3,3,256,128]{3,2,1,0:T(8,128)(2,1)S(1)}, bf16[3,3,256,128]{3,2,1,0:T(8,128)(2,1)}, u32[]{:S(2)}, u32[]{:S(2)}) collective-permute-start(bf16[3,3,256,128]{3,2,1,0:T(8,128)(2,1)S(1)} %copy-done.4), channel_id=1, source_target_pairs={{0,3},{1,0},{2,1},{3,2},{4,7},{5,4},{6,5},{7,6},{8,11},{9,8},{10,9... | collective-permute-start | bytes 1769480 | tf_op jit(solution)/shard_map/ppermute | solution.py:61
  18.6 5.2 %collective-permute-done.refs_2_.refs_3_.refs_4_ = bf16[3,3,256,128]{3,2,1,0:T(8,128)(2,1)S(1)} collective-permute-done((bf16[3,3,256,128]{3,2,1,0:T(8,128)(2,1)S(1)}, bf16[3,3,256,128]{3,2,1,0:T(8,128)(2,1)S(1)}, u32[]{:S(2)}, u32[]{:S(2)}) %collective-permute-start) | collective-permute-done | bytes 589856 | tf_op jit(solution)/shard_map/ppermute | solution.py:61
  23.8 7.2 %collective-permute-done.1.refs_4_.refs_5_ = bf16[3,3,256,128]{3,2,1,0:T(8,128)(2,1)} collective-permute-done((bf16[3,3,256,128]{3,2,1,0:T(8,128)(2,1)S(1)}, bf16[3,3,256,128]{3,2,1,0:T(8,128)(2,1)}, u32[]{:S(2)}, u32[]{:S(2)}) %collective-permute-start.1) | collective-permute-done | bytes 589856 | tf_op jit(solution)/shard_map/ppermute | solution.py:61
  31.0 0.1 collective-permute-done.2.refs_6_.refs_7_
  31.2 0.0 copy-done.1
  31.2 3.5 %join.1 = (bf16[3,1024,128]{2,1,0:T(8,128)(2,1)}, bf16[3,128,1024]{2,1,0:T(8,128)(2,1)}) custom-call(bf16[3,3,256,128]{3,2,1,0:T(8,128)(2,1)} %get-tuple-element.21.refs_0_.refs_1_.refs_3_, bf16[3,3,256,128]{3,2,1,0:T(8,128)(2,1)} %get-tuple-element.21.refs_0_.refs_1_.refs_3_, bf16[3,3,256,128]{3,2,1,0:T(8,128)(2,1)} %copy-done.1, ...), custom_call_target="tpu_custom_call" | custom-call | bytes 3145728 | tf_op jit(solution)/shard_map/join/pallas_call | solution.py:465
  34.6 1.9 %collective-permute-start.3 = (bf16[3,1024,128]{2,1,0:T(8,128)(2,1)}, bf16[3,1024,128]{2,1,0:T(8,128)(2,1)}, u32[]{:S(2)}, u32[]{:S(2)}) collective-permute-start(bf16[3,1024,128]{2,1,0:T(8,128)(2,1)} %get-tuple-element.25.refs_0_.refs_4_), channel_id=1, source_target_pairs={{0,4},{1,5},{2,6},{3,7},{4,8},{5,9},{6,10},{7,11},{8,12},{9,13},{1... | collective-permute-start | bytes 2359304 | tf_op jit(solution)/shard_map/ppermute | solution.py:61
  36.6 2.2 %collective-permute-start.5 = (bf16[3,128,1024]{2,1,0:T(8,128)(2,1)}, bf16[3,128,1024]{2,1,0:T(8,128)(2,1)}, u32[]{:S(2)}, u32[]{:S(2)}) collective-permute-start(bf16[3,128,1024]{2,1,0:T(8,128)(2,1)} %get-tuple-element.26.refs_1_.refs_8_), channel_id=1, source_target_pairs={{0,12},{1,13},{2,14},{3,15},{4,0},{5,1},{6,2},{7,3},{8,4},{9,5},{1... | collective-permute-start | bytes 2359304 | tf_op jit(solution)/shard_map/ppermute | solution.py:61
  38.8 1.9 %collective-permute-start.7 = (bf16[3,1024,128]{2,1,0:T(8,128)(2,1)}, bf16[3,1024,128]{2,1,0:T(8,128)(2,1)}, u32[]{:S(2)}, u32[]{:S(2)}) collective-permute-start(bf16[3,1024,128]{2,1,0:T(8,128)(2,1)} %get-tuple-element.25.refs_0_.refs_4_), channel_id=1, source_target_pairs={{0,12},{1,13},{2,14},{3,15},{4,0},{5,1},{6,2},{7,3},{8,4},{9,5},{1... | collective-permute-start | bytes 2359304 | tf_op jit(solution)/shard_map/ppermute | solution.py:61
  40.7 0.1 collective-permute-start.8
  40.8 0.0 copy-done.3
  40.8 0.7 copy.9.mask_ref
  41.5 6.6 %spatial_attention.3 = (bf16[3,1024,256]{2,1,0:T(8,128)(2,1)}, f32[3,136,1024]{2,1,0:T(8,128)}) custom-call(s32[24]{0:T(128)} %get-tuple-element.19.order, s32[3]{0:T(128)} %get-tuple-element.20.where, bf16[3,1024,128]{2,1,0:T(8,128)(2,1)} %get-tuple-element.25.refs_0_.refs_4_, bf16[3,128,1024]{2,1,0:T(8,128)(2,1)} %get-tuple-element.26.refs_1_.refs_8_, ...), custom_call_target="tpu_custom_call" | custom-call | flops 3221225472 | bytes 4194304 | tf_op jit(solution)/shard_map/spatial_attention/pallas_call | solution.py:342
  48.1 0.9 collective-permute-done.3.refs_0_.refs_5_
  49.0 0.0 collective-permute-start.4
  49.0 0.0 collective-permute-done.5.refs_3_.refs_10_
  49.0 3.3 %collective-permute-start.6 = (bf16[3,128,1024]{2,1,0:T(8,128)(2,1)}, bf16[3,128,1024]{2,1,0:T(8,128)(2,1)}, u32[]{:S(2)}, u32[]{:S(2)}) collective-permute-start(bf16[3,128,1024]{2,1,0:T(8,128)(2,1)} %collective-permute-done.5.refs_3_.refs_10_), channel_id=1, source_target_pairs={{0,12},{1,13},{2,14},{3,15},{4,0},{5,1},{6,2},{7,3},{8,4},{9,5},{1... | collective-permute-start | bytes 2359304 | tf_op jit(solution)/shard_map/ppermute | solution.py:61
  52.3 0.0 all-to-all-done
  52.3 4.3 %temporal_attention.1 = bf16[256,1536]{1,0:T(8,128)(2,1)} custom-call(s32[24]{0:T(128)} %get-tuple-element.19.order, s32[24,8,8]{2,1,0:T(8,128)} %copy.9.mask_ref, s32[1,8]{1,0:T(1,128)} %bitcast.18, bf16[256,4608]{1,0:T(8,128)(2,1)} %bitcast.5.q_ref.k_ref.v_ref, bf16[256,4608]{1,0:T(8,128)(2,1)} %bitcast.5.q_ref.k_ref.v_ref, ...), custom_call_target="tpu_custom_call" | custom-call | flops 3221225472 | bytes 4194304 | tf_op jit(solution)/shard_map/temporal_attention/pallas_call | solution.py:399
  56.6 4.8 %all-to-all-start.1 = ((bf16[8,32,1536]{2,1,0:T(8,128)(2,1)}), bf16[8,32,1536]{2,1,0:T(8,128)(2,1)S(1)}, u32[]{:S(2)}, u32[]{:S(2)}) async-start(bf16[8,32,1536]{2,1,0:T(8,128)(2,1)} %bitcast.17), calls=%async_computation.1 | async-start | bytes 1572864 | tf_op jit(solution)/shard_map/all_to_all | solution.py:503
  61.4 0.0 collective-permute-done.7.refs_1_.refs_6_
  61.4 0.0 collective-permute-done.8.refs_2_.refs_9_
  61.4 9.2 %spatial_attention.4.refs_3_ = f32[3,136,1024]{2,1,0:T(8,128)} custom-call(s32[24]{0:T(128)} %get-tuple-element.19.order, s32[3]{0:T(128)} %get-tuple-element.20.where, bf16[3,1024,128]{2,1,0:T(8,128)(2,1)} %collective-permute-done.3.refs_0_.refs_5_, bf16[3,1024,128]{2,1,0:T(8,128)(2,1)} %collective-permute-done.7.refs_1_.refs_6_, ...), custom_call_target="tpu_custom_call" | custom-call | flops 6442450944 | bytes 4194304 | tf_op jit(solution)/shard_map/spatial_attention/pallas_call | solution.py:342
  70.6 0.0 collective-permute-done.4.refs_0_.refs_7_
  70.6 0.0 collective-permute-done.6.refs_1_.refs_11_
  70.6 6.9 %spatial_attention.5 = (bf16[3,256,128]{2,1,0:T(8,128)(2,1)}, bf16[3,256,128]{2,1,0:T(8,128)(2,1)}, bf16[3,256,128]{2,1,0:T(8,128)(2,1)}, bf16[3,256,128]{2,1,0:T(8,128)(2,1)}) custom-call(s32[24]{0:T(128)} %get-tuple-element.19.order, s32[3]{0:T(128)} %get-tuple-element.20.where, bf16[3,1024,128]{2,1,0:T(8,128)(2,1)} %collective-permute-done.4.refs_0_.refs_7_, ...), custom_call_target="tpu_custom_call" | custom-call | flops 3221225472 | bytes 4194304 | tf_op jit(solution)/shard_map/spatial_attention/pallas_call | solution.py:342
  77.6 3.3 %collective-permute-start.10 = (bf16[3,256,128]{2,1,0:T(8,128)(2,1)}, bf16[3,256,128]{2,1,0:T(8,128)(2,1)S(1)}, u32[]{:S(2)}, u32[]{:S(2)}) collective-permute-start(bf16[3,256,128]{2,1,0:T(8,128)(2,1)} %get-tuple-element.30), channel_id=1, source_target_pairs={{0,2},{1,3},{2,0},{3,1},{4,6},{5,7},{6,4},{7,5},{8,10},{9,11},{10,... | collective-permute-start | bytes 589832 | tf_op jit(solution)/shard_map/ppermute | solution.py:61
  80.9 0.3 collective-permute-start.11
  81.2 3.0 %collective-permute-start.9 = (bf16[3,256,128]{2,1,0:T(8,128)(2,1)}, bf16[3,256,128]{2,1,0:T(8,128)(2,1)}, u32[]{:S(2)}, u32[]{:S(2)}) collective-permute-start(bf16[3,256,128]{2,1,0:T(8,128)(2,1)} %get-tuple-element.29), channel_id=1, source_target_pairs={{0,3},{1,0},{2,1},{3,2},{4,7},{5,4},{6,5},{7,6},{8,11},{9,8},{10,9... | collective-permute-start | bytes 589832 | tf_op jit(solution)/shard_map/ppermute | solution.py:61
  84.1 0.0 all-to-all-done.1
  84.1 0.9 copy-done
  85.0 3.0 %place_first.1.refs_3_ = bf16[256,3072]{1,0:T(8,128)(2,1)} custom-call(s32[24]{0:T(128)} %get-tuple-element.19.order, s32[3]{0:T(128)} %get-tuple-element.20.where, bf16[256,1536]{1,0:T(8,128)(2,1)} %bitcast.16, bf16[3,256,128]{2,1,0:T(8,128)(2,1)} %get-tuple-element.32.own_ref), custom_call_target="tpu_custom_call" | custom-call | bytes 3145728 | tf_op jit(solution)/shard_map/place_first/pallas_call | solution.py:419
  88.1 0.0 collective-permute-done.10.refs_1_
  88.1 0.0 collective-permute-done.11.refs_2_
  88.1 0.0 collective-permute-done.9.refs_0_
  88.1 0.7 copy-done.2
  88.8 2.5 %place_rest.1 = bf16[256,3072]{1,0:T(8,128)(2,1)} custom-call(s32[24]{0:T(128)} %get-tuple-element.19.order, s32[3]{0:T(128)} %get-tuple-element.20.where, bf16[3,256,128]{2,1,0:T(8,128)(2,1)} %collective-permute-done.9.refs_0_, bf16[3,256,128]{2,1,0:T(8,128)(2,1)} %copy-done.2, ...), custom_call_target="tpu_custom_call", output_to_operand_aliasing={{}: (5, {})} | custom-call | bytes 1048576 | tf_op jit(solution)/shard_map/place_rest/pallas_call | solution.py:419
  (4 shorter events, 0.0 us)
Async XLA Ops:
  7.6 5.1 %copy-start.6 = (bf16[3,3,256,128]{3,2,1,0:T(8,128)(2,1)S(1)}, bf16[3,3,256,128]{3,2,1,0:T(8,128)(2,1)}, u32[]{:S(2)}) copy-start(bf16[3,3,256,128]{3,2,1,0:T(8,128)(2,1)} %get-tuple-element.22) | copy-start | bytes 1769476
  7.6 6.6 %copy-start.5 = (bf16[3,3,256,128]{3,2,1,0:T(8,128)(2,1)S(1)}, bf16[3,3,256,128]{3,2,1,0:T(8,128)(2,1)}, u32[]{:S(2)}) copy-start(bf16[3,3,256,128]{3,2,1,0:T(8,128)(2,1)} %get-tuple-element.23) | copy-start | bytes 1769476
  7.7 9.1 %copy-start.4 = (bf16[3,3,256,128]{3,2,1,0:T(8,128)(2,1)S(1)}, bf16[3,3,256,128]{3,2,1,0:T(8,128)(2,1)}, u32[]{:S(2)}) copy-start(bf16[3,3,256,128]{3,2,1,0:T(8,128)(2,1)} %get-tuple-element.24) | copy-start | bytes 1769476
  7.7 44.6 %all-to-all-start = ((bf16[8,32,4608]{2,1,0:T(8,128)(2,1)}), bf16[8,32,4608]{2,1,0:T(8,128)(2,1)}, u32[]{:S(2)}, u32[]{:S(2)}) async-start(bf16[8,32,4608]{2,1,0:T(8,128)(2,1)} %bitcast.9), calls=%async_computation | async-start | bytes 4718592 | tf_op jit(solution)/shard_map/all_to_all | solution.py:460
  12.7 11.1 %collective-permute-start = (bf16[3,3,256,128]{3,2,1,0:T(8,128)(2,1)S(1)}, bf16[3,3,256,128]{3,2,1,0:T(8,128)(2,1)S(1)}, u32[]{:S(2)}, u32[]{:S(2)}) collective-permute-start(bf16[3,3,256,128]{3,2,1,0:T(8,128)(2,1)S(1)} %copy-done.6), channel_id=1, source_target_pairs={{0,1},{1,2},{2,3},{3,0},{4,5},{5,6},{6,7},{7,4},{8,9},{9,10},{10,1... | collective-permute-start | bytes 1769480 | tf_op jit(solution)/shard_map/ppermute | solution.py:61
  14.2 16.8 %collective-permute-start.1 = (bf16[3,3,256,128]{3,2,1,0:T(8,128)(2,1)S(1)}, bf16[3,3,256,128]{3,2,1,0:T(8,128)(2,1)}, u32[]{:S(2)}, u32[]{:S(2)}) collective-permute-start(bf16[3,3,256,128]{3,2,1,0:T(8,128)(2,1)S(1)} %copy-done.5), channel_id=1, source_target_pairs={{0,2},{1,3},{2,0},{3,1},{4,6},{5,7},{6,4},{7,5},{8,10},{9,11},{10,... | collective-permute-start | bytes 1769480 | tf_op jit(solution)/shard_map/ppermute | solution.py:61
  16.8 14.4 %collective-permute-start.2 = (bf16[3,3,256,128]{3,2,1,0:T(8,128)(2,1)S(1)}, bf16[3,3,256,128]{3,2,1,0:T(8,128)(2,1)}, u32[]{:S(2)}, u32[]{:S(2)}) collective-permute-start(bf16[3,3,256,128]{3,2,1,0:T(8,128)(2,1)S(1)} %copy-done.4), channel_id=1, source_target_pairs={{0,3},{1,0},{2,1},{3,2},{4,7},{5,4},{6,5},{7,6},{8,11},{9,8},{10,9... | collective-permute-start | bytes 1769480 | tf_op jit(solution)/shard_map/ppermute | solution.py:61
  23.8 7.3 %copy-start.1 = (bf16[3,3,256,128]{3,2,1,0:T(8,128)(2,1)}, bf16[3,3,256,128]{3,2,1,0:T(8,128)(2,1)S(1)}, u32[]{:S(2)}) copy-start(bf16[3,3,256,128]{3,2,1,0:T(8,128)(2,1)S(1)} %collective-permute-done.refs_2_.refs_3_.refs_4_) | copy-start | bytes 1769476
  31.2 9.6 %copy-start.3 = (s32[24,8,8]{0,2,1:T(8,128)S(1)}, s32[24,8,8]{0,2,1:T(8,128)}, u32[]{:S(2)}) copy-start(s32[24,8,8]{0,2,1:T(8,128)} %param.12) | copy-start | bytes 18436
  34.6 14.3 %collective-permute-start.3 = (bf16[3,1024,128]{2,1,0:T(8,128)(2,1)}, bf16[3,1024,128]{2,1,0:T(8,128)(2,1)}, u32[]{:S(2)}, u32[]{:S(2)}) collective-permute-start(bf16[3,1024,128]{2,1,0:T(8,128)(2,1)} %get-tuple-element.25.refs_0_.refs_4_), channel_id=1, source_target_pairs={{0,4},{1,5},{2,6},{3,7},{4,8},{5,9},{6,10},{7,11},{8,12},{9,13},{1... | collective-permute-start | bytes 2359304 | tf_op jit(solution)/shard_map/ppermute | solution.py:61
  36.6 12.4 %collective-permute-start.5 = (bf16[3,128,1024]{2,1,0:T(8,128)(2,1)}, bf16[3,128,1024]{2,1,0:T(8,128)(2,1)}, u32[]{:S(2)}, u32[]{:S(2)}) collective-permute-start(bf16[3,128,1024]{2,1,0:T(8,128)(2,1)} %get-tuple-element.26.refs_1_.refs_8_), channel_id=1, source_target_pairs={{0,12},{1,13},{2,14},{3,15},{4,0},{5,1},{6,2},{7,3},{8,4},{9,5},{1... | collective-permute-start | bytes 2359304 | tf_op jit(solution)/shard_map/ppermute | solution.py:61
  38.8 22.6 %collective-permute-start.7 = (bf16[3,1024,128]{2,1,0:T(8,128)(2,1)}, bf16[3,1024,128]{2,1,0:T(8,128)(2,1)}, u32[]{:S(2)}, u32[]{:S(2)}) collective-permute-start(bf16[3,1024,128]{2,1,0:T(8,128)(2,1)} %get-tuple-element.25.refs_0_.refs_4_), channel_id=1, source_target_pairs={{0,12},{1,13},{2,14},{3,15},{4,0},{5,1},{6,2},{7,3},{8,4},{9,5},{1... | collective-permute-start | bytes 2359304 | tf_op jit(solution)/shard_map/ppermute | solution.py:61
  40.7 20.7 %collective-permute-start.8 = (bf16[3,128,1024]{2,1,0:T(8,128)(2,1)}, bf16[3,128,1024]{2,1,0:T(8,128)(2,1)}, u32[]{:S(2)}, u32[]{:S(2)}) collective-permute-start(bf16[3,128,1024]{2,1,0:T(8,128)(2,1)} %get-tuple-element.26.refs_1_.refs_8_), channel_id=1, source_target_pairs={{0,4},{1,5},{2,6},{3,7},{4,8},{5,9},{6,10},{7,11},{8,12},{9,13},{1... | collective-permute-start | bytes 2359304 | tf_op jit(solution)/shard_map/ppermute | solution.py:61
  49.0 21.7 %collective-permute-start.4 = (bf16[3,1024,128]{2,1,0:T(8,128)(2,1)}, bf16[3,1024,128]{2,1,0:T(8,128)(2,1)}, u32[]{:S(2)}, u32[]{:S(2)}) collective-permute-start(bf16[3,1024,128]{2,1,0:T(8,128)(2,1)} %collective-permute-done.3.refs_0_.refs_5_), channel_id=1, source_target_pairs={{0,4},{1,5},{2,6},{3,7},{4,8},{5,9},{6,10},{7,11},{8,12},{9,13},{1... | collective-permute-start | bytes 2359304 | tf_op jit(solution)/shard_map/ppermute | solution.py:61
  49.0 21.7 %collective-permute-start.6 = (bf16[3,128,1024]{2,1,0:T(8,128)(2,1)}, bf16[3,128,1024]{2,1,0:T(8,128)(2,1)}, u32[]{:S(2)}, u32[]{:S(2)}) collective-permute-start(bf16[3,128,1024]{2,1,0:T(8,128)(2,1)} %collective-permute-done.5.refs_3_.refs_10_), channel_id=1, source_target_pairs={{0,12},{1,13},{2,14},{3,15},{4,0},{5,1},{6,2},{7,3},{8,4},{9,5},{1... | collective-permute-start | bytes 2359304 | tf_op jit(solution)/shard_map/ppermute | solution.py:61
  56.6 27.5 %all-to-all-start.1 = ((bf16[8,32,1536]{2,1,0:T(8,128)(2,1)}), bf16[8,32,1536]{2,1,0:T(8,128)(2,1)S(1)}, u32[]{:S(2)}, u32[]{:S(2)}) async-start(bf16[8,32,1536]{2,1,0:T(8,128)(2,1)} %bitcast.17), calls=%async_computation.1 | async-start | bytes 1572864 | tf_op jit(solution)/shard_map/all_to_all | solution.py:503
  77.6 10.5 %collective-permute-start.10 = (bf16[3,256,128]{2,1,0:T(8,128)(2,1)}, bf16[3,256,128]{2,1,0:T(8,128)(2,1)S(1)}, u32[]{:S(2)}, u32[]{:S(2)}) collective-permute-start(bf16[3,256,128]{2,1,0:T(8,128)(2,1)} %get-tuple-element.30), channel_id=1, source_target_pairs={{0,2},{1,3},{2,0},{3,1},{4,6},{5,7},{6,4},{7,5},{8,10},{9,11},{10,... | collective-permute-start | bytes 589832 | tf_op jit(solution)/shard_map/ppermute | solution.py:61
  80.9 7.2 %collective-permute-start.11 = (bf16[3,256,128]{2,1,0:T(8,128)(2,1)}, bf16[3,256,128]{2,1,0:T(8,128)(2,1)}, u32[]{:S(2)}, u32[]{:S(2)}) collective-permute-start(bf16[3,256,128]{2,1,0:T(8,128)(2,1)} %get-tuple-element.31), channel_id=1, source_target_pairs={{0,1},{1,2},{2,3},{3,0},{4,5},{5,6},{6,7},{7,4},{8,9},{9,10},{10,1... | collective-permute-start | bytes 589832 | tf_op jit(solution)/shard_map/ppermute | solution.py:61
  81.2 6.9 %collective-permute-start.9 = (bf16[3,256,128]{2,1,0:T(8,128)(2,1)}, bf16[3,256,128]{2,1,0:T(8,128)(2,1)}, u32[]{:S(2)}, u32[]{:S(2)}) collective-permute-start(bf16[3,256,128]{2,1,0:T(8,128)(2,1)} %get-tuple-element.29), channel_id=1, source_target_pairs={{0,3},{1,0},{2,1},{3,2},{4,7},{5,4},{6,5},{7,6},{8,11},{9,8},{10,9... | collective-permute-start | bytes 589832 | tf_op jit(solution)/shard_map/ppermute | solution.py:61
  84.1 0.9 copy-start
  88.1 0.7 copy-start.2

commit v4 on v3

--- a/solution.py
+++ b/solution.py
@@ -21,6 +21,9 @@
 HALVES = ROWS // BLK
 PART = ROWS // FRAMES
 TIME_STEP = 6
+HALF = TOKENS // 2
+H0 = 2
+H1 = 3
 NEG = -1e30
 LEVEL = BLOCKS
 LARGE = 2.0**100
@@ -28,7 +31,7 @@
 AXES = ("frame", "region")
 BF16 = jnp.bfloat16
 F32 = jnp.float32
-ANY = pl.BlockSpec(memory_space=pl.ANY)
+HBM = pl.BlockSpec(memory_space=pltpu.HBM)
 SMEM = pl.BlockSpec(memory_space=pltpu.SMEM)
 VMEM = pl.BlockSpec(memory_space=pltpu.VMEM)
 PARAMS = pltpu.CompilerParams(vmem_limit_bytes=63 * 1024 * 1024)
@@ -127,26 +130,30 @@
 
 
 def join(*refs):
-    k_out, v_out = refs[2 * RING:]
+    threes, outs = refs[:RING], refs[RING:RING + 2]
+    held, v_held, sem_k, sem_v, sem_out = refs[RING + 2:]
+    copies = []
     for slot in range(RING):
-        rows = pl.ds(slot * ROWS, ROWS)
-        k_out[0, rows, :] = refs[2 * slot][0, 0]
-        v_out[0, :, rows] = refs[2 * slot + 1][0, 0].T
-
-
-def place_first(order, where, time_ref, own_ref, out_ref, held, sem_in, sem_out):
-    own = pltpu.make_async_copy(own_ref, held, sem_in)
-    own.start()
-    for place in range(TEMP_HEADS):
-        pltpu.make_async_copy(
-            time_ref.at[:, pl.ds(place * HEAD, HEAD)],
-            out_ref.at[:, columns(order[SPAT_HEADS + place])],
-            sem_out.at[0],
-        ).start()
-    own.wait()
-    place_group(order, where, 0, held, out_ref, sem_out.at[1])
-    pltpu.make_async_copy(time_ref, time_ref, sem_out.at[0]).wait()
-    pltpu.make_async_copy(held, held, sem_out.at[1]).wait()
+        half, rows = slot // 2, pl.ds(slot % 2 * ROWS, ROWS)
+        copies.append((
+            pltpu.make_async_copy(threes[slot].at[2], v_held.at[slot], sem_v.at[slot]),
+            pltpu.make_async_copy(threes[slot].at[1], held.at[half, :, 0, rows, :], sem_k.at[slot]),
+        ))
+        copies[-1][0].start()
+        copies[-1][1].start()
+    sent = []
+    for half in range(2):
+        for slot in (2 * half, 2 * half + 1):
+            copies[slot][0].wait()
+            for head in range(GROUP):
+                for block in range(0, ROWS, BLK):
+                    rows = pl.ds(slot % 2 * ROWS + block, BLK)
+                    held[half, head, 1, rows, :] = v_held[slot, head, block:block + BLK, :].T
+            copies[slot][1].wait()
+        sent.append(pltpu.make_async_copy(held.at[half], outs[half], sem_out.at[half]))
+        sent[-1].start()
+    for copy in sent:
+        copy.wait()
 
 
 def place_group(order, where, slot, held, out_ref, sem):
@@ -157,17 +164,24 @@
         ).start()
 
 
-def place_rest(order, where, *refs):
-    count = RING - 1
-    parts, (_, out_ref, held, sem_in, sem_out) = refs[:count], refs[count:]
-    copies = [
-        pltpu.make_async_copy(parts[i], held.at[i], sem_in.at[i]) for i in range(count)
-    ]
+def place(order, where, time_ref, *refs):
+    parts, (out_ref, time_held, held, sem_time, sem_in, sem_out) = refs[:RING], refs[RING:]
+    time = pltpu.make_async_copy(time_ref, time_held, sem_time.at[0])
+    copies = [pltpu.make_async_copy(parts[i], held.at[i], sem_in.at[i]) for i in range(RING)]
+    time.start()
     for copy in copies:
         copy.start()
-    for i, copy in enumerate(copies):
+    time.wait()
+    for place in range(TEMP_HEADS):
+        pltpu.make_async_copy(
+            time_held.at[:, pl.ds(place * HEAD, HEAD)],
+            out_ref.at[:, columns(order[SPAT_HEADS + place])],
+            sem_time.at[1],
+        ).start()
+    for slot, copy in enumerate(copies):
         copy.wait()
-        place_group(order, where, i + 1, held.at[i], out_ref, sem_out)
+        place_group(order, where, slot, held.at[slot], out_ref, sem_out)
+    pltpu.make_async_copy(time_held, time_held, sem_time.at[1]).wait()
     pltpu.make_async_copy(held, held, sem_out).wait()
 
 
@@ -177,7 +191,7 @@
     return jnp.where(where[0] == 0, ring * RING + place, place * RING + ring) * HALVES
 
 
-def mark_queries(where, mask_ref, q_refs, keys, marked_ref):
+def mark_queries(where, mask_ref, q_refs, kv_refs, marked_ref):
     lane = lax.broadcasted_iota(jnp.int32, (1, BLOCKS), 1)
     wide = lax.broadcasted_iota(jnp.int32, (BLK, HEAD), 1)
     for slot in range(RING):
@@ -188,50 +202,52 @@
             line = jnp.concatenate([line, jnp.zeros((1, HEAD - BLOCKS), F32)], axis=1)
             rows = pl.ds(slot * ROWS + half * BLK, BLK)
             query = q_refs[slot][0, 0, half * BLK:(half + 1) * BLK, :]
+            key = kv_refs[slot // 2][0, 0, pl.ds(slot % 2 * ROWS + half * BLK, BLK), :]
             level = jnp.sum(
-                query.astype(F32) * keys[0, rows, :].astype(F32), axis=1, keepdims=True
+                query.astype(F32) * key.astype(F32), axis=1, keepdims=True
             )
             mark = jnp.where(wide == LEVEL, -level, jnp.broadcast_to(line, (BLK, HEAD)))
             marked_ref[0, rows, :HEAD] = query
             marked_ref[0, rows, HEAD:] = mark.astype(BF16)
 
 
-def mark_keys(where, offset, marks):
+def mark_keys(where, offset, half, marks):
     lane = lax.broadcasted_iota(jnp.int32, (ROWS, HEAD), 1)
-    half = lax.broadcasted_iota(jnp.int32, (ROWS, HEAD), 0) // BLK
-    for slot in range(RING):
-        block = first_block(where, slot, offset) + half
+    line = lax.broadcasted_iota(jnp.int32, (ROWS, HEAD), 0) // BLK
+    for i in range(2):
+        block = first_block(where, 2 * half + i, offset) + line
         mark = jnp.where((lane == block) | (lane == LEVEL), 1.0, 0.0)
-        marks[slot * ROWS:(slot + 1) * ROWS, :] = mark.astype(BF16)
-
-
-def attend_again(where, marked_ref, keys_all, vals_all, out_refs, marks, keys, vals, sem):
+        marks[i * ROWS:(i + 1) * ROWS, :] = mark.astype(BF16)
+
+
+def turned(kv_ref, *lead):
+    return jnp.concatenate(
+        [kv_ref[(*lead, 1, pl.ds(block, BLK))] for block in range(0, HALF, BLK)], axis=1
+    )
+
+
+def attend_again(where, marked_ref, chunks, kv_all, out_refs, marks, kv, sem):
     head = pl.program_id(0)
     lane = lax.broadcasted_iota(jnp.int32, (TOKENS, 2 * HEAD), 1)
     query = marked_ref[0]
     query = jnp.where(lane == HEAD + LEVEL, jnp.zeros_like(query), query)
-    offsets = (0, RING - 1, 1, 2)
 
     def step(turn, carry):
         top, sums, total = carry
-        offset = jnp.int32(0)
-        for i in range(RING):
-            offset = jnp.where(turn == i, offsets[i], offset)
+        offset, half = jnp.int32(0), jnp.int32(0)
+        for i, (one, other) in enumerate(chunks):
+            offset = jnp.where(turn == i, one, offset)
+            half = jnp.where(turn == i, other, half)
 
             @pl.when(turn == i)
             def _(i=i):
-                copies = [
-                    pltpu.make_async_copy(keys_all[i].at[head], keys, sem.at[0]),
-                    pltpu.make_async_copy(vals_all[i].at[head], vals, sem.at[1]),
-                ]
-                for copy in copies:
-                    copy.start()
-                for copy in copies:
-                    copy.wait()
-
-        mark_keys(where, offset, marks)
+                copy = pltpu.make_async_copy(kv_all[i].at[head], kv, sem)
+                copy.start()
+                copy.wait()
+
+        mark_keys(where, offset, half, marks)
         scores = lax.dot_general(
-            jnp.concatenate([keys[...], marks[...]], axis=1),
+            jnp.concatenate([kv[0], marks[...]], axis=1),
             query,
             (((1,), (1,)), ((), ())),
             preferred_element_type=F32,
@@ -240,7 +256,7 @@
         weights = jnp.exp2((scores - new) * LOG2_SCALE).astype(BF16)
         decay = jnp.exp2((top - new) * LOG2_SCALE)
         sums = sums * decay + jnp.sum(weights.astype(F32), axis=0, keepdims=True)
-        total = total * decay + jnp.dot(vals[...], weights, preferred_element_type=F32)
+        total = total * decay + jnp.dot(turned(kv), weights, preferred_element_type=F32)
         return new, sums, total
 
     start = (
@@ -248,48 +264,49 @@
         jnp.zeros((1, TOKENS), F32),
         jnp.zeros((HEAD, TOKENS), F32),
     )
-    _, sums, total = lax.fori_loop(0, RING, step, start)
+    _, sums, total = lax.fori_loop(0, len(chunks), step, start)
     result = total / sums
     for slot in range(RING):
         out_refs[slot][0] = result[:, slot * ROWS:(slot + 1) * ROWS].T.astype(BF16)
 
 
-def attend(offsets, order, where, *refs):
-    count = len(offsets)
-    first, last = offsets == (0,), offsets == (2,)
-    key_refs, val_refs, refs = refs[:count], refs[count:2 * count], refs[2 * count:]
+def attend(chunks, everything, order, where, *refs):
+    count = len(chunks)
+    first, last = chunks[0][0] == 0, everything is not None
+    kv_refs, refs = refs[:count], refs[count:]
     if first:
         mask_ref, q_refs, refs = refs[0], refs[1:1 + RING], refs[1 + RING:]
         marked_ref, state_ref, marks = refs
-        mark_queries(where, mask_ref, q_refs, key_refs[0], marked_ref)
+        mark_queries(where, mask_ref, q_refs, kv_refs, marked_ref)
         state = jnp.zeros((HEAD + 8, TOKENS), F32)
     else:
         marked_ref, before_ref, refs = refs[0], refs[1], refs[2:]
         state = before_ref[0]
         if last:
-            keys_all, vals_all, refs = refs[:RING], refs[RING:2 * RING], refs[2 * RING:]
-            out_refs, (marks, marks_more, keys, vals, sem) = refs[:RING], refs[RING:]
+            kv_all, refs = refs[:len(everything)], refs[len(everything):]
+            out_refs, (marks, marks_more, kv, sem) = refs[:RING], refs[RING:]
         else:
             state_ref, marks = refs
 
     @pl.when(pl.program_id(0) == 0)
     def _():
-        for i, offset in enumerate(offsets):
-            mark_keys(where, offset, marks.at[pl.ds(i * TOKENS, TOKENS)])
+        for i, (offset, half) in enumerate(chunks):
+            mark_keys(where, offset, half, marks.at[pl.ds(i * HALF, HALF)])
 
     ones = jnp.ones((8, TOKENS), BF16)
-    for i in range(count):
+    for i in range(0, count, 2):
+        pair = kv_refs[i:i + 2]
+        keys = jnp.concatenate([kv_ref[0, 0] for kv_ref in pair], axis=0)
+        vals = jnp.concatenate([turned(kv_ref, 0) for kv_ref in pair], axis=1)
         scores = lax.dot_general(
-            jnp.concatenate([key_refs[i][0], marks[i * TOKENS:(i + 1) * TOKENS]], axis=1),
+            jnp.concatenate([keys, marks[i * HALF:(i + 2) * HALF]], axis=1),
             marked_ref[0],
             (((1,), (1,)), ((), ())),
             preferred_element_type=F32,
         )
         weights = jnp.exp2(scores * LOG2_SCALE).astype(BF16)
         state += jnp.dot(
-            jnp.concatenate([val_refs[i][0], ones], axis=0),
-            weights,
-            preferred_element_type=F32,
+            jnp.concatenate([vals, ones], axis=0), weights, preferred_element_type=F32
         )
     if not last:
         state_ref[0] = state
@@ -302,23 +319,21 @@
 
     @pl.when(jnp.logical_not(fine))
     def _():
-        attend_again(
-            where, marked_ref, keys_all, vals_all, out_refs, marks_more, keys, vals, sem
-        )
-
-
-def attention(offsets, order, where, keys, vals, mask=None, queries=(), carried=(), every=()):
+        attend_again(where, marked_ref, everything, kv_all, out_refs, marks_more, kv, sem)
+
+
+def attention(held, chunks, order, where, mask=None, queries=(), carried=(), everything=None):
     def at(*block):
         zeros = (0,) * (len(block) - 1)
         return pl.BlockSpec(block, lambda h, o, w: (h,) + zeros)
 
-    count = len(offsets)
+    count = len(chunks)
     slot_spec = at(1, ROWS, HEAD)
     marked_spec, state_spec = at(1, TOKENS, 2 * HEAD), at(1, HEAD + 8, TOKENS)
-    in_specs = [at(1, TOKENS, HEAD)] * count + [at(1, HEAD, TOKENS)] * count
+    in_specs = [at(1, 2, HALF, HEAD)] * count
     marked_shape = jax.ShapeDtypeStruct((GROUP, TOKENS, 2 * HEAD), BF16)
     state_shape = jax.ShapeDtypeStruct((GROUP, HEAD + 8, TOKENS), F32)
-    scratch = [pltpu.VMEM((count * TOKENS, HEAD), BF16)]
+    scratch = [pltpu.VMEM((count * HALF, HEAD), BF16)]
     extra = []
     if queries:
         extra = [mask]
@@ -332,15 +347,16 @@
     else:
         in_specs += [marked_spec, state_spec]
         out_specs, out_shape = state_spec, state_shape
-    if every:
-        in_specs += [ANY] * len(every)
+    every = []
+    if everything is not None:
+        every = [held[chunk] for chunk in everything]
+        in_specs += [HBM] * len(every)
         out_specs = [slot_spec] * RING
         out_shape = [jax.ShapeDtypeStruct((GROUP, ROWS, HEAD), BF16)] * RING
-        scratch += [pltpu.VMEM((TOKENS, HEAD), BF16)] * 2
-        scratch += [pltpu.VMEM((HEAD, TOKENS), BF16), pltpu.SemaphoreType.DMA((2,))]
-    flops = 8 * GROUP * TOKENS * count * TOKENS * HEAD
+        scratch += [pltpu.VMEM((HALF, HEAD), BF16), pltpu.VMEM((2, HALF, HEAD), BF16), DMA]
+    flops = (H0 if queries else H1 if everything is None else 1) * 8 * GROUP * TOKENS * count * HALF * HEAD
     return pl.pallas_call(
-        functools.partial(attend, offsets),
+        functools.partial(attend, chunks, everything),
         grid_spec=pltpu.PrefetchScalarGridSpec(
             num_scalar_prefetch=2,
             grid=(GROUP,),
@@ -352,7 +368,7 @@
         compiler_params=PARAMS,
         cost_estimate=pl.CostEstimate(flops=flops, bytes_accessed=4 << 20, transcendentals=0),
         name="spatial_attention",
-    )(order, where, *keys, *vals, *extra, *queries, *carried, *every)
+    )(order, where, *[held[chunk] for chunk in chunks], *extra, *queries, *carried, *every)
 
 
 def attend_time(order, mask_ref, valid_ref, q_ref, k_ref, v_ref, out_ref):
@@ -365,12 +381,14 @@
     ones = jnp.ones((ROWS, HEAD), BF16)
     short = lax.broadcasted_iota(jnp.int32, (FRAMES, FRAMES), 1)
     same = short == lax.broadcasted_iota(jnp.int32, (FRAMES, FRAMES), 0)
+    which = lax.broadcasted_iota(jnp.int32, mask_ref.shape, 2)
     every = range(TIME_STEP)
     at = [slice(slot * HEAD, (slot + 1) * HEAD) for slot in every]
     scores = []
     for slot in every:
         head = order[SPAT_HEADS + pl.program_id(0) * TIME_STEP + slot]
-        seen = (mask_ref[head] == 1) & (valid_ref[...] == 1)
+        seen = jnp.sum(jnp.where(which == head, mask_ref[...], 0), axis=2)
+        seen = (seen == 1) & (valid_ref[...] == 1)
         pairs = jnp.where(seen | same, 0.0, NEG)
         pairs = jnp.concatenate([pairs, jnp.zeros((FRAMES, HEAD - FRAMES), F32)], axis=1)
         pairs = jnp.broadcast_to(pairs[:, None, :], (FRAMES, PART, HEAD)).reshape(ROWS, HEAD)
@@ -439,8 +457,8 @@
         pack_spatial,
         "pack_spatial",
         5,
-        [SMEM, ANY, ANY, ANY],
-        [ANY] * RING + [SMEM] * 2,
+        [SMEM, HBM, HBM, HBM],
+        [HBM] * RING + [SMEM] * 2,
         [jax.ShapeDtypeStruct(three_shape, BF16)] * RING
         + [jax.ShapeDtypeStruct((HEADS,), jnp.int32), jax.ShapeDtypeStruct((3,), jnp.int32)],
         [pltpu.VMEM((RING,) + three_shape, BF16), DMAS, DMAS],
@@ -450,78 +468,72 @@
     packed = call(
         pack_temporal,
         "pack_temporal",
-        5,
-        [SMEM] + [ANY] * 3,
-        ANY,
+        40,
+        [SMEM] + [HBM] * 3,
+        HBM,
         jax.ShapeDtypeStruct(wide_shape, BF16),
         [pltpu.VMEM(wide_shape, BF16), DMAS, DMAS],
         order, queries, keys, values,
     )
     gathered = lax.all_to_all(packed, "frame", 0, 0, tiled=True)
 
-    def head_block(*block):
-        return pl.BlockSpec((1,) + block, lambda h: (h, 0, 0))
-
-    own_keys, own_vals = pl.pallas_call(
+    half_shape = (GROUP, 2, HALF, HEAD)
+    held = {}
+    held[0, 0], held[0, 1] = call(
         join,
-        grid=(GROUP,),
-        in_specs=[
-            pl.BlockSpec((1, 1, ROWS, HEAD), lambda h, i=i: (i, h, 0, 0))
-            for _ in range(RING)
-            for i in (1, 2)
+        "join",
+        3,
+        [HBM] * RING,
+        [HBM] * 2,
+        [jax.ShapeDtypeStruct(half_shape, BF16)] * 2,
+        [
+            pltpu.VMEM((2,) + half_shape, BF16),
+            pltpu.VMEM((RING,) + slot_shape, BF16),
+            DMAS,
+            DMAS,
+            DMAS,
         ],
-        out_specs=[head_block(TOKENS, HEAD), head_block(HEAD, TOKENS)],
-        out_shape=[
-            jax.ShapeDtypeStruct((GROUP, TOKENS, HEAD), BF16),
-            jax.ShapeDtypeStruct((GROUP, HEAD, TOKENS), BF16),
-        ],
-        compiler_params=PARAMS,
-        cost_estimate=pl.CostEstimate(flops=0, bytes_accessed=3 << 20, transcendentals=0),
-        name="join",
-    )(*[three for three in threes for _ in range(2)])
-    left_keys = shift(own_keys, 1, False)
-    right_vals = shift(own_vals, RING - 1, False)
-    left_vals = shift(own_vals, 1, False)
-    right_keys = shift(own_keys, RING - 1, False)
-    carried = attention(
-        (0,), order, where, [own_keys], [own_vals], mask=spatial_mask, queries=threes
-    )
-    far_keys = shift(left_keys, 1, False)
-    far_vals = shift(right_vals, RING - 1, False)
-    marked, state = carried
-    state = attention(
-        (RING - 1, 1), order, where, [left_keys, right_keys], [left_vals, right_vals],
+        *threes,
+    )
+    left, right, far = RING - 1, 1, 2
+    held[left, 0] = shift(held[0, 0], 1, False)
+    held[right, 1] = shift(held[0, 1], RING - 1, False)
+    held[left, 1] = shift(held[0, 1], 1, False)
+    held[right, 0] = shift(held[0, 0], RING - 1, False)
+    marked, state = attention(
+        held, [(0, 0), (0, 1)], order, where, mask=spatial_mask, queries=threes
+    )
+    held[far, 0] = shift(held[left, 0], 1, False)
+    held[far, 1] = shift(held[right, 1], RING - 1, False)
+    state = attention(held, [(left, 0), (right, 1)], order, where, carried=(marked, state))
+    parts = attention(
+        held,
+        [(left, 1), (right, 0), (far, 0), (far, 1)],
+        order,
+        where,
         carried=(marked, state),
-    )
-    every = [own_keys, left_keys, right_keys, far_keys, own_vals, left_vals, right_vals, far_vals]
-    parts = attention(
-        (2,), order, where, [far_keys], [far_vals], carried=(marked, state), every=every
+        everything=[(offset, half) for offset in (0, left, right, far) for half in range(2)],
     )
     parts = [parts[0]] + [shift(parts[s], RING - s, True) for s in range(1, RING)]
 
-    time_out = time_attention(order, temporal_mask, frame_valid[None], gathered)
+    time_out = time_attention(order, jnp.transpose(temporal_mask, (1, 2, 0)), frame_valid[None], gathered)
     time_out = lax.all_to_all(time_out, "frame", 0, 0, tiled=True)
     out_shape = jax.ShapeDtypeStruct((rows, width), BF16)
-    base = call(
-        place_first,
-        "place_first",
-        3,
-        [SMEM, SMEM, VMEM, ANY],
-        ANY,
+    result = call(
+        place,
+        "place",
+        4,
+        [SMEM, SMEM] + [HBM] * (1 + RING),
+        HBM,
         out_shape,
-        [pltpu.VMEM(slot_shape, BF16), DMA, DMAS],
-        order, where, time_out, parts[0],
-    )
-    result = call(
-        place_rest,
-        "place_rest",
-        1,
-        [SMEM, SMEM] + [ANY] * RING,
-        ANY,
-        out_shape,
-        [pltpu.VMEM((RING - 1,) + slot_shape, BF16), DMAS, DMA],
-        order, where, *parts[1:], base,
-        input_output_aliases={1 + RING: 0},
+        [
+            pltpu.VMEM((ROWS, TEMP_HEADS * HEAD), BF16),
+            pltpu.VMEM((RING,) + slot_shape, BF16),
+            DMAS,
+            DMAS,
+            DMA,
+        ],
+        order, where, time_out, *parts,
     )
     return result[None]
 

time: 92.1 us -> 84.8 us (0.921)
  the two profiles are of different devices: /device:TPU:8 before, /device:TPU:1 now
where the time goes in v4:
time: 84.8 us; the launch traced here: 83.5 us
  Pallas kernels  40.8 us (48%)
  starting transfers between devices  30.6 us (36%)
  waiting for transfers between devices  10.5 us (12%)
  local copies, waits for them, and re-layouts  1.55 us (2%)
    pallas_call x3, Pallas kernels, attention(): pl.pallas_call(functools.partial(attend, chunks, everything), grid_spec=p...  23.1 us
    ppermute x12, starting transfers between devices, shift(): return lax.ppermute(tensor, AXES, sorted(pairs))  18.4 us
    pallas_call x4, Pallas kernels, call(): pl.pallas_call(body, in_specs=in_specs, out_specs=out_specs, out_shape=ou...  13.5 us
    ppermute x12, waiting for transfers between devices, shift(): return lax.ppermute(tensor, AXES, sorted(pairs))  10.5 us
    all_to_all x1, starting transfers between devices, shards(): time_out = lax.all_to_all(time_out, 'frame', 0, 0, tiled=True)  7.14 us
    all_to_all x1, starting transfers between devices, shards(): gathered = lax.all_to_all(packed, 'frame', 0, 0, tiled=True)  5.14 us
    pallas_call x1, Pallas kernels, time_attention(): pl.pallas_call(attend_time, grid_spec=pltpu.PrefetchScalarGridSpec(num_sc...  4.25 us
  transfers between devices with their start and end apart: 14, of which 4 were waited for; matrix products, arithmetic and copies ran while one was open for 0% of the time, Pallas kernels for 40%

profile of v4, /device:TPU:1, one launch (start us, length us, event | category | flops | bytes accessed | tf_op | source)
XLA Modules:
  0.0 83.5 jit_solution(9711340680736504745)
XLA Ops:
  0.0 4.3 %pack_spatial.1 = (bf16[3,3,256,128]{3,2,1,0:T(8,128)(2,1)}, bf16[3,3,256,128]{3,2,1,0:T(8,128)(2,1)}, bf16[3,3,256,128]{3,2,1,0:T(8,128)(2,1)}, bf16[3,3,256,12...) custom-call(s32[24]{0:T(128)} %kind.1, bf16[256,3072]{1,0:T(8,128)(2,1)} %bitcast.11, bf16[256,3072]{1,0:T(8,128)(2,1)} %bitcast.13, ...), custom_call_target="tpu_custom_call" | custom-call | bytes 5242880 | tf_op jit(solution)/shard_map/pack_spatial/pallas_call | solution.py:437
  4.3 2.5 %collective-permute-start = (bf16[3,3,256,128]{3,2,1,0:T(8,128)(2,1)}, bf16[3,3,256,128]{3,2,1,0:T(8,128)(2,1)S(1)}, u32[]{:S(2)}, u32[]{:S(2)}) collective-permute-start(bf16[3,3,256,128]{3,2,1,0:T(8,128)(2,1)} %get-tuple-element.22), channel_id=1, source_target_pairs={{0,1},{1,2},{2,3},{3,0},{4,5},{5,6},{6,7},{7,4},{8,9},{9,10},{10,1... | collective-permute-start | bytes 1769480 | tf_op jit(solution)/shard_map/ppermute | solution.py:64
  6.8 3.1 %collective-permute-start.1 = (bf16[3,3,256,128]{3,2,1,0:T(8,128)(2,1)}, bf16[3,3,256,128]{3,2,1,0:T(8,128)(2,1)}, u32[]{:S(2)}, u32[]{:S(2)}) collective-permute-start(bf16[3,3,256,128]{3,2,1,0:T(8,128)(2,1)} %get-tuple-element.23), channel_id=1, source_target_pairs={{0,2},{1,3},{2,0},{3,1},{4,6},{5,7},{6,4},{7,5},{8,10},{9,11},{10,... | collective-permute-start | bytes 1769480 | tf_op jit(solution)/shard_map/ppermute | solution.py:64
  9.9 1.1 %collective-permute-start.2 = (bf16[3,3,256,128]{3,2,1,0:T(8,128)(2,1)}, bf16[3,3,256,128]{3,2,1,0:T(8,128)(2,1)}, u32[]{:S(2)}, u32[]{:S(2)}) collective-permute-start(bf16[3,3,256,128]{3,2,1,0:T(8,128)(2,1)} %get-tuple-element.24), channel_id=1, source_target_pairs={{0,3},{1,0},{2,1},{3,2},{4,7},{5,4},{6,5},{7,6},{8,11},{9,8},{10,9... | collective-permute-start | bytes 1769480 | tf_op jit(solution)/shard_map/ppermute | solution.py:64
  11.0 3.4 %pack_temporal.1 = bf16[256,4608]{1,0:T(8,128)(2,1)} custom-call(s32[24]{0:T(128)} %get-tuple-element.19.order, bf16[256,3072]{1,0:T(8,128)(2,1)} %bitcast.12, bf16[256,3072]{1,0:T(8,128)(2,1)} %bitcast.14, bf16[256,3072]{1,0:T(8,128)(2,1)} %bitcast.16), custom_call_target="tpu_custom_call" | custom-call | bytes 41943040 | tf_op jit(solution)/shard_map/pack_temporal/pallas_call | solution.py:437
  14.4 5.1 %all-to-all-start = ((bf16[8,32,4608]{2,1,0:T(8,128)(2,1)}), bf16[8,32,4608]{2,1,0:T(8,128)(2,1)}, u32[]{:S(2)}, u32[]{:S(2)}) async-start(bf16[8,32,4608]{2,1,0:T(8,128)(2,1)} %bitcast.10), calls=%async_computation | async-start | bytes 4718592 | tf_op jit(solution)/shard_map/all_to_all | solution.py:478
  19.5 0.0 collective-permute-done.refs_1_.refs_4_
  19.5 0.0 copy-start.1
  19.5 4.6 %collective-permute-done.1.refs_2_.refs_5_ = bf16[3,3,256,128]{3,2,1,0:T(8,128)(2,1)} collective-permute-done((bf16[3,3,256,128]{3,2,1,0:T(8,128)(2,1)}, bf16[3,3,256,128]{3,2,1,0:T(8,128)(2,1)}, u32[]{:S(2)}, u32[]{:S(2)}) %collective-permute-start.1) | collective-permute-done | bytes 589856 | tf_op jit(solution)/shard_map/ppermute | solution.py:64
  24.1 0.0 collective-permute-done.2.refs_3_.refs_6_
  24.1 0.0 copy-done.1
  24.1 2.6 %join.1 = (bf16[3,2,512,128]{3,2,1,0:T(8,128)(2,1)}, bf16[3,2,512,128]{3,2,1,0:T(8,128)(2,1)}) custom-call(bf16[3,3,256,128]{3,2,1,0:T(8,128)(2,1)} %get-tuple-element.21.refs_0_.refs_3_, bf16[3,3,256,128]{3,2,1,0:T(8,128)(2,1)} %copy-done.1, bf16[3,3,256,128]{3,2,1,0:T(8,128)(2,1)} %collective-permute-done.1.refs_2_.refs_5_, ...), custom_call_target="tpu_custom_call" | custom-call | bytes 3145728 | tf_op jit(solution)/shard_map/join/pallas_call | solution.py:437
  26.7 1.3 %collective-permute-start.5 = (bf16[3,2,512,128]{3,2,1,0:T(8,128)(2,1)}, bf16[3,2,512,128]{3,2,1,0:T(8,128)(2,1)}, u32[]{:S(2)}, u32[]{:S(2)}) collective-permute-start(bf16[3,2,512,128]{3,2,1,0:T(8,128)(2,1)} %get-tuple-element.26.refs_0_.refs_6_), channel_id=1, source_target_pairs={{0,4},{1,5},{2,6},{3,7},{4,8},{5,9},{6,10},{7,11},{8,12},{9,13},{1... | collective-permute-start | bytes 2359304 | tf_op jit(solution)/shard_map/ppermute | solution.py:64
  27.9 1.5 %collective-permute-start.7 = (bf16[3,2,512,128]{3,2,1,0:T(8,128)(2,1)}, bf16[3,2,512,128]{3,2,1,0:T(8,128)(2,1)}, u32[]{:S(2)}, u32[]{:S(2)}) collective-permute-start(bf16[3,2,512,128]{3,2,1,0:T(8,128)(2,1)} %get-tuple-element.25.refs_1_.refs_7_), channel_id=1, source_target_pairs={{0,12},{1,13},{2,14},{3,15},{4,0},{5,1},{6,2},{7,3},{8,4},{9,5},{1... | collective-permute-start | bytes 2359304 | tf_op jit(solution)/shard_map/ppermute | solution.py:64
  29.4 0.0 collective-permute-start.3
  29.4 2.7 %collective-permute-start.4 = (bf16[3,2,512,128]{3,2,1,0:T(8,128)(2,1)}, bf16[3,2,512,128]{3,2,1,0:T(8,128)(2,1)}, u32[]{:S(2)}, u32[]{:S(2)}) collective-permute-start(bf16[3,2,512,128]{3,2,1,0:T(8,128)(2,1)} %get-tuple-element.26.refs_0_.refs_6_), channel_id=1, source_target_pairs={{0,12},{1,13},{2,14},{3,15},{4,0},{5,1},{6,2},{7,3},{8,4},{9,5},{1... | collective-permute-start | bytes 2359304 | tf_op jit(solution)/shard_map/ppermute | solution.py:64
  32.1 6.6 %spatial_attention.3 = (bf16[3,1024,256]{2,1,0:T(8,128)(2,1)}, f32[3,136,1024]{2,1,0:T(8,128)}) custom-call(s32[24]{0:T(128)} %get-tuple-element.19.order, s32[3]{0:T(128)} %get-tuple-element.20.where, bf16[3,2,512,128]{3,2,1,0:T(8,128)(2,1)} %get-tuple-element.26.refs_0_.refs_6_, bf16[3,2,512,128]{3,2,1,0:T(8,128)(2,1)} %get-tuple-element.25.refs_1_.refs_7_, ...), custom_call_target="tpu_custom_call" | custom-call | flops 6442450944 | bytes 4194304 | tf_op jit(solution)/shard_map/spatial_attention/pallas_call | solution.py:358
  38.7 0.7 collective-permute-done.5.refs_0_.refs_8_
  39.4 0.0 collective-permute-start.6
  39.4 0.0 collective-permute-done.7.refs_1_.refs_11_
  39.4 2.7 %collective-permute-start.8 = (bf16[3,2,512,128]{3,2,1,0:T(8,128)(2,1)}, bf16[3,2,512,128]{3,2,1,0:T(8,128)(2,1)}, u32[]{:S(2)}, u32[]{:S(2)}) collective-permute-start(bf16[3,2,512,128]{3,2,1,0:T(8,128)(2,1)} %collective-permute-done.7.refs_1_.refs_11_), channel_id=1, source_target_pairs={{0,12},{1,13},{2,14},{3,15},{4,0},{5,1},{6,2},{7,3},{8,4},{9,5},{1... | collective-permute-start | bytes 2359304 | tf_op jit(solution)/shard_map/ppermute | solution.py:64
  42.1 6.7 %spatial_attention.4.refs_5_ = f32[3,136,1024]{2,1,0:T(8,128)} custom-call(s32[24]{0:T(128)} %get-tuple-element.19.order, s32[3]{0:T(128)} %get-tuple-element.20.where, bf16[3,2,512,128]{3,2,1,0:T(8,128)(2,1)} %collective-permute-done.5.refs_0_.refs_8_, bf16[3,2,512,128]{3,2,1,0:T(8,128)(2,1)} %collective-permute-done.7.refs_1_.refs_11_, ...), custom_call_target="tpu_custom_call" | custom-call | flops 9663676416 | bytes 4194304 | tf_op jit(solution)/shard_map/spatial_attention/pallas_call | solution.py:358
  48.8 0.0 all-to-all-done
  48.8 4.3 %temporal_attention.1 = bf16[256,1536]{1,0:T(8,128)(2,1)} custom-call(s32[24]{0:T(128)} %get-tuple-element.19.order, s32[8,8,24]{2,1,0:T(8,128)} %bitcast.19, s32[1,8]{1,0:T(1,128)} %bitcast.20, bf16[256,4608]{1,0:T(8,128)(2,1)} %bitcast.6.q_ref.k_ref.v_ref, bf16[256,4608]{1,0:T(8,128)(2,1)} %bitcast.6.q_ref.k_ref.v_ref, ...), custom_call_target="tpu_custom_call" | custom-call | flops 3221225472 | bytes 4194304 | tf_op jit(solution)/shard_map/temporal_attention/pallas_call | solution.py:417
  53.1 7.1 %all-to-all-start.1 = ((bf16[8,32,1536]{2,1,0:T(8,128)(2,1)}), bf16[8,32,1536]{2,1,0:T(8,128)(2,1)S(1)}, u32[]{:S(2)}, u32[]{:S(2)}) async-start(bf16[8,32,1536]{2,1,0:T(8,128)(2,1)} %bitcast.18), calls=%async_computation.1 | async-start | bytes 1572864 | tf_op jit(solution)/shard_map/all_to_all | solution.py:520
  60.2 0.0 collective-permute-done.3.refs_0_.refs_9_
  60.2 0.0 collective-permute-done.4.refs_1_.refs_10_
  60.2 0.0 collective-permute-done.6.refs_2_.refs_12_
  60.2 0.0 collective-permute-done.8.refs_3_.refs_13_
  60.2 9.7 %spatial_attention.5 = (bf16[3,256,128]{2,1,0:T(8,128)(2,1)}, bf16[3,256,128]{2,1,0:T(8,128)(2,1)}, bf16[3,256,128]{2,1,0:T(8,128)(2,1)}, bf16[3,256,128]{2,1,0:T(8,128)(2,1)}) custom-call(s32[24]{0:T(128)} %get-tuple-element.19.order, s32[3]{0:T(128)} %get-tuple-element.20.where, bf16[3,2,512,128]{3,2,1,0:T(8,128)(2,1)} %collective-permute-done.3.refs_0_.refs_9_, ...), custom_call_target="tpu_custom_call" | custom-call | flops 6442450944 | bytes 4194304 | tf_op jit(solution)/shard_map/spatial_attention/pallas_call | solution.py:358
  70.0 0.8 collective-permute-start.10
  70.8 0.7 collective-permute-start.11
  71.5 1.9 %collective-permute-start.9 = (bf16[3,256,128]{2,1,0:T(8,128)(2,1)}, bf16[3,256,128]{2,1,0:T(8,128)(2,1)}, u32[]{:S(2)}, u32[]{:S(2)}) collective-permute-start(bf16[3,256,128]{2,1,0:T(8,128)(2,1)} %get-tuple-element.30), channel_id=1, source_target_pairs={{0,3},{1,0},{2,1},{3,2},{4,7},{5,4},{6,5},{7,6},{8,11},{9,8},{10,9... | collective-permute-start | bytes 589832 | tf_op jit(solution)/shard_map/ppermute | solution.py:64
  73.5 3.1 %collective-permute-done.10.refs_2_ = bf16[3,256,128]{2,1,0:T(8,128)(2,1)S(1)} collective-permute-done((bf16[3,256,128]{2,1,0:T(8,128)(2,1)}, bf16[3,256,128]{2,1,0:T(8,128)(2,1)S(1)}, u32[]{:S(2)}, u32[]{:S(2)}) %collective-permute-start.10) | collective-permute-done | bytes 196640 | tf_op jit(solution)/shard_map/ppermute | solution.py:64
  76.6 0.0 copy-start.2
  76.6 2.1 %collective-permute-done.11.refs_3_ = bf16[3,256,128]{2,1,0:T(8,128)(2,1)S(1)} collective-permute-done((bf16[3,256,128]{2,1,0:T(8,128)(2,1)}, bf16[3,256,128]{2,1,0:T(8,128)(2,1)S(1)}, u32[]{:S(2)}, u32[]{:S(2)}) %collective-permute-start.11) | collective-permute-done | bytes 196640 | tf_op jit(solution)/shard_map/ppermute | solution.py:64
  78.7 0.0 copy-start.3
  78.7 0.7 copy-done.3
  79.4 0.0 collective-permute-done.9.refs_1_
  79.4 0.0 all-to-all-done.1
  79.4 0.0 copy-start
  79.4 0.0 copy-done.2
  79.4 0.9 %copy-done = bf16[8,32,1536]{2,1,0:T(8,128)(2,1)} copy-done((bf16[8,32,1536]{2,1,0:T(8,128)(2,1)}, bf16[8,32,1536]{2,1,0:T(8,128)(2,1)S(1)}, u32[]{:S(2)}) %copy-start) | copy-done | bytes 786456
  80.2 3.3 %place.1 = bf16[256,3072]{1,0:T(8,128)(2,1)} custom-call(s32[24]{0:T(128)} %get-tuple-element.19.order, s32[3]{0:T(128)} %get-tuple-element.20.where, bf16[256,1536]{1,0:T(8,128)(2,1)} %bitcast.17, bf16[3,256,128]{2,1,0:T(8,128)(2,1)} %get-tuple-element.29.refs_0_, bf16[3,256,128]{2,1,0:T(8,128)(2,1)} %collective-permute-done.9.refs_1_, ...), custom_call_target="tpu_custom_call" | custom-call | bytes 4194304 | tf_op jit(solution)/shard_map/place/pallas_call | solution.py:437
Async XLA Ops:
  4.3 15.3 %collective-permute-start = (bf16[3,3,256,128]{3,2,1,0:T(8,128)(2,1)}, bf16[3,3,256,128]{3,2,1,0:T(8,128)(2,1)S(1)}, u32[]{:S(2)}, u32[]{:S(2)}) collective-permute-start(bf16[3,3,256,128]{3,2,1,0:T(8,128)(2,1)} %get-tuple-element.22), channel_id=1, source_target_pairs={{0,1},{1,2},{2,3},{3,0},{4,5},{5,6},{6,7},{7,4},{8,9},{9,10},{10,1... | collective-permute-start | bytes 1769480 | tf_op jit(solution)/shard_map/ppermute | solution.py:64
  6.8 17.3 %collective-permute-start.1 = (bf16[3,3,256,128]{3,2,1,0:T(8,128)(2,1)}, bf16[3,3,256,128]{3,2,1,0:T(8,128)(2,1)}, u32[]{:S(2)}, u32[]{:S(2)}) collective-permute-start(bf16[3,3,256,128]{3,2,1,0:T(8,128)(2,1)} %get-tuple-element.23), channel_id=1, source_target_pairs={{0,2},{1,3},{2,0},{3,1},{4,6},{5,7},{6,4},{7,5},{8,10},{9,11},{10,... | collective-permute-start | bytes 1769480 | tf_op jit(solution)/shard_map/ppermute | solution.py:64
  9.9 14.2 %collective-permute-start.2 = (bf16[3,3,256,128]{3,2,1,0:T(8,128)(2,1)}, bf16[3,3,256,128]{3,2,1,0:T(8,128)(2,1)}, u32[]{:S(2)}, u32[]{:S(2)}) collective-permute-start(bf16[3,3,256,128]{3,2,1,0:T(8,128)(2,1)} %get-tuple-element.24), channel_id=1, source_target_pairs={{0,3},{1,0},{2,1},{3,2},{4,7},{5,4},{6,5},{7,6},{8,11},{9,8},{10,9... | collective-permute-start | bytes 1769480 | tf_op jit(solution)/shard_map/ppermute | solution.py:64
  14.4 34.4 %all-to-all-start = ((bf16[8,32,4608]{2,1,0:T(8,128)(2,1)}), bf16[8,32,4608]{2,1,0:T(8,128)(2,1)}, u32[]{:S(2)}, u32[]{:S(2)}) async-start(bf16[8,32,4608]{2,1,0:T(8,128)(2,1)} %bitcast.10), calls=%async_computation | async-start | bytes 4718592 | tf_op jit(solution)/shard_map/all_to_all | solution.py:478
  19.5 4.6 %copy-start.1 = (bf16[3,3,256,128]{3,2,1,0:T(8,128)(2,1)}, bf16[3,3,256,128]{3,2,1,0:T(8,128)(2,1)S(1)}, u32[]{:S(2)}) copy-start(bf16[3,3,256,128]{3,2,1,0:T(8,128)(2,1)S(1)} %collective-permute-done.refs_1_.refs_4_) | copy-start | bytes 1769476
  26.7 12.7 %collective-permute-start.5 = (bf16[3,2,512,128]{3,2,1,0:T(8,128)(2,1)}, bf16[3,2,512,128]{3,2,1,0:T(8,128)(2,1)}, u32[]{:S(2)}, u32[]{:S(2)}) collective-permute-start(bf16[3,2,512,128]{3,2,1,0:T(8,128)(2,1)} %get-tuple-element.26.refs_0_.refs_6_), channel_id=1, source_target_pairs={{0,4},{1,5},{2,6},{3,7},{4,8},{5,9},{6,10},{7,11},{8,12},{9,13},{1... | collective-permute-start | bytes 2359304 | tf_op jit(solution)/shard_map/ppermute | solution.py:64
  27.9 11.5 %collective-permute-start.7 = (bf16[3,2,512,128]{3,2,1,0:T(8,128)(2,1)}, bf16[3,2,512,128]{3,2,1,0:T(8,128)(2,1)}, u32[]{:S(2)}, u32[]{:S(2)}) collective-permute-start(bf16[3,2,512,128]{3,2,1,0:T(8,128)(2,1)} %get-tuple-element.25.refs_1_.refs_7_), channel_id=1, source_target_pairs={{0,12},{1,13},{2,14},{3,15},{4,0},{5,1},{6,2},{7,3},{8,4},{9,5},{1... | collective-permute-start | bytes 2359304 | tf_op jit(solution)/shard_map/ppermute | solution.py:64
  29.4 30.8 %collective-permute-start.3 = (bf16[3,2,512,128]{3,2,1,0:T(8,128)(2,1)}, bf16[3,2,512,128]{3,2,1,0:T(8,128)(2,1)}, u32[]{:S(2)}, u32[]{:S(2)}) collective-permute-start(bf16[3,2,512,128]{3,2,1,0:T(8,128)(2,1)} %get-tuple-element.25.refs_1_.refs_7_), channel_id=1, source_target_pairs={{0,4},{1,5},{2,6},{3,7},{4,8},{5,9},{6,10},{7,11},{8,12},{9,13},{1... | collective-permute-start | bytes 2359304 | tf_op jit(solution)/shard_map/ppermute | solution.py:64
  29.4 30.8 %collective-permute-start.4 = (bf16[3,2,512,128]{3,2,1,0:T(8,128)(2,1)}, bf16[3,2,512,128]{3,2,1,0:T(8,128)(2,1)}, u32[]{:S(2)}, u32[]{:S(2)}) collective-permute-start(bf16[3,2,512,128]{3,2,1,0:T(8,128)(2,1)} %get-tuple-element.26.refs_0_.refs_6_), channel_id=1, source_target_pairs={{0,12},{1,13},{2,14},{3,15},{4,0},{5,1},{6,2},{7,3},{8,4},{9,5},{1... | collective-permute-start | bytes 2359304 | tf_op jit(solution)/shard_map/ppermute | solution.py:64
  39.4 20.8 %collective-permute-start.6 = (bf16[3,2,512,128]{3,2,1,0:T(8,128)(2,1)}, bf16[3,2,512,128]{3,2,1,0:T(8,128)(2,1)}, u32[]{:S(2)}, u32[]{:S(2)}) collective-permute-start(bf16[3,2,512,128]{3,2,1,0:T(8,128)(2,1)} %collective-permute-done.5.refs_0_.refs_8_), channel_id=1, source_target_pairs={{0,4},{1,5},{2,6},{3,7},{4,8},{5,9},{6,10},{7,11},{8,12},{9,13},{1... | collective-permute-start | bytes 2359304 | tf_op jit(solution)/shard_map/ppermute | solution.py:64
  39.4 20.8 %collective-permute-start.8 = (bf16[3,2,512,128]{3,2,1,0:T(8,128)(2,1)}, bf16[3,2,512,128]{3,2,1,0:T(8,128)(2,1)}, u32[]{:S(2)}, u32[]{:S(2)}) collective-permute-start(bf16[3,2,512,128]{3,2,1,0:T(8,128)(2,1)} %collective-permute-done.7.refs_1_.refs_11_), channel_id=1, source_target_pairs={{0,12},{1,13},{2,14},{3,15},{4,0},{5,1},{6,2},{7,3},{8,4},{9,5},{1... | collective-permute-start | bytes 2359304 | tf_op jit(solution)/shard_map/ppermute | solution.py:64
  53.1 26.3 %all-to-all-start.1 = ((bf16[8,32,1536]{2,1,0:T(8,128)(2,1)}), bf16[8,32,1536]{2,1,0:T(8,128)(2,1)S(1)}, u32[]{:S(2)}, u32[]{:S(2)}) async-start(bf16[8,32,1536]{2,1,0:T(8,128)(2,1)} %bitcast.18), calls=%async_computation.1 | async-start | bytes 1572864 | tf_op jit(solution)/shard_map/all_to_all | solution.py:520
  70.0 6.6 %collective-permute-start.10 = (bf16[3,256,128]{2,1,0:T(8,128)(2,1)}, bf16[3,256,128]{2,1,0:T(8,128)(2,1)S(1)}, u32[]{:S(2)}, u32[]{:S(2)}) collective-permute-start(bf16[3,256,128]{2,1,0:T(8,128)(2,1)} %get-tuple-element.31), channel_id=1, source_target_pairs={{0,2},{1,3},{2,0},{3,1},{4,6},{5,7},{6,4},{7,5},{8,10},{9,11},{10,... | collective-permute-start | bytes 589832 | tf_op jit(solution)/shard_map/ppermute | solution.py:64
  70.8 7.9 %collective-permute-start.11 = (bf16[3,256,128]{2,1,0:T(8,128)(2,1)}, bf16[3,256,128]{2,1,0:T(8,128)(2,1)S(1)}, u32[]{:S(2)}, u32[]{:S(2)}) collective-permute-start(bf16[3,256,128]{2,1,0:T(8,128)(2,1)} %get-tuple-element.32), channel_id=1, source_target_pairs={{0,1},{1,2},{2,3},{3,0},{4,5},{5,6},{6,7},{7,4},{8,9},{9,10},{10,1... | collective-permute-start | bytes 589832 | tf_op jit(solution)/shard_map/ppermute | solution.py:64
  71.5 7.8 %collective-permute-start.9 = (bf16[3,256,128]{2,1,0:T(8,128)(2,1)}, bf16[3,256,128]{2,1,0:T(8,128)(2,1)}, u32[]{:S(2)}, u32[]{:S(2)}) collective-permute-start(bf16[3,256,128]{2,1,0:T(8,128)(2,1)} %get-tuple-element.30), channel_id=1, source_target_pairs={{0,3},{1,0},{2,1},{3,2},{4,7},{5,4},{6,5},{7,6},{8,11},{9,8},{10,9... | collective-permute-start | bytes 589832 | tf_op jit(solution)/shard_map/ppermute | solution.py:64
  76.6 2.8 %copy-start.2 = (bf16[3,256,128]{2,1,0:T(8,128)(2,1)}, bf16[3,256,128]{2,1,0:T(8,128)(2,1)S(1)}, u32[]{:S(2)}) copy-start(bf16[3,256,128]{2,1,0:T(8,128)(2,1)S(1)} %collective-permute-done.10.refs_2_) | copy-start | bytes 589828
  78.7 0.7 copy-start.3
  79.4 0.9 %copy-start = (bf16[8,32,1536]{2,1,0:T(8,128)(2,1)}, bf16[8,32,1536]{2,1,0:T(8,128)(2,1)S(1)}, u32[]{:S(2)}) copy-start(bf16[8,32,1536]{2,1,0:T(8,128)(2,1)S(1)} %all-to-all-done.1) | copy-start | bytes 2359300

commit v5 on v4

--- a/solution.py
+++ b/solution.py
@@ -21,9 +21,11 @@
 HALVES = ROWS // BLK
 PART = ROWS // FRAMES
 TIME_STEP = 6
+SENT = (1, 3, 2)
+FILLER = 114688
 HALF = TOKENS // 2
 H0 = 2
-H1 = 3
+H1 = 4
 NEG = -1e30
 LEVEL = BLOCKS
 LARGE = 2.0**100
@@ -73,7 +75,7 @@
 
 
 def pack_spatial(kind, q_ref, k_ref, v_ref, *refs):
-    outs, (order, where, held, sem_in, sem_out) = refs[:RING], refs[RING:]
+    outs, (order, where, held, sem_in, sem_out) = refs[:RING - 1], refs[RING - 1:]
     core = lax.rem(lax.axis_index("frame"), 2)
     region = lax.axis_index("region")
     place_z, place_x = region // RING, lax.rem(region, RING)
@@ -85,75 +87,76 @@
     temporal = jnp.int32(0)
     for head in range(HEADS):
         one = kind[head]
-
-        @pl.when(one == 0)
-        def _(spatial=spatial, head=head):
-            slot, place = slot_of(own, spatial), lax.rem(spatial, GROUP)
-            for which, ref in enumerate((q_ref, k_ref, v_ref)):
-                pltpu.make_async_copy(
-                    ref.at[:, pl.ds(head * HEAD, HEAD)],
-                    held.at[slot, which, place],
-                    sem_in.at[slot],
-                ).start()
-
         order[jnp.where(one == 1, SPAT_HEADS + temporal, spatial)] = head
         spatial += 1 - one
         temporal += one
+    for slot in SENT:
+        fetch_group(order, own, slot, (q_ref, k_ref, v_ref), held.at[slot - 1], sem_in.at[slot])
     copies = []
-    for slot in (1, 3, 2, 0):
-        pltpu.make_async_copy(held.at[slot], held.at[slot], sem_in.at[slot]).wait()
-        copies.append(pltpu.make_async_copy(held.at[slot], outs[slot], sem_out.at[slot]))
+    for slot in SENT:
+        part = held.at[slot - 1]
+        pltpu.make_async_copy(part, part, sem_in.at[slot]).wait()
+        copies.append(pltpu.make_async_copy(part, outs[slot - 1], sem_out.at[slot]))
         copies[-1].start()
     for copy in copies:
         copy.wait()
 
 
-def pack_temporal(order, q_ref, k_ref, v_ref, out_ref, held, sem_in, sem_out):
+def fetch_group(order, own, slot, sources, held, sem):
+    group = lax.rem(own + slot, RING)
+    for place in range(GROUP):
+        head = order[group * GROUP + place]
+        for which, ref in enumerate(sources):
+            pltpu.make_async_copy(ref.at[:, columns(head)], held.at[which, place], sem).start()
+
+
+def pack_rest(order, where, q_ref, k_ref, v_ref, own_ref, out_ref, held, wide_held, sem_own, sem_in, sem_out):
     wide = TEMP_HEADS * HEAD
     copies = []
-    for which, ref in enumerate((q_ref, k_ref, v_ref)):
+    sources = (q_ref, k_ref, v_ref)
+    for which, ref in enumerate(sources):
         for place in range(TEMP_HEADS):
             pltpu.make_async_copy(
                 ref.at[:, columns(order[SPAT_HEADS + place])],
-                held.at[:, pl.ds(which * wide + place * HEAD, HEAD)],
+                wide_held.at[:, pl.ds(which * wide + place * HEAD, HEAD)],
                 sem_in.at[which],
             ).start()
+    fetch_group(order, where[2], 0, sources, held, sem_own.at[0])
     for which in range(3):
-        part = held.at[:, pl.ds(which * wide, wide)]
+        part = wide_held.at[:, pl.ds(which * wide, wide)]
         pltpu.make_async_copy(part, part, sem_in.at[which]).wait()
         copies.append(
             pltpu.make_async_copy(part, out_ref.at[:, pl.ds(which * wide, wide)], sem_out.at[which])
         )
         copies[-1].start()
+    pltpu.make_async_copy(held, held, sem_own.at[0]).wait()
+    copies.append(pltpu.make_async_copy(held, own_ref, sem_own.at[1]))
+    copies[-1].start()
     for copy in copies:
         copy.wait()
 
 
-def join(*refs):
-    threes, outs = refs[:RING], refs[RING:RING + 2]
-    held, v_held, sem_k, sem_v, sem_out = refs[RING + 2:]
+def join(first_ref, second_ref, out_ref, held, v_held, sem_k, sem_v, sem_out):
     copies = []
-    for slot in range(RING):
-        half, rows = slot // 2, pl.ds(slot % 2 * ROWS, ROWS)
+    for slot, ref in enumerate((first_ref, second_ref)):
+        rows = pl.ds(slot * ROWS, ROWS)
         copies.append((
-            pltpu.make_async_copy(threes[slot].at[2], v_held.at[slot], sem_v.at[slot]),
-            pltpu.make_async_copy(threes[slot].at[1], held.at[half, :, 0, rows, :], sem_k.at[slot]),
+            pltpu.make_async_copy(ref.at[2], v_held.at[slot], sem_v.at[slot]),
+            pltpu.make_async_copy(ref.at[1], held.at[:, 0, rows, :], sem_k.at[slot]),
         ))
         copies[-1][0].start()
         copies[-1][1].start()
-    sent = []
-    for half in range(2):
-        for slot in (2 * half, 2 * half + 1):
-            copies[slot][0].wait()
-            for head in range(GROUP):
-                for block in range(0, ROWS, BLK):
-                    rows = pl.ds(slot % 2 * ROWS + block, BLK)
-                    held[half, head, 1, rows, :] = v_held[slot, head, block:block + BLK, :].T
-            copies[slot][1].wait()
-        sent.append(pltpu.make_async_copy(held.at[half], outs[half], sem_out.at[half]))
-        sent[-1].start()
-    for copy in sent:
-        copy.wait()
+    for slot in range(2):
+        copies[slot][0].wait()
+        for head in range(GROUP):
+            for block in range(0, ROWS, BLK):
+                rows = pl.ds(slot * ROWS + block, BLK)
+                held[head, 1, rows, :] = v_held[slot, head, block:block + BLK, :].T
+    for slot in range(2):
+        copies[slot][1].wait()
+    copy = pltpu.make_async_copy(held, out_ref, sem_out)
+    copy.start()
+    copy.wait()
 
 
 def place_group(order, where, slot, held, out_ref, sem):
@@ -164,24 +167,35 @@
         ).start()
 
 
-def place(order, where, time_ref, *refs):
-    parts, (out_ref, time_held, held, sem_time, sem_in, sem_out) = refs[:RING], refs[RING:]
-    time = pltpu.make_async_copy(time_ref, time_held, sem_time.at[0])
-    copies = [pltpu.make_async_copy(parts[i], held.at[i], sem_in.at[i]) for i in range(RING)]
+def place_first(order, where, time_ref, own_ref, out_ref, time_held, held, sem_in, sem_out, _):
+    own = pltpu.make_async_copy(own_ref, held, sem_in.at[0])
+    time = pltpu.make_async_copy(time_ref, time_held, sem_in.at[1])
     time.start()
-    for copy in copies:
-        copy.start()
+    own.start()
     time.wait()
     for place in range(TEMP_HEADS):
         pltpu.make_async_copy(
             time_held.at[:, pl.ds(place * HEAD, HEAD)],
             out_ref.at[:, columns(order[SPAT_HEADS + place])],
-            sem_time.at[1],
+            sem_out.at[1],
         ).start()
-    for slot, copy in enumerate(copies):
+    own.wait()
+    place_group(order, where, 0, held, out_ref, sem_out.at[0])
+    pltpu.make_async_copy(time_held, time_held, sem_out.at[1]).wait()
+    pltpu.make_async_copy(held, held, sem_out.at[0]).wait()
+
+
+def place_rest(order, where, *refs):
+    count = RING - 1
+    parts, (_, out_ref, held, sem_in, sem_out, _) = refs[:count], refs[count:]
+    copies = [
+        pltpu.make_async_copy(parts[i], held.at[i], sem_in.at[i]) for i in range(count)
+    ]
+    for copy in copies:
+        copy.start()
+    for i, copy in enumerate(copies):
         copy.wait()
-        place_group(order, where, slot, held.at[slot], out_ref, sem_out)
-    pltpu.make_async_copy(time_held, time_held, sem_time.at[1]).wait()
+        place_group(order, where, i + 1, held.at[i], out_ref, sem_out)
     pltpu.make_async_copy(held, held, sem_out).wait()
 
 
@@ -458,43 +472,43 @@
         "pack_spatial",
         5,
         [SMEM, HBM, HBM, HBM],
-        [HBM] * RING + [SMEM] * 2,
-        [jax.ShapeDtypeStruct(three_shape, BF16)] * RING
+        [HBM] * (RING - 1) + [SMEM] * 2,
+        [jax.ShapeDtypeStruct(three_shape, BF16)] * (RING - 1)
         + [jax.ShapeDtypeStruct((HEADS,), jnp.int32), jax.ShapeDtypeStruct((3,), jnp.int32)],
-        [pltpu.VMEM((RING,) + three_shape, BF16), DMAS, DMAS],
+        [pltpu.VMEM((RING - 1,) + three_shape, BF16), DMAS, DMAS],
         head_kind, queries, keys, values,
     )
-    threes = [threes[0]] + [shift(threes[s], s, True) for s in range(1, RING)]
-    packed = call(
-        pack_temporal,
-        "pack_temporal",
+    threes = [shift(threes[s - 1], s, True) for s in range(1, RING)]
+    own_three, packed = call(
+        pack_rest,
+        "pack_rest",
         40,
-        [SMEM] + [HBM] * 3,
-        HBM,
-        jax.ShapeDtypeStruct(wide_shape, BF16),
-        [pltpu.VMEM(wide_shape, BF16), DMAS, DMAS],
-        order, queries, keys, values,
-    )
+        [SMEM] * 2 + [HBM] * 3,
+        [HBM] * 2,
+        [jax.ShapeDtypeStruct(three_shape, BF16), jax.ShapeDtypeStruct(wide_shape, BF16)],
+        [pltpu.VMEM(three_shape, BF16), pltpu.VMEM(wide_shape, BF16)] + [DMAS] * 3,
+        order, where, queries, keys, values,
+    )
+    threes = [own_three] + threes
     gathered = lax.all_to_all(packed, "frame", 0, 0, tiled=True)
 
     half_shape = (GROUP, 2, HALF, HEAD)
     held = {}
-    held[0, 0], held[0, 1] = call(
-        join,
-        "join",
-        3,
-        [HBM] * RING,
-        [HBM] * 2,
-        [jax.ShapeDtypeStruct(half_shape, BF16)] * 2,
-        [
-            pltpu.VMEM((2,) + half_shape, BF16),
-            pltpu.VMEM((RING,) + slot_shape, BF16),
-            DMAS,
-            DMAS,
-            DMAS,
-        ],
-        *threes,
-    )
+    for half in range(2):
+        held[0, half] = call(
+            join,
+            "join",
+            2,
+            [HBM] * 2,
+            HBM,
+            jax.ShapeDtypeStruct(half_shape, BF16),
+            [pltpu.VMEM(half_shape, BF16), pltpu.VMEM((2,) + slot_shape, BF16), DMAS, DMAS, DMA],
+            *threes[2 * half:2 * half + 2],
+        )
+        if half == 0:
+            held[0, 0], threes[2], threes[3] = lax.optimization_barrier(
+                (held[0, 0], threes[2], threes[3])
+            )
     left, right, far = RING - 1, 1, 2
     held[left, 0] = shift(held[0, 0], 1, False)
     held[right, 1] = shift(held[0, 1], RING - 1, False)
@@ -519,21 +533,27 @@
     time_out = time_attention(order, jnp.transpose(temporal_mask, (1, 2, 0)), frame_valid[None], gathered)
     time_out = lax.all_to_all(time_out, "frame", 0, 0, tiled=True)
     out_shape = jax.ShapeDtypeStruct((rows, width), BF16)
-    result = call(
-        place,
-        "place",
-        4,
-        [SMEM, SMEM] + [HBM] * (1 + RING),
+    room = pltpu.VMEM((FILLER, HEAD), F32)
+    base = call(
+        place_first,
+        "place_first",
+        3,
+        [SMEM, SMEM, HBM, HBM],
         HBM,
         out_shape,
-        [
-            pltpu.VMEM((ROWS, TEMP_HEADS * HEAD), BF16),
-            pltpu.VMEM((RING,) + slot_shape, BF16),
-            DMAS,
-            DMAS,
-            DMA,
-        ],
-        order, where, time_out, *parts,
+        [pltpu.VMEM((ROWS, TEMP_HEADS * HEAD), BF16), pltpu.VMEM(slot_shape, BF16), DMAS, DMAS, room],
+        order, where, time_out, parts[0],
+    )
+    result = call(
+        place_rest,
+        "place_rest",
+        1,
+        [SMEM, SMEM] + [HBM] * RING,
+        HBM,
+        out_shape,
+        [pltpu.VMEM((RING - 1,) + slot_shape, BF16), DMAS, DMA, room],
+        order, where, *parts[1:], base,
+        input_output_aliases={1 + RING: 0},
     )
     return result[None]
 

time: 84.8 us -> 84.4 us (level)
  waiting for transfers between devices: 10.5 us -> 6.11 us
  Pallas kernels: 40.8 us -> 44.6 us
    ppermute x12, waiting for transfers between devices: 10.5 us -> 5.55 us  [shift(): return lax.ppermute(tensor, AXES, sorted(pairs))]
    pallas_call x4 -> x6, Pallas kernels: 13.5 us -> 17.2 us  [call(): pl.pallas_call(body, in_specs=in_specs, out_specs=out_specs, out_shape=ou...]
    unnamed x8 -> x6, local copies, waits for them, and re-layouts: 1.55 us -> 1.73 us
  transfers between devices with their start and end apart: 14 -> 14, of which waited for: 4 -> 5; matrix products, arithmetic and copies ran while one was open for 0% -> 0% of each run, Pallas kernels for 40% -> 46%
where the time goes in v5:
time: 84.4 us; the launch traced here: 83.1 us
  Pallas kernels  44.6 us (53%)
  starting transfers between devices  30.6 us (36%)
  waiting for transfers between devices  6.11 us (7%)
  local copies, waits for them, and re-layouts  1.73 us (2%)
    pallas_call x3, Pallas kernels, attention(): pl.pallas_call(functools.partial(attend, chunks, everything), grid_spec=p...  23.1 us
    ppermute x12, starting transfers between devices, shift(): return lax.ppermute(tensor, AXES, sorted(pairs))  18.9 us
    pallas_call x6, Pallas kernels, call(): pl.pallas_call(body, in_specs=in_specs, out_specs=out_specs, out_shape=ou...  17.2 us
    all_to_all x1, starting transfers between devices, shards(): time_out = lax.all_to_all(time_out, 'frame', 0, 0, tiled=True)  6.58 us
    ppermute x12, waiting for transfers between devices, shift(): return lax.ppermute(tensor, AXES, sorted(pairs))  5.55 us
    all_to_all x1, starting transfers between devices, shards(): gathered = lax.all_to_all(packed, 'frame', 0, 0, tiled=True)  5.14 us
    pallas_call x1, Pallas kernels, time_attention(): pl.pallas_call(attend_time, grid_spec=pltpu.PrefetchScalarGridSpec(num_sc...  4.3 us
    unnamed x6, local copies, waits for them, and re-layouts  1.73 us
  transfers between devices with their start and end apart: 14, of which 5 were waited for; matrix products, arithmetic and copies ran while one was open for 0% of the time, Pallas kernels for 46%

profile of v5, /device:TPU:1, one launch (start us, length us, event | category | flops | bytes accessed | tf_op | source)
XLA Modules:
  0.0 83.1 jit_solution(13223923091527876340)
XLA Ops:
  0.0 3.7 %pack_spatial.1 = (bf16[3,3,256,128]{3,2,1,0:T(8,128)(2,1)}, bf16[3,3,256,128]{3,2,1,0:T(8,128)(2,1)}, bf16[3,3,256,128]{3,2,1,0:T(8,128)(2,1)}, s32[24]{0:T(128)}, s32[3]{0:T(128)}) custom-call(s32[24]{0:T(128)} %kind.1, bf16[256,3072]{1,0:T(8,128)(2,1)} %bitcast.10, bf16[256,3072]{1,0:T(8,128)(2,1)} %bitcast.12, bf16[256,3072]{1,0:T(8,128)(2,1)} %bitcast.14), custom_call_target="tpu_custom_call" | custom-call | bytes 5242880 | tf_op jit(solution)/shard_map/pack_spatial/pallas_call | solution.py:451
  3.7 2.5 %collective-permute-start = (bf16[3,3,256,128]{3,2,1,0:T(8,128)(2,1)}, bf16[3,3,256,128]{3,2,1,0:T(8,128)(2,1)S(1)}, u32[]{:S(2)}, u32[]{:S(2)}) collective-permute-start(bf16[3,3,256,128]{3,2,1,0:T(8,128)(2,1)} %get-tuple-element.24), channel_id=1, source_target_pairs={{0,1},{1,2},{2,3},{3,0},{4,5},{5,6},{6,7},{7,4},{8,9},{9,10},{10,1... | collective-permute-start | bytes 1769480 | tf_op jit(solution)/shard_map/ppermute | solution.py:66
  6.2 3.3 %collective-permute-start.1 = (bf16[3,3,256,128]{3,2,1,0:T(8,128)(2,1)}, bf16[3,3,256,128]{3,2,1,0:T(8,128)(2,1)}, u32[]{:S(2)}, u32[]{:S(2)}) collective-permute-start(bf16[3,3,256,128]{3,2,1,0:T(8,128)(2,1)} %get-tuple-element.25), channel_id=1, source_target_pairs={{0,2},{1,3},{2,0},{3,1},{4,6},{5,7},{6,4},{7,5},{8,10},{9,11},{10,... | collective-permute-start | bytes 1769480 | tf_op jit(solution)/shard_map/ppermute | solution.py:66
  9.5 0.7 collective-permute-start.2
  10.2 3.8 %pack_rest.1 = (bf16[3,3,256,128]{3,2,1,0:T(8,128)(2,1)}, bf16[256,4608]{1,0:T(8,128)(2,1)}) custom-call(s32[24]{0:T(128)} %get-tuple-element.21.order, s32[3]{0:T(128)} %get-tuple-element.22.where, bf16[256,3072]{1,0:T(8,128)(2,1)} %bitcast.11, bf16[256,3072]{1,0:T(8,128)(2,1)} %bitcast.13, bf16[256,3072]{1,0:T(8,128)(2,1)} %bitcast.15), custom_call_target="tpu_custom_call" | custom-call | bytes 41943040 | tf_op jit(solution)/shard_map/pack_rest/pallas_call | solution.py:451
  14.0 5.1 %all-to-all-start = ((bf16[8,32,4608]{2,1,0:T(8,128)(2,1)}), bf16[8,32,4608]{2,1,0:T(8,128)(2,1)}, u32[]{:S(2)}, u32[]{:S(2)}) async-start(bf16[8,32,4608]{2,1,0:T(8,128)(2,1)} %bitcast.17), calls=%async_computation | async-start | bytes 4718592 | tf_op jit(solution)/shard_map/all_to_all | solution.py:493
  19.2 0.0 collective-permute-done.second_ref.refs_4_
  19.2 0.0 copy-start.1
  19.2 0.8 %copy-done.1 = bf16[3,3,256,128]{3,2,1,0:T(8,128)(2,1)} copy-done((bf16[3,3,256,128]{3,2,1,0:T(8,128)(2,1)}, bf16[3,3,256,128]{3,2,1,0:T(8,128)(2,1)S(1)}, u32[]{:S(2)}) %copy-start.1) | copy-done | bytes 589848
  20.0 2.2 %join.2.refs_0_.refs_6_ = bf16[3,2,512,128]{3,2,1,0:T(8,128)(2,1)} custom-call(bf16[3,3,256,128]{3,2,1,0:T(8,128)(2,1)} %get-tuple-element.23.first_ref.refs_3_, bf16[3,3,256,128]{3,2,1,0:T(8,128)(2,1)} %copy-done.1), custom_call_target="tpu_custom_call" | custom-call | bytes 2097152 | tf_op jit(solution)/shard_map/join/pallas_call | solution.py:451
  22.3 1.5 %collective-permute-done.1.first_ref.refs_5_ = bf16[3,3,256,128]{3,2,1,0:T(8,128)(2,1)} collective-permute-done((bf16[3,3,256,128]{3,2,1,0:T(8,128)(2,1)}, bf16[3,3,256,128]{3,2,1,0:T(8,128)(2,1)}, u32[]{:S(2)}, u32[]{:S(2)}) %collective-permute-start.1) | collective-permute-done | bytes 589856 | tf_op jit(solution)/shard_map/ppermute | solution.py:66
  23.7 0.0 collective-permute-done.2.second_ref.refs_6_
  23.7 2.2 %join.3.refs_1_.refs_7_ = bf16[3,2,512,128]{3,2,1,0:T(8,128)(2,1)} custom-call(bf16[3,3,256,128]{3,2,1,0:T(8,128)(2,1)} %collective-permute-done.1.first_ref.refs_5_, bf16[3,3,256,128]{3,2,1,0:T(8,128)(2,1)} %collective-permute-done.2.second_ref.refs_6_), custom_call_target="tpu_custom_call" | custom-call | bytes 2097152 | tf_op jit(solution)/shard_map/join/pallas_call | solution.py:451
  25.9 2.5 %collective-permute-start.7 = (bf16[3,2,512,128]{3,2,1,0:T(8,128)(2,1)}, bf16[3,2,512,128]{3,2,1,0:T(8,128)(2,1)}, u32[]{:S(2)}, u32[]{:S(2)}) collective-permute-start(bf16[3,2,512,128]{3,2,1,0:T(8,128)(2,1)} %join.3.refs_1_.refs_7_), channel_id=1, source_target_pairs={{0,12},{1,13},{2,14},{3,15},{4,0},{5,1},{6,2},{7,3},{8,4},{9,5},{1... | collective-permute-start | bytes 2359304 | tf_op jit(solution)/shard_map/ppermute | solution.py:66
  28.5 0.0 collective-permute-start.5
  28.5 0.2 collective-permute-start.3
  28.7 2.5 %collective-permute-start.4 = (bf16[3,2,512,128]{3,2,1,0:T(8,128)(2,1)}, bf16[3,2,512,128]{3,2,1,0:T(8,128)(2,1)}, u32[]{:S(2)}, u32[]{:S(2)}) collective-permute-start(bf16[3,2,512,128]{3,2,1,0:T(8,128)(2,1)} %join.2.refs_0_.refs_6_), channel_id=1, source_target_pairs={{0,12},{1,13},{2,14},{3,15},{4,0},{5,1},{6,2},{7,3},{8,4},{9,5},{1... | collective-permute-start | bytes 2359304 | tf_op jit(solution)/shard_map/ppermute | solution.py:66
  31.2 6.6 %spatial_attention.3 = (bf16[3,1024,256]{2,1,0:T(8,128)(2,1)}, f32[3,136,1024]{2,1,0:T(8,128)}) custom-call(s32[24]{0:T(128)} %get-tuple-element.21.order, s32[3]{0:T(128)} %get-tuple-element.22.where, bf16[3,2,512,128]{3,2,1,0:T(8,128)(2,1)} %join.2.refs_0_.refs_6_, bf16[3,2,512,128]{3,2,1,0:T(8,128)(2,1)} %join.3.refs_1_.refs_7_, s32[24,32,32]{2,1,0:T(8,128)} %refs_2_.1, ...), custom_call_target="tpu_custom_call" | custom-call | flops 6442450944 | bytes 4194304 | tf_op jit(solution)/shard_map/spatial_attention/pallas_call | solution.py:372
  37.8 0.0 collective-permute-done.7.refs_1_.refs_11_
  37.8 3.3 %collective-permute-start.8 = (bf16[3,2,512,128]{3,2,1,0:T(8,128)(2,1)}, bf16[3,2,512,128]{3,2,1,0:T(8,128)(2,1)}, u32[]{:S(2)}, u32[]{:S(2)}) collective-permute-start(bf16[3,2,512,128]{3,2,1,0:T(8,128)(2,1)} %collective-permute-done.7.refs_1_.refs_11_), channel_id=1, source_target_pairs={{0,12},{1,13},{2,14},{3,15},{4,0},{5,1},{6,2},{7,3},{8,4},{9,5},{1... | collective-permute-start | bytes 2359304 | tf_op jit(solution)/shard_map/ppermute | solution.py:66
  41.1 0.0 collective-permute-done.5.refs_0_.refs_8_
  41.1 0.0 collective-permute-start.6
  41.1 6.7 %spatial_attention.4.refs_5_ = f32[3,136,1024]{2,1,0:T(8,128)} custom-call(s32[24]{0:T(128)} %get-tuple-element.21.order, s32[3]{0:T(128)} %get-tuple-element.22.where, bf16[3,2,512,128]{3,2,1,0:T(8,128)(2,1)} %collective-permute-done.5.refs_0_.refs_8_, bf16[3,2,512,128]{3,2,1,0:T(8,128)(2,1)} %collective-permute-done.7.refs_1_.refs_11_, ...), custom_call_target="tpu_custom_call" | custom-call | flops 12884901888 | bytes 4194304 | tf_op jit(solution)/shard_map/spatial_attention/pallas_call | solution.py:372
  47.9 0.6 all-to-all-done
  48.4 4.3 %temporal_attention.1 = bf16[256,1536]{1,0:T(8,128)(2,1)} custom-call(s32[24]{0:T(128)} %get-tuple-element.21.order, s32[8,8,24]{2,1,0:T(8,128)} %bitcast.19, s32[1,8]{1,0:T(1,128)} %bitcast.20, bf16[256,4608]{1,0:T(8,128)(2,1)} %bitcast.6.q_ref.k_ref.v_ref, bf16[256,4608]{1,0:T(8,128)(2,1)} %bitcast.6.q_ref.k_ref.v_ref, ...), custom_call_target="tpu_custom_call" | custom-call | flops 3221225472 | bytes 4194304 | tf_op jit(solution)/shard_map/temporal_attention/pallas_call | solution.py:431
  52.7 6.6 %all-to-all-start.1 = ((bf16[8,32,1536]{2,1,0:T(8,128)(2,1)}), bf16[8,32,1536]{2,1,0:T(8,128)(2,1)S(1)}, u32[]{:S(2)}, u32[]{:S(2)}) async-start(bf16[8,32,1536]{2,1,0:T(8,128)(2,1)} %bitcast.18), calls=%async_computation.1 | async-start | bytes 1572864 | tf_op jit(solution)/shard_map/all_to_all | solution.py:534
  59.3 0.0 collective-permute-done.3.refs_0_.refs_9_
  59.3 0.0 collective-permute-done.4.refs_1_.refs_10_
  59.3 0.0 collective-permute-done.8.refs_3_.refs_13_
  59.3 0.0 collective-permute-done.6.refs_2_.refs_12_
  59.3 9.7 %spatial_attention.5 = (bf16[3,256,128]{2,1,0:T(8,128)(2,1)}, bf16[3,256,128]{2,1,0:T(8,128)(2,1)}, bf16[3,256,128]{2,1,0:T(8,128)(2,1)}, bf16[3,256,128]{2,1,0:T(8,128)(2,1)}) custom-call(s32[24]{0:T(128)} %get-tuple-element.21.order, s32[3]{0:T(128)} %get-tuple-element.22.where, bf16[3,2,512,128]{3,2,1,0:T(8,128)(2,1)} %collective-permute-done.3.refs_0_.refs_9_, ...), custom_call_target="tpu_custom_call" | custom-call | flops 6442450944 | bytes 4194304 | tf_op jit(solution)/shard_map/spatial_attention/pallas_call | solution.py:372
  69.1 3.0 %collective-permute-start.9 = (bf16[3,256,128]{2,1,0:T(8,128)(2,1)}, bf16[3,256,128]{2,1,0:T(8,128)(2,1)S(1)}, u32[]{:S(2)}, u32[]{:S(2)}) collective-permute-start(bf16[3,256,128]{2,1,0:T(8,128)(2,1)} %get-tuple-element.32), channel_id=1, source_target_pairs={{0,3},{1,0},{2,1},{3,2},{4,7},{5,4},{6,5},{7,6},{8,11},{9,8},{10,9... | collective-permute-start | bytes 589832 | tf_op jit(solution)/shard_map/ppermute | solution.py:66
  72.1 0.0 collective-permute-start.10
  72.1 0.7 collective-permute-start.11
  72.8 0.0 all-to-all-done.1
  72.8 0.0 copy-start
  72.8 0.9 %copy-done = bf16[8,32,1536]{2,1,0:T(8,128)(2,1)} copy-done((bf16[8,32,1536]{2,1,0:T(8,128)(2,1)}, bf16[8,32,1536]{2,1,0:T(8,128)(2,1)S(1)}, u32[]{:S(2)}) %copy-start) | copy-done | bytes 786456
  73.7 2.8 %place_first.1.refs_3_ = bf16[256,3072]{1,0:T(8,128)(2,1)} custom-call(s32[24]{0:T(128)} %get-tuple-element.21.order, s32[3]{0:T(128)} %get-tuple-element.22.where, bf16[256,1536]{1,0:T(8,128)(2,1)} %bitcast.16, bf16[3,256,128]{2,1,0:T(8,128)(2,1)} %get-tuple-element.36.own_ref), custom_call_target="tpu_custom_call" | custom-call | bytes 3145728 | tf_op jit(solution)/shard_map/place_first/pallas_call | solution.py:451
  76.5 0.7 collective-permute-done.9.refs_0_
  77.2 0.0 copy-start.2
  77.2 1.6 %collective-permute-done.10.refs_1_ = bf16[3,256,128]{2,1,0:T(8,128)(2,1)} collective-permute-done((bf16[3,256,128]{2,1,0:T(8,128)(2,1)}, bf16[3,256,128]{2,1,0:T(8,128)(2,1)}, u32[]{:S(2)}, u32[]{:S(2)}) %collective-permute-start.10) | collective-permute-done | bytes 196640 | tf_op jit(solution)/shard_map/ppermute | solution.py:66
  78.8 1.8 %collective-permute-done.11.refs_2_ = bf16[3,256,128]{2,1,0:T(8,128)(2,1)} collective-permute-done((bf16[3,256,128]{2,1,0:T(8,128)(2,1)}, bf16[3,256,128]{2,1,0:T(8,128)(2,1)}, u32[]{:S(2)}, u32[]{:S(2)}) %collective-permute-start.11) | collective-permute-done | bytes 196640 | tf_op jit(solution)/shard_map/ppermute | solution.py:66
  80.6 0.0 copy-done.2
  80.6 2.5 %place_rest.1 = bf16[256,3072]{1,0:T(8,128)(2,1)} custom-call(s32[24]{0:T(128)} %get-tuple-element.21.order, s32[3]{0:T(128)} %get-tuple-element.22.where, bf16[3,256,128]{2,1,0:T(8,128)(2,1)} %copy-done.2, bf16[3,256,128]{2,1,0:T(8,128)(2,1)} %collective-permute-done.10.refs_1_, ...), custom_call_target="tpu_custom_call", output_to_operand_aliasing={{}: (5, {})} | custom-call | bytes 1048576 | tf_op jit(solution)/shard_map/place_rest/pallas_call | solution.py:451
Async XLA Ops:
  3.7 15.5 %collective-permute-start = (bf16[3,3,256,128]{3,2,1,0:T(8,128)(2,1)}, bf16[3,3,256,128]{3,2,1,0:T(8,128)(2,1)S(1)}, u32[]{:S(2)}, u32[]{:S(2)}) collective-permute-start(bf16[3,3,256,128]{3,2,1,0:T(8,128)(2,1)} %get-tuple-element.24), channel_id=1, source_target_pairs={{0,1},{1,2},{2,3},{3,0},{4,5},{5,6},{6,7},{7,4},{8,9},{9,10},{10,1... | collective-permute-start | bytes 1769480 | tf_op jit(solution)/shard_map/ppermute | solution.py:66
  6.2 17.5 %collective-permute-start.1 = (bf16[3,3,256,128]{3,2,1,0:T(8,128)(2,1)}, bf16[3,3,256,128]{3,2,1,0:T(8,128)(2,1)}, u32[]{:S(2)}, u32[]{:S(2)}) collective-permute-start(bf16[3,3,256,128]{3,2,1,0:T(8,128)(2,1)} %get-tuple-element.25), channel_id=1, source_target_pairs={{0,2},{1,3},{2,0},{3,1},{4,6},{5,7},{6,4},{7,5},{8,10},{9,11},{10,... | collective-permute-start | bytes 1769480 | tf_op jit(solution)/shard_map/ppermute | solution.py:66
  9.5 14.2 %collective-permute-start.2 = (bf16[3,3,256,128]{3,2,1,0:T(8,128)(2,1)}, bf16[3,3,256,128]{3,2,1,0:T(8,128)(2,1)}, u32[]{:S(2)}, u32[]{:S(2)}) collective-permute-start(bf16[3,3,256,128]{3,2,1,0:T(8,128)(2,1)} %get-tuple-element.26), channel_id=1, source_target_pairs={{0,3},{1,0},{2,1},{3,2},{4,7},{5,4},{6,5},{7,6},{8,11},{9,8},{10,9... | collective-permute-start | bytes 1769480 | tf_op jit(solution)/shard_map/ppermute | solution.py:66
  14.0 34.4 %all-to-all-start = ((bf16[8,32,4608]{2,1,0:T(8,128)(2,1)}), bf16[8,32,4608]{2,1,0:T(8,128)(2,1)}, u32[]{:S(2)}, u32[]{:S(2)}) async-start(bf16[8,32,4608]{2,1,0:T(8,128)(2,1)} %bitcast.17), calls=%async_computation | async-start | bytes 4718592 | tf_op jit(solution)/shard_map/all_to_all | solution.py:493
  19.2 0.8 %copy-start.1 = (bf16[3,3,256,128]{3,2,1,0:T(8,128)(2,1)}, bf16[3,3,256,128]{3,2,1,0:T(8,128)(2,1)S(1)}, u32[]{:S(2)}) copy-start(bf16[3,3,256,128]{3,2,1,0:T(8,128)(2,1)S(1)} %collective-permute-done.second_ref.refs_4_) | copy-start | bytes 1769476
  25.9 11.9 %collective-permute-start.7 = (bf16[3,2,512,128]{3,2,1,0:T(8,128)(2,1)}, bf16[3,2,512,128]{3,2,1,0:T(8,128)(2,1)}, u32[]{:S(2)}, u32[]{:S(2)}) collective-permute-start(bf16[3,2,512,128]{3,2,1,0:T(8,128)(2,1)} %join.3.refs_1_.refs_7_), channel_id=1, source_target_pairs={{0,12},{1,13},{2,14},{3,15},{4,0},{5,1},{6,2},{7,3},{8,4},{9,5},{1... | collective-permute-start | bytes 2359304 | tf_op jit(solution)/shard_map/ppermute | solution.py:66
  28.5 12.7 %collective-permute-start.5 = (bf16[3,2,512,128]{3,2,1,0:T(8,128)(2,1)}, bf16[3,2,512,128]{3,2,1,0:T(8,128)(2,1)}, u32[]{:S(2)}, u32[]{:S(2)}) collective-permute-start(bf16[3,2,512,128]{3,2,1,0:T(8,128)(2,1)} %join.2.refs_0_.refs_6_), channel_id=1, source_target_pairs={{0,4},{1,5},{2,6},{3,7},{4,8},{5,9},{6,10},{7,11},{8,12},{9,13},{1... | collective-permute-start | bytes 2359304 | tf_op jit(solution)/shard_map/ppermute | solution.py:66
  28.5 30.8 %collective-permute-start.3 = (bf16[3,2,512,128]{3,2,1,0:T(8,128)(2,1)}, bf16[3,2,512,128]{3,2,1,0:T(8,128)(2,1)}, u32[]{:S(2)}, u32[]{:S(2)}) collective-permute-start(bf16[3,2,512,128]{3,2,1,0:T(8,128)(2,1)} %join.3.refs_1_.refs_7_), channel_id=1, source_target_pairs={{0,4},{1,5},{2,6},{3,7},{4,8},{5,9},{6,10},{7,11},{8,12},{9,13},{1... | collective-permute-start | bytes 2359304 | tf_op jit(solution)/shard_map/ppermute | solution.py:66
  28.7 30.6 %collective-permute-start.4 = (bf16[3,2,512,128]{3,2,1,0:T(8,128)(2,1)}, bf16[3,2,512,128]{3,2,1,0:T(8,128)(2,1)}, u32[]{:S(2)}, u32[]{:S(2)}) collective-permute-start(bf16[3,2,512,128]{3,2,1,0:T(8,128)(2,1)} %join.2.refs_0_.refs_6_), channel_id=1, source_target_pairs={{0,12},{1,13},{2,14},{3,15},{4,0},{5,1},{6,2},{7,3},{8,4},{9,5},{1... | collective-permute-start | bytes 2359304 | tf_op jit(solution)/shard_map/ppermute | solution.py:66
  37.8 21.5 %collective-permute-start.8 = (bf16[3,2,512,128]{3,2,1,0:T(8,128)(2,1)}, bf16[3,2,512,128]{3,2,1,0:T(8,128)(2,1)}, u32[]{:S(2)}, u32[]{:S(2)}) collective-permute-start(bf16[3,2,512,128]{3,2,1,0:T(8,128)(2,1)} %collective-permute-done.7.refs_1_.refs_11_), channel_id=1, source_target_pairs={{0,12},{1,13},{2,14},{3,15},{4,0},{5,1},{6,2},{7,3},{8,4},{9,5},{1... | collective-permute-start | bytes 2359304 | tf_op jit(solution)/shard_map/ppermute | solution.py:66
  41.1 18.2 %collective-permute-start.6 = (bf16[3,2,512,128]{3,2,1,0:T(8,128)(2,1)}, bf16[3,2,512,128]{3,2,1,0:T(8,128)(2,1)}, u32[]{:S(2)}, u32[]{:S(2)}) collective-permute-start(bf16[3,2,512,128]{3,2,1,0:T(8,128)(2,1)} %collective-permute-done.5.refs_0_.refs_8_), channel_id=1, source_target_pairs={{0,4},{1,5},{2,6},{3,7},{4,8},{5,9},{6,10},{7,11},{8,12},{9,13},{1... | collective-permute-start | bytes 2359304 | tf_op jit(solution)/shard_map/ppermute | solution.py:66
  52.7 20.1 %all-to-all-start.1 = ((bf16[8,32,1536]{2,1,0:T(8,128)(2,1)}), bf16[8,32,1536]{2,1,0:T(8,128)(2,1)S(1)}, u32[]{:S(2)}, u32[]{:S(2)}) async-start(bf16[8,32,1536]{2,1,0:T(8,128)(2,1)} %bitcast.18), calls=%async_computation.1 | async-start | bytes 1572864 | tf_op jit(solution)/shard_map/all_to_all | solution.py:534
  69.1 8.1 %collective-permute-start.9 = (bf16[3,256,128]{2,1,0:T(8,128)(2,1)}, bf16[3,256,128]{2,1,0:T(8,128)(2,1)S(1)}, u32[]{:S(2)}, u32[]{:S(2)}) collective-permute-start(bf16[3,256,128]{2,1,0:T(8,128)(2,1)} %get-tuple-element.32), channel_id=1, source_target_pairs={{0,3},{1,0},{2,1},{3,2},{4,7},{5,4},{6,5},{7,6},{8,11},{9,8},{10,9... | collective-permute-start | bytes 589832 | tf_op jit(solution)/shard_map/ppermute | solution.py:66
  72.1 6.7 %collective-permute-start.10 = (bf16[3,256,128]{2,1,0:T(8,128)(2,1)}, bf16[3,256,128]{2,1,0:T(8,128)(2,1)}, u32[]{:S(2)}, u32[]{:S(2)}) collective-permute-start(bf16[3,256,128]{2,1,0:T(8,128)(2,1)} %get-tuple-element.33), channel_id=1, source_target_pairs={{0,2},{1,3},{2,0},{3,1},{4,6},{5,7},{6,4},{7,5},{8,10},{9,11},{10,... | collective-permute-start | bytes 589832 | tf_op jit(solution)/shard_map/ppermute | solution.py:66
  72.1 8.4 %collective-permute-start.11 = (bf16[3,256,128]{2,1,0:T(8,128)(2,1)}, bf16[3,256,128]{2,1,0:T(8,128)(2,1)}, u32[]{:S(2)}, u32[]{:S(2)}) collective-permute-start(bf16[3,256,128]{2,1,0:T(8,128)(2,1)} %get-tuple-element.34), channel_id=1, source_target_pairs={{0,1},{1,2},{2,3},{3,0},{4,5},{5,6},{6,7},{7,4},{8,9},{9,10},{10,1... | collective-permute-start | bytes 589832 | tf_op jit(solution)/shard_map/ppermute | solution.py:66
  72.8 0.9 %copy-start = (bf16[8,32,1536]{2,1,0:T(8,128)(2,1)}, bf16[8,32,1536]{2,1,0:T(8,128)(2,1)S(1)}, u32[]{:S(2)}) copy-start(bf16[8,32,1536]{2,1,0:T(8,128)(2,1)S(1)} %all-to-all-done.1) | copy-start | bytes 2359300
  77.2 3.4 %copy-start.2 = (bf16[3,256,128]{2,1,0:T(8,128)(2,1)}, bf16[3,256,128]{2,1,0:T(8,128)(2,1)S(1)}, u32[]{:S(2)}) copy-start(bf16[3,256,128]{2,1,0:T(8,128)(2,1)S(1)} %collective-permute-done.9.refs_0_) | copy-start | bytes 589828

commit v6 on v5

--- a/solution.py
+++ b/solution.py
@@ -167,24 +167,6 @@
         ).start()
 
 
-def place_first(order, where, time_ref, own_ref, out_ref, time_held, held, sem_in, sem_out, _):
-    own = pltpu.make_async_copy(own_ref, held, sem_in.at[0])
-    time = pltpu.make_async_copy(time_ref, time_held, sem_in.at[1])
-    time.start()
-    own.start()
-    time.wait()
-    for place in range(TEMP_HEADS):
-        pltpu.make_async_copy(
-            time_held.at[:, pl.ds(place * HEAD, HEAD)],
-            out_ref.at[:, columns(order[SPAT_HEADS + place])],
-            sem_out.at[1],
-        ).start()
-    own.wait()
-    place_group(order, where, 0, held, out_ref, sem_out.at[0])
-    pltpu.make_async_copy(time_held, time_held, sem_out.at[1]).wait()
-    pltpu.make_async_copy(held, held, sem_out.at[0]).wait()
-
-
 def place_rest(order, where, *refs):
     count = RING - 1
     parts, (_, out_ref, held, sem_in, sem_out, _) = refs[:count], refs[count:]
@@ -214,7 +196,7 @@
             line = mask_ref[0, pl.ds(block, 1), :]
             line = jnp.where((line == 1) | (lane == block), 0.0, NEG)
             line = jnp.concatenate([line, jnp.zeros((1, HEAD - BLOCKS), F32)], axis=1)
-            rows = pl.ds(slot * ROWS + half * BLK, BLK)
+            rows = pl.ds((slot - 1) % RING * ROWS + half * BLK, BLK)
             query = q_refs[slot][0, 0, half * BLK:(half + 1) * BLK, :]
             key = kv_refs[slot // 2][0, 0, pl.ds(slot % 2 * ROWS + half * BLK, BLK), :]
             level = jnp.sum(
@@ -240,9 +222,9 @@
     )
 
 
-def attend_again(where, marked_ref, chunks, kv_all, out_refs, marks, kv, sem):
-    head = pl.program_id(0)
-    lane = lax.broadcasted_iota(jnp.int32, (TOKENS, 2 * HEAD), 1)
+def attend_again(head, where, marked_ref, chunks, kv_all, out_refs, marks, kv, sem):
+    tokens = marked_ref.shape[1]
+    lane = lax.broadcasted_iota(jnp.int32, (tokens, 2 * HEAD), 1)
     query = marked_ref[0]
     query = jnp.where(lane == HEAD + LEVEL, jnp.zeros_like(query), query)
 
@@ -274,17 +256,20 @@
         return new, sums, total
 
     start = (
-        jnp.full((1, TOKENS), -3e38, F32),
-        jnp.zeros((1, TOKENS), F32),
-        jnp.zeros((HEAD, TOKENS), F32),
+        jnp.full((1, tokens), -3e38, F32),
+        jnp.zeros((1, tokens), F32),
+        jnp.zeros((HEAD, tokens), F32),
     )
     _, sums, total = lax.fori_loop(0, len(chunks), step, start)
-    result = total / sums
-    for slot in range(RING):
-        out_refs[slot][0] = result[:, slot * ROWS:(slot + 1) * ROWS].T.astype(BF16)
-
-
-def attend(chunks, everything, order, where, *refs):
+    store(total / sums, out_refs)
+
+
+def store(result, out_refs):
+    for i, ref in enumerate(out_refs):
+        ref[0] = result[:, i * ROWS:(i + 1) * ROWS].T.astype(BF16)
+
+
+def attend(chunks, everything, tail, order, where, *refs):
     count = len(chunks)
     first, last = chunks[0][0] == 0, everything is not None
     kv_refs, refs = refs[:count], refs[count:]
@@ -292,13 +277,17 @@
         mask_ref, q_refs, refs = refs[0], refs[1:1 + RING], refs[1 + RING:]
         marked_ref, state_ref, marks = refs
         mark_queries(where, mask_ref, q_refs, kv_refs, marked_ref)
-        state = jnp.zeros((HEAD + 8, TOKENS), F32)
+        states = [jnp.zeros((HEAD + 8, TOKENS), F32)]
     else:
         marked_ref, before_ref, refs = refs[0], refs[1], refs[2:]
-        state = before_ref[0]
-        if last:
+        if tail:
+            kv_all, time_ref, refs = refs[:len(everything)], refs[len(everything)], refs[len(everything) + 1:]
+            out_ref, marks, marks_more, kv, sem, own_held, time_held, sem_time, sem_own = refs
+            time = pltpu.make_async_copy(time_ref, time_held, sem_time.at[0])
+            time.start()
+        elif last:
             kv_all, refs = refs[:len(everything)], refs[len(everything):]
-            out_refs, (marks, marks_more, kv, sem) = refs[:RING], refs[RING:]
+            out_refs, (marks, marks_more, kv, sem) = refs[:RING - 1], refs[RING - 1:]
         else:
             state_ref, marks = refs
 
@@ -307,43 +296,79 @@
         for i, (offset, half) in enumerate(chunks):
             mark_keys(where, offset, half, marks.at[pl.ds(i * HALF, HALF)])
 
+    heads = range(GROUP if tail else 1)
+    if not first:
+        states = [before_ref[head] for head in heads]
     ones = jnp.ones((8, TOKENS), BF16)
     for i in range(0, count, 2):
         pair = kv_refs[i:i + 2]
-        keys = jnp.concatenate([kv_ref[0, 0] for kv_ref in pair], axis=0)
-        vals = jnp.concatenate([turned(kv_ref, 0) for kv_ref in pair], axis=1)
-        scores = lax.dot_general(
-            jnp.concatenate([keys, marks[i * HALF:(i + 2) * HALF]], axis=1),
-            marked_ref[0],
-            (((1,), (1,)), ((), ())),
-            preferred_element_type=F32,
-        )
-        weights = jnp.exp2(scores * LOG2_SCALE).astype(BF16)
-        state += jnp.dot(
-            jnp.concatenate([vals, ones], axis=0), weights, preferred_element_type=F32
-        )
+        scores = []
+        for head in heads:
+            keys = jnp.concatenate([kv_ref[head, 0] for kv_ref in pair], axis=0)
+            scores.append(lax.dot_general(
+                jnp.concatenate([keys, marks[i * HALF:(i + 2) * HALF]], axis=1),
+                marked_ref[head],
+                (((1,), (1,)), ((), ())),
+                preferred_element_type=F32,
+            ))
+        weights = [jnp.exp2(score * LOG2_SCALE).astype(BF16) for score in scores]
+        for head in heads:
+            vals = jnp.concatenate([turned(kv_ref, head) for kv_ref in pair], axis=1)
+            states[head] += jnp.dot(
+                jnp.concatenate([vals, ones], axis=0),
+                weights[head],
+                preferred_element_type=F32,
+            )
     if not last:
-        state_ref[0] = state
+        state_ref[0] = states[0]
         return
-    sums = state[HEAD:HEAD + 1]
-    result = state[:HEAD] / sums
-    for slot in range(RING):
-        out_refs[slot][0] = result[:, slot * ROWS:(slot + 1) * ROWS].T.astype(BF16)
-    fine = jnp.max(jnp.where(sums < LARGE, 0.0, 1.0)) == 0.0
-
-    @pl.when(jnp.logical_not(fine))
-    def _():
-        attend_again(where, marked_ref, everything, kv_all, out_refs, marks_more, kv, sem)
-
-
-def attention(held, chunks, order, where, mask=None, queries=(), carried=(), everything=None):
-    def at(*block):
-        zeros = (0,) * (len(block) - 1)
-        return pl.BlockSpec(block, lambda h, o, w: (h,) + zeros)
+    if tail:
+        time.wait()
+        for place in range(TEMP_HEADS):
+            pltpu.make_async_copy(
+                time_held.at[:, pl.ds(place * HEAD, HEAD)],
+                out_ref.at[:, columns(order[SPAT_HEADS + place])],
+                sem_time.at[1],
+            ).start()
+    for head in heads:
+        if tail:
+            out_refs = [own_held.at[pl.ds(head, 1)]]
+        state = states[head]
+        sums = state[HEAD:HEAD + 1]
+        store(state[:HEAD] / sums, out_refs)
+        fine = jnp.max(jnp.where(sums < LARGE, 0.0, 1.0)) == 0.0
+
+        @pl.when(jnp.logical_not(fine))
+        def _(head=head, out_refs=out_refs):
+            attend_again(
+                head if tail else pl.program_id(0), where, marked_ref.at[pl.ds(head, 1)],
+                everything, kv_all, out_refs, marks_more, kv, sem,
+            )
+
+        if tail:
+            spatial = order[where[2] * GROUP + head]
+            pltpu.make_async_copy(
+                own_held.at[head], out_ref.at[:, columns(spatial)], sem_own
+            ).start()
+    if tail:
+        pltpu.make_async_copy(time_held, time_held, sem_time.at[1]).wait()
+        pltpu.make_async_copy(own_held, own_held, sem_own).wait()
+
+
+def attention(held, chunks, order, where, mask=None, queries=(), carried=(), everything=None, time=None):
+    several = 1 if time is None else GROUP
+
+    def at(_, *block):
+        zeros = (0,) * len(block)
+        return pl.BlockSpec((several,) + block, lambda h, o, w: (h,) + zeros)
 
     count = len(chunks)
     slot_spec = at(1, ROWS, HEAD)
-    marked_spec, state_spec = at(1, TOKENS, 2 * HEAD), at(1, HEAD + 8, TOKENS)
+    tokens, start = TOKENS, 0
+    if everything is not None:
+        tokens, start = (TOKENS - ROWS, 0) if time is None else (ROWS, RING - 1)
+    marked_spec = pl.BlockSpec((several, tokens, 2 * HEAD), lambda h, o, w: (h, start, 0))
+    state_spec = pl.BlockSpec((several, HEAD + 8, tokens), lambda h, o, w: (h, 0, start))
     in_specs = [at(1, 2, HALF, HEAD)] * count
     marked_shape = jax.ShapeDtypeStruct((GROUP, TOKENS, 2 * HEAD), BF16)
     state_shape = jax.ShapeDtypeStruct((GROUP, HEAD + 8, TOKENS), F32)
@@ -365,15 +390,24 @@
     if everything is not None:
         every = [held[chunk] for chunk in everything]
         in_specs += [HBM] * len(every)
-        out_specs = [slot_spec] * RING
-        out_shape = [jax.ShapeDtypeStruct((GROUP, ROWS, HEAD), BF16)] * RING
         scratch += [pltpu.VMEM((HALF, HEAD), BF16), pltpu.VMEM((2, HALF, HEAD), BF16), DMA]
-    flops = (H0 if queries else H1 if everything is None else 1) * 8 * GROUP * TOKENS * count * HALF * HEAD
+        if time is None:
+            out_specs = [slot_spec] * (RING - 1)
+            out_shape = [jax.ShapeDtypeStruct((GROUP, ROWS, HEAD), BF16)] * (RING - 1)
+        else:
+            every.append(time)
+            in_specs += [HBM]
+            out_specs = HBM
+            out_shape = jax.ShapeDtypeStruct((ROWS, HEADS * HEAD), BF16)
+            scratch += [pltpu.VMEM((GROUP, ROWS, HEAD), BF16)]
+            scratch += [pltpu.VMEM((ROWS, TEMP_HEADS * HEAD), BF16), DMAS, DMA]
+    hint = H0 if queries else H1 if everything is None else 2 if time is None else 1
+    flops = hint * 8 * GROUP * tokens * count * HALF * HEAD
     return pl.pallas_call(
-        functools.partial(attend, chunks, everything),
+        functools.partial(attend, chunks, everything, time is not None),
         grid_spec=pltpu.PrefetchScalarGridSpec(
             num_scalar_prefetch=2,
-            grid=(GROUP,),
+            grid=(GROUP // several,),
             in_specs=in_specs,
             out_specs=out_specs,
             scratch_shapes=scratch,
@@ -520,39 +554,32 @@
     held[far, 0] = shift(held[left, 0], 1, False)
     held[far, 1] = shift(held[right, 1], RING - 1, False)
     state = attention(held, [(left, 0), (right, 1)], order, where, carried=(marked, state))
-    parts = attention(
-        held,
-        [(left, 1), (right, 0), (far, 0), (far, 1)],
-        order,
-        where,
-        carried=(marked, state),
-        everything=[(offset, half) for offset in (0, left, right, far) for half in range(2)],
-    )
-    parts = [parts[0]] + [shift(parts[s], RING - s, True) for s in range(1, RING)]
-
-    time_out = time_attention(order, jnp.transpose(temporal_mask, (1, 2, 0)), frame_valid[None], gathered)
+    time_out = time_attention(
+        order, jnp.transpose(temporal_mask, (1, 2, 0)), frame_valid[None], gathered
+    )
     time_out = lax.all_to_all(time_out, "frame", 0, 0, tiled=True)
-    out_shape = jax.ShapeDtypeStruct((rows, width), BF16)
-    room = pltpu.VMEM((FILLER, HEAD), F32)
-    base = call(
-        place_first,
-        "place_first",
-        3,
-        [SMEM, SMEM, HBM, HBM],
-        HBM,
-        out_shape,
-        [pltpu.VMEM((ROWS, TEMP_HEADS * HEAD), BF16), pltpu.VMEM(slot_shape, BF16), DMAS, DMAS, room],
-        order, where, time_out, parts[0],
-    )
+    chunks = [(left, 1), (right, 0), (far, 0), (far, 1)]
+    everything = [(offset, half) for offset in (0, left, right, far) for half in range(2)]
+    finish = functools.partial(
+        attention, held, chunks, order, where, carried=(marked, state), everything=everything
+    )
+    parts = finish()
+    parts = [shift(parts[s - 1], RING - s, True) for s in range(1, RING)]
+    base = finish(time=time_out)
     result = call(
         place_rest,
         "place_rest",
         1,
         [SMEM, SMEM] + [HBM] * RING,
         HBM,
-        out_shape,
-        [pltpu.VMEM((RING - 1,) + slot_shape, BF16), DMAS, DMA, room],
-        order, where, *parts[1:], base,
+        jax.ShapeDtypeStruct((rows, width), BF16),
+        [
+            pltpu.VMEM((RING - 1,) + slot_shape, BF16),
+            DMAS,
+            DMA,
+            pltpu.VMEM((FILLER, HEAD), F32),
+        ],
+        order, where, *parts, base,
         input_output_aliases={1 + RING: 0},
     )
     return result[None]

time: 84.4 us -> 83.7 us (level)
  waiting for transfers between devices: 6.11 us -> 3.18 us
  Pallas kernels: 44.6 us -> 46.6 us
    pallas_call x3 -> x4, Pallas kernels: 23.1 us -> 28 us  [attention(): pl.pallas_call(functools.partial(attend, chunks, everything, time is not...]
    ppermute x12, waiting for transfers between devices: 5.55 us -> 2.57 us  [shift(): return lax.ppermute(tensor, AXES, sorted(pairs))]
    pallas_call x6 -> x5, Pallas kernels: 17.2 us -> 14.3 us  [call(): pl.pallas_call(body, in_specs=in_specs, out_specs=out_specs, out_shape=ou...]
  transfers between devices with their start and end apart: 14 -> 14, of which waited for: 5 -> 3; matrix products, arithmetic and copies ran while one was open for 0% -> 0% of each run, Pallas kernels for 46% -> 49%
where the time goes in v6:
time: 83.7 us; the launch traced here: 82.2 us
  Pallas kernels  46.6 us (56%)
  starting transfers between devices  30.5 us (36%)
  waiting for transfers between devices  3.18 us (4%)
  local copies, waits for them, and re-layouts  1.71 us (2%)
    pallas_call x4, Pallas kernels, attention(): pl.pallas_call(functools.partial(attend, chunks, everything, time is not...  28 us
    ppermute x12, starting transfers between devices, shift(): return lax.ppermute(tensor, AXES, sorted(pairs))  18.9 us
    pallas_call x5, Pallas kernels, call(): pl.pallas_call(body, in_specs=in_specs, out_specs=out_specs, out_shape=ou...  14.3 us
    all_to_all x1, starting transfers between devices, shards(): time_out = lax.all_to_all(time_out, 'frame', 0, 0, tiled=True)  6.51 us
    all_to_all x1, starting transfers between devices, shards(): gathered = lax.all_to_all(packed, 'frame', 0, 0, tiled=True)  5.14 us
    pallas_call x1, Pallas kernels, time_attention(): pl.pallas_call(attend_time, grid_spec=pltpu.PrefetchScalarGridSpec(num_sc...  4.28 us
    ppermute x12, waiting for transfers between devices, shift(): return lax.ppermute(tensor, AXES, sorted(pairs))  2.57 us
    unnamed x6, local copies, waits for them, and re-layouts  1.71 us
  transfers between devices with their start and end apart: 14, of which 3 were waited for; matrix products, arithmetic and copies ran while one was open for 0% of the time, Pallas kernels for 49%

profile of v6, /device:TPU:1, one launch (start us, length us, event | category | flops | bytes accessed | tf_op | source)
XLA Modules:
  0.0 82.2 jit_solution(6194894909530528384)
XLA Ops:
  0.0 3.7 %pack_spatial.1 = (bf16[3,3,256,128]{3,2,1,0:T(8,128)(2,1)}, bf16[3,3,256,128]{3,2,1,0:T(8,128)(2,1)}, bf16[3,3,256,128]{3,2,1,0:T(8,128)(2,1)}, s32[24]{0:T(128)}, s32[3]{0:T(128)}) custom-call(s32[24]{0:T(128)} %kind.1, bf16[256,3072]{1,0:T(8,128)(2,1)} %bitcast.10, bf16[256,3072]{1,0:T(8,128)(2,1)} %bitcast.12, bf16[256,3072]{1,0:T(8,128)(2,1)} %bitcast.14), custom_call_target="tpu_custom_call" | custom-call | bytes 5242880 | tf_op jit(solution)/shard_map/pack_spatial/pallas_call | solution.py:485
  3.7 2.5 %collective-permute-start = (bf16[3,3,256,128]{3,2,1,0:T(8,128)(2,1)}, bf16[3,3,256,128]{3,2,1,0:T(8,128)(2,1)S(1)}, u32[]{:S(2)}, u32[]{:S(2)}) collective-permute-start(bf16[3,3,256,128]{3,2,1,0:T(8,128)(2,1)} %get-tuple-element.23), channel_id=1, source_target_pairs={{0,1},{1,2},{2,3},{3,0},{4,5},{5,6},{6,7},{7,4},{8,9},{9,10},{10,1... | collective-permute-start | bytes 1769480 | tf_op jit(solution)/shard_map/ppermute | solution.py:66
  6.2 3.3 %collective-permute-start.1 = (bf16[3,3,256,128]{3,2,1,0:T(8,128)(2,1)}, bf16[3,3,256,128]{3,2,1,0:T(8,128)(2,1)}, u32[]{:S(2)}, u32[]{:S(2)}) collective-permute-start(bf16[3,3,256,128]{3,2,1,0:T(8,128)(2,1)} %get-tuple-element.24), channel_id=1, source_target_pairs={{0,2},{1,3},{2,0},{3,1},{4,6},{5,7},{6,4},{7,5},{8,10},{9,11},{10,... | collective-permute-start | bytes 1769480 | tf_op jit(solution)/shard_map/ppermute | solution.py:66
  9.5 0.7 collective-permute-start.2
  10.2 3.8 %pack_rest.1 = (bf16[3,3,256,128]{3,2,1,0:T(8,128)(2,1)}, bf16[256,4608]{1,0:T(8,128)(2,1)}) custom-call(s32[24]{0:T(128)} %get-tuple-element.20.order, s32[3]{0:T(128)} %get-tuple-element.21.where, bf16[256,3072]{1,0:T(8,128)(2,1)} %bitcast.11, bf16[256,3072]{1,0:T(8,128)(2,1)} %bitcast.13, bf16[256,3072]{1,0:T(8,128)(2,1)} %bitcast.15), custom_call_target="tpu_custom_call" | custom-call | bytes 41943040 | tf_op jit(solution)/shard_map/pack_rest/pallas_call | solution.py:485
  14.0 5.1 %all-to-all-start = ((bf16[8,32,4608]{2,1,0:T(8,128)(2,1)}), bf16[8,32,4608]{2,1,0:T(8,128)(2,1)}, u32[]{:S(2)}, u32[]{:S(2)}) async-start(bf16[8,32,4608]{2,1,0:T(8,128)(2,1)} %bitcast.17), calls=%async_computation | async-start | bytes 4718592 | tf_op jit(solution)/shard_map/all_to_all | solution.py:527
  19.2 0.0 collective-permute-done.second_ref.refs_4_
  19.2 0.0 copy-start.1
  19.2 0.8 copy-done.1
  20.0 2.2 %join.2.refs_0_.refs_6_ = bf16[3,2,512,128]{3,2,1,0:T(8,128)(2,1)} custom-call(bf16[3,3,256,128]{3,2,1,0:T(8,128)(2,1)} %get-tuple-element.22.first_ref.refs_3_, bf16[3,3,256,128]{3,2,1,0:T(8,128)(2,1)} %copy-done.1), custom_call_target="tpu_custom_call" | custom-call | bytes 2097152 | tf_op jit(solution)/shard_map/join/pallas_call | solution.py:485
  22.2 1.5 %collective-permute-done.1.first_ref.refs_5_ = bf16[3,3,256,128]{3,2,1,0:T(8,128)(2,1)} collective-permute-done((bf16[3,3,256,128]{3,2,1,0:T(8,128)(2,1)}, bf16[3,3,256,128]{3,2,1,0:T(8,128)(2,1)}, u32[]{:S(2)}, u32[]{:S(2)}) %collective-permute-start.1) | collective-permute-done | bytes 589856 | tf_op jit(solution)/shard_map/ppermute | solution.py:66
  23.7 0.0 collective-permute-done.2.second_ref.refs_6_
  23.7 2.2 %join.3.refs_1_.refs_7_ = bf16[3,2,512,128]{3,2,1,0:T(8,128)(2,1)} custom-call(bf16[3,3,256,128]{3,2,1,0:T(8,128)(2,1)} %collective-permute-done.1.first_ref.refs_5_, bf16[3,3,256,128]{3,2,1,0:T(8,128)(2,1)} %collective-permute-done.2.second_ref.refs_6_), custom_call_target="tpu_custom_call" | custom-call | bytes 2097152 | tf_op jit(solution)/shard_map/join/pallas_call | solution.py:485
  25.9 2.5 %collective-permute-start.7 = (bf16[3,2,512,128]{3,2,1,0:T(8,128)(2,1)}, bf16[3,2,512,128]{3,2,1,0:T(8,128)(2,1)}, u32[]{:S(2)}, u32[]{:S(2)}) collective-permute-start(bf16[3,2,512,128]{3,2,1,0:T(8,128)(2,1)} %join.3.refs_1_.refs_7_), channel_id=1, source_target_pairs={{0,12},{1,13},{2,14},{3,15},{4,0},{5,1},{6,2},{7,3},{8,4},{9,5},{1... | collective-permute-start | bytes 2359304 | tf_op jit(solution)/shard_map/ppermute | solution.py:66
  28.5 0.0 collective-permute-start.5
  28.5 0.2 collective-permute-start.3
  28.7 2.5 %collective-permute-start.4 = (bf16[3,2,512,128]{3,2,1,0:T(8,128)(2,1)}, bf16[3,2,512,128]{3,2,1,0:T(8,128)(2,1)}, u32[]{:S(2)}, u32[]{:S(2)}) collective-permute-start(bf16[3,2,512,128]{3,2,1,0:T(8,128)(2,1)} %join.2.refs_0_.refs_6_), channel_id=1, source_target_pairs={{0,12},{1,13},{2,14},{3,15},{4,0},{5,1},{6,2},{7,3},{8,4},{9,5},{1... | collective-permute-start | bytes 2359304 | tf_op jit(solution)/shard_map/ppermute | solution.py:66
  31.2 6.6 %spatial_attention.4 = (bf16[3,1024,256]{2,1,0:T(8,128)(2,1)}, f32[3,136,1024]{2,1,0:T(8,128)}) custom-call(s32[24]{0:T(128)} %get-tuple-element.20.order, s32[3]{0:T(128)} %get-tuple-element.21.where, bf16[3,2,512,128]{3,2,1,0:T(8,128)(2,1)} %join.2.refs_0_.refs_6_, bf16[3,2,512,128]{3,2,1,0:T(8,128)(2,1)} %join.3.refs_1_.refs_7_, s32[24,32,32]{2,1,0:T(8,128)} %refs_2_.1, ...), custom_call_target="tpu_custom_call" | custom-call | flops 6442450944 | bytes 4194304 | tf_op jit(solution)/shard_map/spatial_attention/pallas_call | solution.py:406
  37.8 0.0 collective-permute-done.7.refs_1_.refs_11_
  37.8 3.3 %collective-permute-start.8 = (bf16[3,2,512,128]{3,2,1,0:T(8,128)(2,1)}, bf16[3,2,512,128]{3,2,1,0:T(8,128)(2,1)}, u32[]{:S(2)}, u32[]{:S(2)}) collective-permute-start(bf16[3,2,512,128]{3,2,1,0:T(8,128)(2,1)} %collective-permute-done.7.refs_1_.refs_11_), channel_id=1, source_target_pairs={{0,12},{1,13},{2,14},{3,15},{4,0},{5,1},{6,2},{7,3},{8,4},{9,5},{1... | collective-permute-start | bytes 2359304 | tf_op jit(solution)/shard_map/ppermute | solution.py:66
  41.1 0.0 collective-permute-done.5.refs_0_.refs_8_
  41.1 0.0 collective-permute-start.6
  41.1 6.7 %spatial_attention.5.refs_5_ = f32[3,136,1024]{2,1,0:T(8,128)} custom-call(s32[24]{0:T(128)} %get-tuple-element.20.order, s32[3]{0:T(128)} %get-tuple-element.21.where, bf16[3,2,512,128]{3,2,1,0:T(8,128)(2,1)} %collective-permute-done.5.refs_0_.refs_8_, bf16[3,2,512,128]{3,2,1,0:T(8,128)(2,1)} %collective-permute-done.7.refs_1_.refs_11_, ...), custom_call_target="tpu_custom_call" | custom-call | flops 12884901888 | bytes 4194304 | tf_op jit(solution)/shard_map/spatial_attention/pallas_call | solution.py:406
  47.8 0.6 all-to-all-done
  48.4 4.3 %temporal_attention.1 = bf16[256,1536]{1,0:T(8,128)(2,1)} custom-call(s32[24]{0:T(128)} %get-tuple-element.20.order, s32[8,8,24]{2,1,0:T(8,128)} %bitcast.19, s32[1,8]{1,0:T(1,128)} %bitcast.20, bf16[256,4608]{1,0:T(8,128)(2,1)} %bitcast.6.q_ref.k_ref.v_ref, bf16[256,4608]{1,0:T(8,128)(2,1)} %bitcast.6.q_ref.k_ref.v_ref, ...), custom_call_target="tpu_custom_call" | custom-call | flops 3221225472 | bytes 4194304 | tf_op jit(solution)/shard_map/temporal_attention/pallas_call | solution.py:465
  52.7 6.5 %all-to-all-start.1 = ((bf16[8,32,1536]{2,1,0:T(8,128)(2,1)}), bf16[8,32,1536]{2,1,0:T(8,128)(2,1)S(1)}, u32[]{:S(2)}, u32[]{:S(2)}) async-start(bf16[8,32,1536]{2,1,0:T(8,128)(2,1)} %bitcast.18), calls=%async_computation.1 | async-start | bytes 1572864 | tf_op jit(solution)/shard_map/all_to_all | solution.py:560
  59.2 0.0 collective-permute-done.3.refs_0_.refs_9_
  59.2 0.0 collective-permute-done.4.refs_1_.refs_10_
  59.2 0.0 collective-permute-done.8.refs_3_.refs_13_
  59.2 0.0 collective-permute-done.6.refs_2_.refs_12_
  59.2 8.9 %spatial_attention.6 = (bf16[3,256,128]{2,1,0:T(8,128)(2,1)}, bf16[3,256,128]{2,1,0:T(8,128)(2,1)}, bf16[3,256,128]{2,1,0:T(8,128)(2,1)}) custom-call(s32[24]{0:T(128)} %get-tuple-element.20.order, s32[3]{0:T(128)} %get-tuple-element.21.where, bf16[3,2,512,128]{3,2,1,0:T(8,128)(2,1)} %collective-permute-done.3.refs_0_.refs_9_, ...), custom_call_target="tpu_custom_call" | custom-call | flops 9663676416 | bytes 4194304 | tf_op jit(solution)/shard_map/spatial_attention/pallas_call | solution.py:406
  68.1 3.0 %collective-permute-start.9 = (bf16[3,256,128]{2,1,0:T(8,128)(2,1)}, bf16[3,256,128]{2,1,0:T(8,128)(2,1)S(1)}, u32[]{:S(2)}, u32[]{:S(2)}) collective-permute-start(bf16[3,256,128]{2,1,0:T(8,128)(2,1)} %get-tuple-element.31), channel_id=1, source_target_pairs={{0,3},{1,0},{2,1},{3,2},{4,7},{5,4},{6,5},{7,6},{8,11},{9,8},{10,9... | collective-permute-start | bytes 589832 | tf_op jit(solution)/shard_map/ppermute | solution.py:66
  71.1 0.0 collective-permute-start.10
  71.1 0.7 collective-permute-start.11
  71.8 0.0 all-to-all-done.1
  71.8 0.0 copy-start
  71.8 0.9 %copy-done = bf16[8,32,1536]{2,1,0:T(8,128)(2,1)} copy-done((bf16[8,32,1536]{2,1,0:T(8,128)(2,1)}, bf16[8,32,1536]{2,1,0:T(8,128)(2,1)S(1)}, u32[]{:S(2)}) %copy-start) | copy-done | bytes 786456
  72.7 5.8 %spatial_attention.7.refs_3_ = bf16[256,3072]{1,0:T(8,128)(2,1)} custom-call(s32[24]{0:T(128)} %get-tuple-element.20.order, s32[3]{0:T(128)} %get-tuple-element.21.where, bf16[3,2,512,128]{3,2,1,0:T(8,128)(2,1)} %collective-permute-done.3.refs_0_.refs_9_, bf16[3,2,512,128]{3,2,1,0:T(8,128)(2,1)} %collective-permute-done.4.refs_1_.refs_10_, ...), custom_call_target="tpu_custom_call" | custom-call | flops 1610612736 | bytes 4194304 | tf_op jit(solution)/shard_map/spatial_attention/pallas_call | solution.py:406
  78.5 0.0 collective-permute-done.9.refs_0_
  78.6 0.0 copy-start.2
  78.6 0.0 collective-permute-done.10.refs_1_
  78.6 1.0 %collective-permute-done.11.refs_2_ = bf16[3,256,128]{2,1,0:T(8,128)(2,1)} collective-permute-done((bf16[3,256,128]{2,1,0:T(8,128)(2,1)}, bf16[3,256,128]{2,1,0:T(8,128)(2,1)}, u32[]{:S(2)}, u32[]{:S(2)}) %collective-permute-start.11) | collective-permute-done | bytes 196640 | tf_op jit(solution)/shard_map/ppermute | solution.py:66
  79.6 0.0 copy-done.2
  79.6 2.5 %place_rest.1 = bf16[256,3072]{1,0:T(8,128)(2,1)} custom-call(s32[24]{0:T(128)} %get-tuple-element.20.order, s32[3]{0:T(128)} %get-tuple-element.21.where, bf16[3,256,128]{2,1,0:T(8,128)(2,1)} %copy-done.2, bf16[3,256,128]{2,1,0:T(8,128)(2,1)} %collective-permute-done.10.refs_1_, ...), custom_call_target="tpu_custom_call", output_to_operand_aliasing={{}: (5, {})} | custom-call | bytes 1048576 | tf_op jit(solution)/shard_map/place_rest/pallas_call | solution.py:485
Async XLA Ops:
  3.7 15.5 %collective-permute-start = (bf16[3,3,256,128]{3,2,1,0:T(8,128)(2,1)}, bf16[3,3,256,128]{3,2,1,0:T(8,128)(2,1)S(1)}, u32[]{:S(2)}, u32[]{:S(2)}) collective-permute-start(bf16[3,3,256,128]{3,2,1,0:T(8,128)(2,1)} %get-tuple-element.23), channel_id=1, source_target_pairs={{0,1},{1,2},{2,3},{3,0},{4,5},{5,6},{6,7},{7,4},{8,9},{9,10},{10,1... | collective-permute-start | bytes 1769480 | tf_op jit(solution)/shard_map/ppermute | solution.py:66
  6.2 17.5 %collective-permute-start.1 = (bf16[3,3,256,128]{3,2,1,0:T(8,128)(2,1)}, bf16[3,3,256,128]{3,2,1,0:T(8,128)(2,1)}, u32[]{:S(2)}, u32[]{:S(2)}) collective-permute-start(bf16[3,3,256,128]{3,2,1,0:T(8,128)(2,1)} %get-tuple-element.24), channel_id=1, source_target_pairs={{0,2},{1,3},{2,0},{3,1},{4,6},{5,7},{6,4},{7,5},{8,10},{9,11},{10,... | collective-permute-start | bytes 1769480 | tf_op jit(solution)/shard_map/ppermute | solution.py:66
  9.5 14.2 %collective-permute-start.2 = (bf16[3,3,256,128]{3,2,1,0:T(8,128)(2,1)}, bf16[3,3,256,128]{3,2,1,0:T(8,128)(2,1)}, u32[]{:S(2)}, u32[]{:S(2)}) collective-permute-start(bf16[3,3,256,128]{3,2,1,0:T(8,128)(2,1)} %get-tuple-element.25), channel_id=1, source_target_pairs={{0,3},{1,0},{2,1},{3,2},{4,7},{5,4},{6,5},{7,6},{8,11},{9,8},{10,9... | collective-permute-start | bytes 1769480 | tf_op jit(solution)/shard_map/ppermute | solution.py:66
  14.0 34.4 %all-to-all-start = ((bf16[8,32,4608]{2,1,0:T(8,128)(2,1)}), bf16[8,32,4608]{2,1,0:T(8,128)(2,1)}, u32[]{:S(2)}, u32[]{:S(2)}) async-start(bf16[8,32,4608]{2,1,0:T(8,128)(2,1)} %bitcast.17), calls=%async_computation | async-start | bytes 4718592 | tf_op jit(solution)/shard_map/all_to_all | solution.py:527
  19.2 0.8 copy-start.1
  25.9 11.9 %collective-permute-start.7 = (bf16[3,2,512,128]{3,2,1,0:T(8,128)(2,1)}, bf16[3,2,512,128]{3,2,1,0:T(8,128)(2,1)}, u32[]{:S(2)}, u32[]{:S(2)}) collective-permute-start(bf16[3,2,512,128]{3,2,1,0:T(8,128)(2,1)} %join.3.refs_1_.refs_7_), channel_id=1, source_target_pairs={{0,12},{1,13},{2,14},{3,15},{4,0},{5,1},{6,2},{7,3},{8,4},{9,5},{1... | collective-permute-start | bytes 2359304 | tf_op jit(solution)/shard_map/ppermute | solution.py:66
  28.5 12.7 %collective-permute-start.5 = (bf16[3,2,512,128]{3,2,1,0:T(8,128)(2,1)}, bf16[3,2,512,128]{3,2,1,0:T(8,128)(2,1)}, u32[]{:S(2)}, u32[]{:S(2)}) collective-permute-start(bf16[3,2,512,128]{3,2,1,0:T(8,128)(2,1)} %join.2.refs_0_.refs_6_), channel_id=1, source_target_pairs={{0,4},{1,5},{2,6},{3,7},{4,8},{5,9},{6,10},{7,11},{8,12},{9,13},{1... | collective-permute-start | bytes 2359304 | tf_op jit(solution)/shard_map/ppermute | solution.py:66
  28.5 30.7 %collective-permute-start.3 = (bf16[3,2,512,128]{3,2,1,0:T(8,128)(2,1)}, bf16[3,2,512,128]{3,2,1,0:T(8,128)(2,1)}, u32[]{:S(2)}, u32[]{:S(2)}) collective-permute-start(bf16[3,2,512,128]{3,2,1,0:T(8,128)(2,1)} %join.3.refs_1_.refs_7_), channel_id=1, source_target_pairs={{0,4},{1,5},{2,6},{3,7},{4,8},{5,9},{6,10},{7,11},{8,12},{9,13},{1... | collective-permute-start | bytes 2359304 | tf_op jit(solution)/shard_map/ppermute | solution.py:66
  28.7 30.6 %collective-permute-start.4 = (bf16[3,2,512,128]{3,2,1,0:T(8,128)(2,1)}, bf16[3,2,512,128]{3,2,1,0:T(8,128)(2,1)}, u32[]{:S(2)}, u32[]{:S(2)}) collective-permute-start(bf16[3,2,512,128]{3,2,1,0:T(8,128)(2,1)} %join.2.refs_0_.refs_6_), channel_id=1, source_target_pairs={{0,12},{1,13},{2,14},{3,15},{4,0},{5,1},{6,2},{7,3},{8,4},{9,5},{1... | collective-permute-start | bytes 2359304 | tf_op jit(solution)/shard_map/ppermute | solution.py:66
  37.8 21.4 %collective-permute-start.8 = (bf16[3,2,512,128]{3,2,1,0:T(8,128)(2,1)}, bf16[3,2,512,128]{3,2,1,0:T(8,128)(2,1)}, u32[]{:S(2)}, u32[]{:S(2)}) collective-permute-start(bf16[3,2,512,128]{3,2,1,0:T(8,128)(2,1)} %collective-permute-done.7.refs_1_.refs_11_), channel_id=1, source_target_pairs={{0,12},{1,13},{2,14},{3,15},{4,0},{5,1},{6,2},{7,3},{8,4},{9,5},{1... | collective-permute-start | bytes 2359304 | tf_op jit(solution)/shard_map/ppermute | solution.py:66
  41.1 18.1 %collective-permute-start.6 = (bf16[3,2,512,128]{3,2,1,0:T(8,128)(2,1)}, bf16[3,2,512,128]{3,2,1,0:T(8,128)(2,1)}, u32[]{:S(2)}, u32[]{:S(2)}) collective-permute-start(bf16[3,2,512,128]{3,2,1,0:T(8,128)(2,1)} %collective-permute-done.5.refs_0_.refs_8_), channel_id=1, source_target_pairs={{0,4},{1,5},{2,6},{3,7},{4,8},{5,9},{6,10},{7,11},{8,12},{9,13},{1... | collective-permute-start | bytes 2359304 | tf_op jit(solution)/shard_map/ppermute | solution.py:66
  52.7 19.1 %all-to-all-start.1 = ((bf16[8,32,1536]{2,1,0:T(8,128)(2,1)}), bf16[8,32,1536]{2,1,0:T(8,128)(2,1)S(1)}, u32[]{:S(2)}, u32[]{:S(2)}) async-start(bf16[8,32,1536]{2,1,0:T(8,128)(2,1)} %bitcast.18), calls=%async_computation.1 | async-start | bytes 1572864 | tf_op jit(solution)/shard_map/all_to_all | solution.py:560
  68.1 10.4 %collective-permute-start.9 = (bf16[3,256,128]{2,1,0:T(8,128)(2,1)}, bf16[3,256,128]{2,1,0:T(8,128)(2,1)S(1)}, u32[]{:S(2)}, u32[]{:S(2)}) collective-permute-start(bf16[3,256,128]{2,1,0:T(8,128)(2,1)} %get-tuple-element.31), channel_id=1, source_target_pairs={{0,3},{1,0},{2,1},{3,2},{4,7},{5,4},{6,5},{7,6},{8,11},{9,8},{10,9... | collective-permute-start | bytes 589832 | tf_op jit(solution)/shard_map/ppermute | solution.py:66
  71.1 7.4 %collective-permute-start.10 = (bf16[3,256,128]{2,1,0:T(8,128)(2,1)}, bf16[3,256,128]{2,1,0:T(8,128)(2,1)}, u32[]{:S(2)}, u32[]{:S(2)}) collective-permute-start(bf16[3,256,128]{2,1,0:T(8,128)(2,1)} %get-tuple-element.32), channel_id=1, source_target_pairs={{0,2},{1,3},{2,0},{3,1},{4,6},{5,7},{6,4},{7,5},{8,10},{9,11},{10,... | collective-permute-start | bytes 589832 | tf_op jit(solution)/shard_map/ppermute | solution.py:66
  71.1 8.4 %collective-permute-start.11 = (bf16[3,256,128]{2,1,0:T(8,128)(2,1)}, bf16[3,256,128]{2,1,0:T(8,128)(2,1)}, u32[]{:S(2)}, u32[]{:S(2)}) collective-permute-start(bf16[3,256,128]{2,1,0:T(8,128)(2,1)} %get-tuple-element.33), channel_id=1, source_target_pairs={{0,1},{1,2},{2,3},{3,0},{4,5},{5,6},{6,7},{7,4},{8,9},{9,10},{10,1... | collective-permute-start | bytes 589832 | tf_op jit(solution)/shard_map/ppermute | solution.py:66
  71.8 0.9 %copy-start = (bf16[8,32,1536]{2,1,0:T(8,128)(2,1)}, bf16[8,32,1536]{2,1,0:T(8,128)(2,1)S(1)}, u32[]{:S(2)}) copy-start(bf16[8,32,1536]{2,1,0:T(8,128)(2,1)S(1)} %all-to-all-done.1) | copy-start | bytes 2359300
  78.6 1.0 %copy-start.2 = (bf16[3,256,128]{2,1,0:T(8,128)(2,1)}, bf16[3,256,128]{2,1,0:T(8,128)(2,1)S(1)}, u32[]{:S(2)}) copy-start(bf16[3,256,128]{2,1,0:T(8,128)(2,1)S(1)} %collective-permute-done.9.refs_0_) | copy-start | bytes 589828
